TPU v7x, 1024 devices: a whole 4x4x32 slice. The times are simulated.
1024 devices in a mesh: row: 8 (over x, z_hi), col: 128 (over y, z_lo, core).
Axes of the slice: x: 4, y: 4, z: 32 (z_hi: 2, z_lo: 16; z = z_hi * 16 + z_lo), core: 2. Of those that a mesh axis runs over, the one named last changes fastest.
Arguments:
- amplitudes: bfloat16 [1024, 16384], P('row', 'col'), may hold values from -6 to 6
- amp_kept: int32 [8, 128], P('row', 'col'), may hold values 0 or 1
- own_tiles: bfloat16 [20480, 128, 128], P('col'), may hold values from -0.15625 to 0.15625
- own_k: int32 [20480], P('col'), may hold values from 0 to 127
- own_out: int32 [20480], P('col'), may hold values from 0 to 3
- own_live: int32 [20480], P('col'), may hold values from 0 to 1, as said below
- help_tiles: bfloat16 [4096, 128, 128], P('col'), may hold values from -0.15625 to 0.15625
- help_k: int32 [4096], P('col'), may hold values from 0 to 127
- help_out: int32 [4096], P('col'), may hold values from 0 to 3
- help_live: int32 [4096], P('col'), may hold values from 0 to 1, as said below
Outputs:
- ladder: bfloat16 [1024, 65536], P('row', 'col')
Inputs may be any that keep to these rules, and one draw needn't show every extreme that they name: `own_live`: live own slots of an index of col come first. Of the two indices c and c + 64, one is busy with 120 or more live own slots, the other has 40 to 80; one busy index has all 160 live in every draw. `help_live`: live handed slots come first. A busy index of col has 16 or more live, one busy index all 32 in every draw; the other index of its pair has at most 8.
All inputs are finite; a program needn't handle non-finite values. No bound on the sum of `amp_kept` on one device may be relied on, other than what follows from the above.
Results may differ from a plain program's by a relative error of at most 0.011.
Values may be sent and summed in bfloat16 or wider, within the bound.
No kernel may reach another device: no remote copies, remote signals or barrier semaphores. Data moves between devices by JAX's collectives and lax.ppermute only.
A program may use at most 32 MiB of HBM per device.

v0:
```python
import jax
import jax.numpy as jnp
from jax import lax
from jax.sharding import PartitionSpec as P

TILE = 128
OB = 4


def owner_terms(blocks, tiles, kinds, outs, live):
    slots = tiles.shape[0]
    width = min(8, slots)
    count = jnp.sum(live)
    rounds = (count + width - 1) // width
    outputs = jnp.arange(OB, dtype=jnp.int32)

    def one_round(step, acc):
        start = step * width
        first = jnp.minimum(start, slots - width)
        tile_part = lax.dynamic_slice_in_dim(tiles, first, width, 0)
        kind_part = lax.dynamic_slice_in_dim(kinds, first, width, 0)
        out_part = lax.dynamic_slice_in_dim(outs, first, width, 0)
        live_part = lax.dynamic_slice_in_dim(live, first, width, 0)
        position = first + jnp.arange(width, dtype=jnp.int32)
        keep = (position >= start).astype(jnp.float32) * live_part.astype(jnp.float32)
        picked = jnp.take(blocks, kind_part, axis=1)
        prod = jnp.einsum("rtk,tkc->rtc", picked, tile_part, preferred_element_type=jnp.float32)
        weights = (out_part[:, None] == outputs[None, :]).astype(jnp.float32) * keep[:, None]
        return acc + jnp.einsum("rtc,to->roc", prod, weights)

    start_acc = jnp.zeros((blocks.shape[0], OB, tiles.shape[2]), jnp.float32)
    return lax.fori_loop(0, rounds, one_round, start_acc)


def shards(
    amplitudes,
    amp_kept,
    own_tiles,
    own_k,
    own_out,
    own_live,
    help_tiles,
    help_k,
    help_out,
    help_live,
):
    kept_amps = amplitudes * amp_kept.astype(jnp.bfloat16)
    gathered = lax.all_gather(kept_amps, "col", axis=1, tiled=True)
    rows_here = gathered.shape[0]
    blocks = gathered.reshape(rows_here, -1, TILE)
    own_sum = owner_terms(blocks, own_tiles, own_k, own_out, own_live)
    help_sum = owner_terms(blocks, help_tiles, help_k, help_out, help_live)
    total = own_sum + help_sum
    return total.reshape(rows_here, OB * TILE).astype(jnp.bfloat16)


def solution(mesh):
    return jax.shard_map(
        shards,
        mesh=mesh,
        in_specs=(
            P("row", "col"),
            P("row", "col"),
            P("col", None, None),
            P("col"),
            P("col"),
            P("col"),
            P("col", None, None),
            P("col"),
            P("col"),
            P("col"),
        ),
        out_specs=P("row", "col"),
        check_vma=False,
    )
```

profile of v0, /device:TPU:9, one launch (start us, length us, event | category | flops | bytes accessed | tf_op | source)
XLA Modules:
  0.0 385.0 jit_solution(7978082004849131949)
XLA Ops:
  10.6 1.4 reduce_sum.18
  12.7 241.8 %all-gather.2.cloned.1.call-done = bf16[128,16384]{0,1:T(8,128)(2,1)} async-done(((bf16[128,128]{0,1:T(8,128)(2,1)}), bf16[128,16384]{0,1:T(8,128)(2,1)}) %all-gather.2.cloned.1.call-update) | async-done | bytes 4194320 | tf_op jit(solution)/shard_map/all_gather | solution.py:48
  254.5 6.4 %copy.15 = bf16[128,128,128]{2,0,1:T(8,128)(2,1)} copy(bf16[128,128,128]{0,2,1:T(8,128)(2,1)} %bitcast.52) | data formatting | bytes 8388608
  261.0 15.2 %while.23 = (s32[]{:T(128)}, f32[128,4,128]{2,1,0:T(4,128)S(1)}, s32[]{:T(128)}, s32[32]{0:T(128)S(1)}, s32[32]{0:T(128)S(1)}, /*index=5*/bf16[32,128,128]{2,1,0...) while((s32[]{:T(128)}, f32[128,4,128]{2,1,0:T(4,128)S(1)}, ...), condition=%wide.region_5.7_spmd.clone, body=%wide.region_4.6_spmd.clone.sunk | while | flops 34800792 | bytes 2626047 | solution.py:32
  261.1 2.8 gather_fusion.1
  263.9 1.3 convolution_bitcast_fusion.7
  266.1 2.8 gather_fusion.1
  271.2 2.8 gather_fusion.1
  276.2 101.1 %while.22 = (s32[]{:T(128)}, f32[128,4,128]{2,1,0:T(4,128)S(1)}, s32[]{:T(128)}, s32[160]{0:T(256)S(1)}, s32[160]{0:T(256)S(1)}, /*index=5*/bf16[160,128,128]{2,...) while((s32[]{:T(128)}, f32[128,4,128]{2,1,0:T(4,128)S(1)}, ...), condition=%wide.region_2.4_spmd.clone, body=%wide.region_1.3_spmd.clone.sunk | while | flops 34800792 | bytes 2626047 | solution.py:32
  276.3 2.8 gather_fusion
  279.1 1.3 convolution_bitcast_fusion.6
  281.4 2.8 gather_fusion
  286.5 2.8 gather_fusion
  291.5 2.8 gather_fusion
  296.6 2.8 gather_fusion
  301.6 2.8 gather_fusion
  304.4 1.3 convolution_bitcast_fusion.6
  306.7 2.8 gather_fusion
  311.7 2.8 gather_fusion
  316.8 2.8 gather_fusion
  319.6 1.3 convolution_bitcast_fusion.6
  321.8 2.8 gather_fusion
  326.9 2.8 gather_fusion
  332.0 2.8 gather_fusion
  337.0 2.8 gather_fusion
  342.1 2.8 gather_fusion
  347.1 2.8 gather_fusion
  352.2 2.8 gather_fusion
  357.2 2.8 gather_fusion
  362.3 2.8 gather_fusion
  367.3 2.8 gather_fusion
  372.4 2.8 gather_fusion
  (178 shorter events, 49.3 us)
Async XLA Ops:
  6.5 247.9 %all-gather.2.cloned.1.call-start = ((), (), s32[]{:S(2)}) async-start(), calls=%async_computation | async-start | bytes 4227072 | tf_op jit(solution)/shard_map/all_gather | solution.py:48
  254.5 6.4 %copy-start = (s32[32]{0:T(128)S(1)}, s32[32]{0:T(128)}, u32[]{:S(2)}) copy-start(s32[32]{0:T(128)} %param.25) | copy-start | bytes 388
  254.5 6.4 %copy-start.1 = (s32[32]{0:T(128)S(1)}, s32[32]{0:T(128)}, u32[]{:S(2)}) copy-start(s32[32]{0:T(128)} %param.23) | copy-start | bytes 388
  254.5 6.5 %copy-start.5 = (s32[32]{0:T(128)S(1)}, s32[32]{0:T(128)}, u32[]{:S(2)}) copy-start(s32[32]{0:T(128)} %param.24) | copy-start | bytes 388
  260.9 15.3 %copy-start.2 = (s32[160]{0:T(256)S(1)}, s32[160]{0:T(256)}, u32[]{:S(2)}) copy-start(s32[160]{0:T(256)} %param.21) | copy-start | bytes 1924
  261.0 15.3 %copy-start.3 = (s32[160]{0:T(256)S(1)}, s32[160]{0:T(256)}, u32[]{:S(2)}) copy-start(s32[160]{0:T(256)} %param.19) | copy-start | bytes 1924
  261.0 15.2 %copy-start.4 = (s32[160]{0:T(256)S(1)}, s32[160]{0:T(256)}, u32[]{:S(2)}) copy-start(s32[160]{0:T(256)} %param.20) | copy-start | bytes 1924
Sparse Core Ops, SparseCore 0:
  10.1 244.3 all-gather.1
where the time goes:
time: 392 us; the launch traced here: 385 us
  waiting for transfers between devices  242 us (62%)
  local copies, waits for them, and re-layouts  78.1 us (20%)
  matrix products  40.9 us (10%)
  between operations  15.5 us (4%)
  other arithmetic  7.3 us (2%)
    all_gather x1, waiting for transfers between devices, shards(): gathered = lax.all_gather(kept_amps, 'col', axis=1, tiled=True)  242 us
    gather x23, local copies, waits for them, and re-layouts, one_round(): picked = jnp.take(blocks, kind_part, axis=1)  64 us
    dot_general x23, matrix products, one_round(): jnp.einsum('rtk,tkc->rtc', picked, tile_part, preferred_element_type=jnp....  30.4 us
    dot_general x23, matrix products, one_round(): return acc + jnp.einsum('rtc,to->roc', prod, weights)  10.5 us
    unnamed x15, local copies, waits for them, and re-layouts  7.96 us
  transfers between devices with their start and end apart: 1, of which 1 were waited for; matrix products, arithmetic and copies ran while one was open for 1% of the time, Pallas kernels for 0%

commit v1 on v0

v1 whole, which is shorter than its diff:
```python
import functools

import jax
import jax.numpy as jnp
import numpy as np
from jax import lax
from jax.experimental import pallas as pl
from jax.experimental.pallas import tpu as pltpu
from jax.sharding import PartitionSpec as P

TILE = 128
OB = 4
NY, NZH, NZL, NC = 4, 4, 4, 2
LINE = NZH * NZL
WIDE = 4
OWN_CHUNK = 16


def split_col(i):
    return i // (LINE * NC), (i // (NZL * NC)) % NZH, (i // NC) % NZL, i % NC


def join_col(y, zh, zl, c):
    return ((y * NZH + zh) * NZL + zl) * NC + c


def shift(dy=0, dzh=0, dzl=0, dc=0):
    pairs = []
    for i in range(NY * LINE * NC):
        y, zh, zl, c = split_col(i)
        j = join_col((y + dy) % NY, (zh + dzh) % NZH, (zl + dzl) % NZL, (c + dc) % NC)
        pairs.append((i, j))
    return pairs


def move(x, **d):
    return lax.ppermute(x, "col", shift(**d))


def prep_kernel(slots_own, slots_help, own_k, own_out, own_live, help_k, help_out, help_live,
                table, lists, counts):
    del slots_own, slots_help
    cap = lists.shape[0] // 3

    def scan(n, ks, outs, live, base, ns):
        def step(s, ns):
            code = table[ks[s]]
            phase, local = code // 64, code % 64
            entry = ((s + base) * 64 + local) * 8 + outs[s]
            on = live[s]
            new = []
            for p in range(3):
                hit = jnp.where(phase == p, on, 0)
                lists[p * cap + ns[p]] = entry
                new.append(ns[p] + hit)
            return tuple(new)

        return lax.fori_loop(0, n, step, ns)

    n_own, n_help = own_k.shape[0], help_k.shape[0]
    ns = scan(n_own, own_k, own_out, own_live, 0, (0, 0, 0))
    ns = scan(n_help, help_k, help_out, help_live, n_own, ns)
    for p in range(3):
        counts[p] = ns[p]
        for w in range(WIDE):
            lists[p * cap + ns[p] + w] = OB


def task_kernel(phase, cap, last, lists, counts, own_tiles, help_tiles, acc_in, *rest):
    n_pieces = len(rest) - 7
    pieces, out = rest[:n_pieces], rest[n_pieces]
    amps, tiles, acc, own_sems, help_sem, amp_sems = rest[n_pieces + 1:]
    n_own = own_tiles.shape[0]
    copies = []
    for j, piece in enumerate(pieces):
        copies.append(pltpu.make_async_copy(piece, amps.at[pl.ds(j * LINE, LINE)], amp_sems.at[j]))
    for j in range(n_own // OWN_CHUNK):
        part = pl.ds(j * OWN_CHUNK, OWN_CHUNK)
        copies.append(pltpu.make_async_copy(own_tiles.at[part], tiles.at[part], own_sems.at[j]))
    copies.append(pltpu.make_async_copy(
        help_tiles, tiles.at[pl.ds(n_own, help_tiles.shape[0])], help_sem.at[0]))
    for copy in copies:
        copy.start()
    acc[pl.ds(0, OB)] = acc_in[...]
    for copy in copies:
        copy.wait()

    def step(g, carry):
        outs, prods = [], []
        for w in range(WIDE):
            entry = lists[phase * cap + g * WIDE + w]
            outs.append(entry % 8)
            a = amps[(entry // 8) % 64]
            b = tiles[entry // 512]
            prods.append(jnp.dot(a, b, preferred_element_type=jnp.float32))
        for w in range(WIDE):
            acc[outs[w]] += prods[w]
        return carry

    lax.fori_loop(0, (counts[phase] + WIDE - 1) // WIDE, step, 0)
    if last:
        for o in range(OB):
            out[:, o * TILE:(o + 1) * TILE] = acc[o].astype(out.dtype)
    else:
        out[...] = acc[pl.ds(0, OB)]


def run_tasks(phase, lists, counts, own_tiles, help_tiles, acc_in, pieces, last):
    n_own, n_help = own_tiles.shape[0], help_tiles.shape[0]
    n = n_own + n_help
    cap = lists.shape[0] // 3
    if last:
        out_shape = jax.ShapeDtypeStruct((TILE, OB * TILE), jnp.bfloat16)
    else:
        out_shape = jax.ShapeDtypeStruct((OB, TILE, TILE), jnp.float32)
    anywhere = pl.BlockSpec(memory_space=pl.ANY)
    smem = pl.BlockSpec(memory_space=pltpu.SMEM)
    vmem = pl.BlockSpec(memory_space=pltpu.VMEM)
    return pl.pallas_call(
        functools.partial(task_kernel, phase, cap, last),
        out_shape=out_shape,
        in_specs=[smem, smem, anywhere, anywhere, vmem] + [anywhere] * len(pieces),
        out_specs=vmem,
        scratch_shapes=[
            pltpu.VMEM((len(pieces) * LINE, TILE, TILE), jnp.bfloat16),
            pltpu.VMEM((n, TILE, TILE), jnp.bfloat16),
            pltpu.VMEM((OB + 1, TILE, TILE), jnp.float32),
            pltpu.SemaphoreType.DMA((n_own // OWN_CHUNK,)),
            pltpu.SemaphoreType.DMA((1,)),
            pltpu.SemaphoreType.DMA((len(pieces),)),
        ],
        compiler_params=pltpu.CompilerParams(vmem_limit_bytes=24 << 20),
        cost_estimate=pl.CostEstimate(flops=n // 3 * 2 * TILE ** 3, bytes_accessed=8 << 20, transcendentals=0),
        name=f"tasks{phase}",
    )(lists, counts, own_tiles, help_tiles, acc_in, *pieces)


def prepare(own_k, own_out, own_live, help_k, help_out, help_live):
    me = lax.axis_index("col")
    y, zh, zl, c = split_col(me)
    ky, kzh, kzl, kc = split_col(jnp.arange(NY * LINE * NC, dtype=jnp.int32))
    dy, dzh, dzl, dc = (y - ky) % NY, (zh - kzh) % NZH, (zl - kzl) % NZL, (c - kc) % NC
    near = dzl * NZH + dzh
    local = jnp.where(dy == 0, dc, dy - 1) * LINE + near
    phase = jnp.where(dy == 0, 0, 1 + dc)
    table = phase * 64 + local
    n = own_k.shape[0] + help_k.shape[0]
    smem = pl.BlockSpec(memory_space=pltpu.SMEM)
    args = (own_k, own_out, own_live, help_k, help_out, help_live, table)

    def kernel(*refs):
        prep_kernel(None, None, *refs)

    return pl.pallas_call(
        kernel,
        out_shape=(jax.ShapeDtypeStruct((3 * (n + 8),), jnp.int32), jax.ShapeDtypeStruct((8,), jnp.int32)),
        in_specs=[smem] * len(args),
        out_specs=(smem, smem),
        name="prep",
        cost_estimate=pl.CostEstimate(flops=0, bytes_accessed=8 << 20, transcendentals=0),
    )(*args)


def shards(
    amplitudes,
    amp_kept,
    own_tiles,
    own_k,
    own_out,
    own_live,
    help_tiles,
    help_k,
    help_out,
    help_live,
):
    kept = amplitudes * amp_kept.astype(jnp.bfloat16)
    lists, counts = prepare(own_k, own_out, own_live, help_k, help_out, help_live)
    first = jnp.stack([kept] + [move(kept, dzh=k) for k in (1, 2, 3)])
    line = jnp.concatenate([first] + [move(first, dzl=k) for k in (1, 2, 3)])
    ys = {k: move(line, dy=k) for k in (1, 3, 2)}
    line_c = move(line, dc=1)
    ys_c = {k: move(ys[k], dc=1) for k in (1, 3, 2)}
    tasks = functools.partial(run_tasks, lists=lists, counts=counts, own_tiles=own_tiles, help_tiles=help_tiles)
    acc = jnp.zeros((OB, TILE, TILE), jnp.float32)
    acc = tasks(0, acc_in=acc, pieces=[line, line_c], last=False)
    acc = tasks(1, acc_in=acc, pieces=[ys[1], ys[2], ys[3]], last=False)
    return tasks(2, acc_in=acc, pieces=[ys_c[1], ys_c[2], ys_c[3]], last=True)


def solution(mesh):
    return jax.shard_map(
        shards,
        mesh=mesh,
        in_specs=(
            P("row", "col"),
            P("row", "col"),
            P("col", None, None),
            P("col"),
            P("col"),
            P("col"),
            P("col", None, None),
            P("col"),
            P("col"),
            P("col"),
        ),
        out_specs=P("row", "col"),
        check_vma=False,
    )
```

time: 392 us -> 112 us (0.29)
  the two profiles are of different devices: /device:TPU:9 before, /device:TPU:1 now
where the time goes in v1:
time: 112 us; the launch traced here: 110 us
  starting transfers between devices  69.6 us (62%)
  Pallas kernels  18.8 us (17%)
  waiting for transfers between devices  14.6 us (13%)
  local copies, waits for them, and re-layouts  5.12 us (5%)
  other arithmetic  1.33 us (1%)
    ppermute x13, starting transfers between devices, move(): return lax.ppermute(x, 'col', shift(**d))  69.6 us
    ppermute x13, waiting for transfers between devices, move(): return lax.ppermute(x, 'col', shift(**d))  14.6 us
    pallas_call x3, Pallas kernels, run_tasks(): pl.pallas_call(functools.partial(task_kernel, phase, cap, last), out_shap...  13.4 us
    pallas_call x1, Pallas kernels, prepare(): pl.pallas_call(kernel, out_shape=(jax.ShapeDtypeStruct((3 * (n + 8),), jn...  5.31 us
    unnamed x13, local copies, waits for them, and re-layouts  5.09 us
  transfers between devices with their start and end apart: 13, of which 4 were waited for; matrix products, arithmetic and copies ran while one was open for 1% of the time, Pallas kernels for 12%

profile of v1, /device:TPU:1, one launch (start us, length us, event | category | flops | bytes accessed | tf_op | source)
XLA Modules:
  0.0 110.4 jit_solution(7501866839168518343)
XLA Ops:
  0.7 0.8 constant_dynamic-update-slice_fusion.6
  1.4 9.6 %collective-permute-start = (bf16[128,128]{1,0:T(8,128)(2,1)S(1)}, bf16[128,128]{1,0:T(8,128)(2,1)S(1)}, u32[]{:S(2)}, u32[]{:S(2)}) collective-permute-start(bf16[128,128]{1,0:T(8,128)(2,1)S(1)} %get-tuple-element.10), channel_id=1, source_target_pairs={{0,8},{1,9},{2,10},{3,11},{4,12},{5,13},{6,14},{7,15},{8,16},{9,17... | collective-permute-start | bytes 98312 | tf_op jit(solution)/shard_map/ppermute | solution.py:37
  11.1 15.4 %collective-permute-start.1 = (bf16[128,128]{1,0:T(8,128)(2,1)S(1)}, bf16[128,128]{1,0:T(8,128)(2,1)S(1)}, u32[]{:S(2)}, u32[]{:S(2)}) collective-permute-start(bf16[128,128]{1,0:T(8,128)(2,1)S(1)} %get-tuple-element.10), channel_id=1, source_target_pairs={{0,16},{1,17},{2,18},{3,19},{4,20},{5,21},{6,22},{7,23},{8,24},{9,... | collective-permute-start | bytes 98312 | tf_op jit(solution)/shard_map/ppermute | solution.py:37
  26.5 5.2 %collective-permute-start.2 = (bf16[128,128]{1,0:T(8,128)(2,1)S(1)}, bf16[128,128]{1,0:T(8,128)(2,1)S(1)}, u32[]{:S(2)}, u32[]{:S(2)}) collective-permute-start(bf16[128,128]{1,0:T(8,128)(2,1)S(1)} %get-tuple-element.10), channel_id=1, source_target_pairs={{0,24},{1,25},{2,26},{3,27},{4,28},{5,29},{6,30},{7,31},{8,0},{9,1... | collective-permute-start | bytes 98312 | tf_op jit(solution)/shard_map/ppermute | solution.py:37
  31.7 0.0 collective-permute-done
  31.7 0.0 collective-permute-done.1
  31.7 3.4 %collective-permute-done.2 = bf16[128,128]{1,0:T(8,128)(2,1)S(1)} collective-permute-done((bf16[128,128]{1,0:T(8,128)(2,1)S(1)}, bf16[128,128]{1,0:T(8,128)(2,1)S(1)}, u32[]{:S(2)}, u32[]{:S(2)}) %collective-permute-start.2) | collective-permute-done | bytes 32800 | tf_op jit(solution)/shard_map/ppermute | solution.py:37
  35.1 3.6 %collective-permute-start.3 = (bf16[4,128,128]{2,1,0:T(8,128)(2,1)S(1)}, bf16[4,128,128]{2,1,0:T(8,128)(2,1)S(1)}, u32[]{:S(2)}, u32[]{:S(2)}) collective-permute-start(bf16[4,128,128]{2,1,0:T(8,128)(2,1)S(1)} %pad_maximum_fusion), channel_id=1, source_target_pairs={{0,2},{1,3},{2,4},{3,5},{4,6},{5,7},{6,0},{7,1},{8,10},{9,11},{10,... | collective-permute-start | bytes 393224 | tf_op jit(solution)/shard_map/ppermute | solution.py:37
  38.7 5.3 %collective-permute-start.4 = (bf16[4,128,128]{2,1,0:T(8,128)(2,1)S(1)}, bf16[4,128,128]{2,1,0:T(8,128)(2,1)S(1)}, u32[]{:S(2)}, u32[]{:S(2)}) collective-permute-start(bf16[4,128,128]{2,1,0:T(8,128)(2,1)S(1)} %pad_maximum_fusion), channel_id=1, source_target_pairs={{0,4},{1,5},{2,6},{3,7},{4,0},{5,1},{6,2},{7,3},{8,12},{9,13},{10,... | collective-permute-start | bytes 393224 | tf_op jit(solution)/shard_map/ppermute | solution.py:37
  44.0 2.6 %collective-permute-start.5 = (bf16[4,128,128]{2,1,0:T(8,128)(2,1)S(1)}, bf16[4,128,128]{2,1,0:T(8,128)(2,1)S(1)}, u32[]{:S(2)}, u32[]{:S(2)}) collective-permute-start(bf16[4,128,128]{2,1,0:T(8,128)(2,1)S(1)} %pad_maximum_fusion), channel_id=1, source_target_pairs={{0,6},{1,7},{2,0},{3,1},{4,2},{5,3},{6,4},{7,5},{8,14},{9,15},{10,... | collective-permute-start | bytes 393224 | tf_op jit(solution)/shard_map/ppermute | solution.py:37
  46.8 4.1 %collective-permute-done.4 = bf16[4,128,128]{2,1,0:T(8,128)(2,1)S(1)} collective-permute-done((bf16[4,128,128]{2,1,0:T(8,128)(2,1)S(1)}, bf16[4,128,128]{2,1,0:T(8,128)(2,1)S(1)}, u32[]{:S(2)}, u32[]{:S(2)}) %collective-permute-start.4) | collective-permute-done | bytes 131104 | tf_op jit(solution)/shard_map/ppermute | solution.py:37
  50.9 0.6 collective-permute-done.5
  51.5 3.8 %collective-permute-start.7 = (bf16[16,128,128]{2,1,0:T(8,128)(2,1)S(1)}, bf16[16,128,128]{2,1,0:T(8,128)(2,1)S(1)}, u32[]{:S(2)}, u32[]{:S(2)}) collective-permute-start(bf16[16,128,128]{2,1,0:T(8,128)(2,1)S(1)} %constant_dynamic-update-slice_fusion.rest_0_), channel_id=1, source_target_pairs={{0,32},{1,33},{2,34},{3,35},{4,36},{5,37},{6,38},{7,39},{8,40},{9,... | collective-permute-start | bytes 1572872 | tf_op jit(solution)/shard_map/ppermute | solution.py:37
  55.4 4.5 %collective-permute-start.8 = (bf16[16,128,128]{2,1,0:T(8,128)(2,1)S(1)}, bf16[16,128,128]{2,1,0:T(8,128)(2,1)S(1)}, u32[]{:S(2)}, u32[]{:S(2)}) collective-permute-start(bf16[16,128,128]{2,1,0:T(8,128)(2,1)S(1)} %constant_dynamic-update-slice_fusion.rest_0_), channel_id=1, source_target_pairs={{0,64},{1,65},{2,66},{3,67},{4,68},{5,69},{6,70},{7,71},{8,72},{9,... | collective-permute-start | bytes 1572872 | tf_op jit(solution)/shard_map/ppermute | solution.py:37
  59.9 3.0 %collective-permute-start.9 = (bf16[16,128,128]{2,1,0:T(8,128)(2,1)S(1)}, bf16[16,128,128]{2,1,0:T(8,128)(2,1)S(1)}, u32[]{:S(2)}, u32[]{:S(2)}) collective-permute-start(bf16[16,128,128]{2,1,0:T(8,128)(2,1)S(1)} %constant_dynamic-update-slice_fusion.rest_0_), channel_id=1, source_target_pairs={{0,96},{1,97},{2,98},{3,99},{4,100},{5,101},{6,102},{7,103},{8,104... | collective-permute-start | bytes 1572872 | tf_op jit(solution)/shard_map/ppermute | solution.py:37
  62.9 4.6 %collective-permute-start.6 = (bf16[16,128,128]{2,1,0:T(8,128)(2,1)S(1)}, bf16[16,128,128]{2,1,0:T(8,128)(2,1)S(1)}, u32[]{:S(2)}, u32[]{:S(2)}) collective-permute-start(bf16[16,128,128]{2,1,0:T(8,128)(2,1)S(1)} %constant_dynamic-update-slice_fusion.rest_0_), channel_id=1, source_target_pairs={{0,1},{1,0},{2,3},{3,2},{4,5},{5,4},{6,7},{7,6},{8,9},{9,8},{10,11... | collective-permute-start | bytes 1572872 | tf_op jit(solution)/shard_map/ppermute | solution.py:37
  67.5 0.0 collective-permute-done.7.rest_0_
  67.5 5.3 %collective-permute-start.10 = (bf16[16,128,128]{2,1,0:T(8,128)(2,1)S(1)}, bf16[16,128,128]{2,1,0:T(8,128)(2,1)S(1)}, u32[]{:S(2)}, u32[]{:S(2)}) collective-permute-start(bf16[16,128,128]{2,1,0:T(8,128)(2,1)S(1)} %collective-permute-done.7.rest_0_), channel_id=1, source_target_pairs={{0,1},{1,0},{2,3},{3,2},{4,5},{5,4},{6,7},{7,6},{8,9},{9,8},{10,11... | collective-permute-start | bytes 1572872 | tf_op jit(solution)/shard_map/ppermute | solution.py:37
  72.8 6.5 %collective-permute-done.8.rest_1_ = bf16[16,128,128]{2,1,0:T(8,128)(2,1)S(1)} collective-permute-done((bf16[16,128,128]{2,1,0:T(8,128)(2,1)S(1)}, bf16[16,128,128]{2,1,0:T(8,128)(2,1)S(1)}, u32[]{:S(2)}, u32[]{:S(2)}) %collective-permute-start.8) | collective-permute-done | bytes 524320 | tf_op jit(solution)/shard_map/ppermute | solution.py:37
  79.3 4.7 %collective-permute-start.11 = (bf16[16,128,128]{2,1,0:T(8,128)(2,1)S(1)}, bf16[16,128,128]{2,1,0:T(8,128)(2,1)}, u32[]{:S(2)}, u32[]{:S(2)}) collective-permute-start(bf16[16,128,128]{2,1,0:T(8,128)(2,1)S(1)} %collective-permute-done.8.rest_1_), channel_id=1, source_target_pairs={{0,1},{1,0},{2,3},{3,2},{4,5},{5,4},{6,7},{7,6},{8,9},{9,8},{10,11... | collective-permute-start | bytes 1572872 | tf_op jit(solution)/shard_map/ppermute | solution.py:37
  84.0 1.9 %collective-permute-start.12 = (bf16[16,128,128]{2,1,0:T(8,128)(2,1)S(1)}, bf16[16,128,128]{2,1,0:T(8,128)(2,1)}, u32[]{:S(2)}, u32[]{:S(2)}) collective-permute-start(bf16[16,128,128]{2,1,0:T(8,128)(2,1)S(1)} %collective-permute-done.9.rest_2_), channel_id=1, source_target_pairs={{0,1},{1,0},{2,3},{3,2},{4,5},{5,4},{6,7},{7,6},{8,9},{9,8},{10,11... | collective-permute-start | bytes 1572872 | tf_op jit(solution)/shard_map/ppermute | solution.py:37
  86.0 0.5 fusion.4.refs_6_
  86.5 5.3 %prep.1 = (s32[600]{0:T(1024)}, s32[8]{0:T(128)}) custom-call(s32[160]{0:T(256)} %refs_0_.1, s32[160]{0:T(256)} %refs_1_.1, s32[160]{0:T(256)} %refs_2_.1, s32[32]{0:T(128)} %refs_3_.1, s32[32]{0:T(128)} %refs_4_.1, s32[32]{0:T(128)} %refs_5_.1, s32[128]{0:T(128)} %fusion.4.refs_6_), custom_call_target="tpu_custom_call" | custom-call | bytes 8388608 | tf_op jit(solution)/shard_map/prep/pallas_call | solution.py:154
  91.8 0.0 collective-permute-done.6.rest_1_
  91.9 0.0 copy-start
  91.9 2.5 %copy-done = bf16[160,128,128]{2,1,0:T(8,128)(2,1)S(1)} copy-done((bf16[160,128,128]{2,1,0:T(8,128)(2,1)S(1)}, bf16[160,128,128]{2,1,0:T(8,128)(2,1)}, u32[]{:S(2)}) %copy-start) | copy-done | bytes 5242904
  94.4 1.2 %copy-done.1 = bf16[32,128,128]{2,1,0:T(8,128)(2,1)S(1)} copy-done((bf16[32,128,128]{2,1,0:T(8,128)(2,1)S(1)}, bf16[32,128,128]{2,1,0:T(8,128)(2,1)}, u32[]{:S(2)}) %copy-start.1) | copy-done | bytes 1048600
  95.6 0.7 copy-done.2
  96.3 0.6 copy-done.3
  96.9 3.7 %tasks0.1.acc_in = f32[4,128,128]{2,1,0:T(8,128)S(1)} custom-call(s32[600]{0:T(1024)S(1)} %copy-done.2, s32[8]{0:T(128)S(1)} %copy-done.3, bf16[160,128,128]{2,1,0:T(8,128)(2,1)S(1)} %copy-done, bf16[32,128,128]{2,1,0:T(8,128)(2,1)S(1)} %copy-done.1, f32[4,128,128]{2,1,0:T(8,128)S(1)} %broadcast_in_dim.5.acc_in, ...), custom_call_target="tpu_custom_call" | custom-call | flops 268435456 | bytes 8388608 | tf_op jit(solution)/shard_map/tasks0/pallas_call | solution.py:119
  100.7 4.0 %tasks1.1.acc_in = f32[4,128,128]{2,1,0:T(8,128)S(1)} custom-call(s32[600]{0:T(1024)S(1)} %copy-done.2, s32[8]{0:T(128)S(1)} %copy-done.3, bf16[160,128,128]{2,1,0:T(8,128)(2,1)S(1)} %copy-done, bf16[32,128,128]{2,1,0:T(8,128)(2,1)S(1)} %copy-done.1, f32[4,128,128]{2,1,0:T(8,128)S(1)} %tasks0.1.acc_in, ...), custom_call_target="tpu_custom_call" | custom-call | flops 268435456 | bytes 8388608 | tf_op jit(solution)/shard_map/tasks1/pallas_call | solution.py:119
  104.7 5.7 %tasks2.1 = bf16[128,512]{1,0:T(8,128)(2,1)} custom-call(s32[600]{0:T(1024)S(1)} %copy-done.2, s32[8]{0:T(128)S(1)} %copy-done.3, bf16[160,128,128]{2,1,0:T(8,128)(2,1)S(1)} %copy-done, bf16[32,128,128]{2,1,0:T(8,128)(2,1)S(1)} %copy-done.1, f32[4,128,128]{2,1,0:T(8,128)S(1)} %tasks1.1.acc_in, bf16[16,128,128]{2,1,0:T(8,128)(2,1)S(1)} %collective-permute-done.10.rest_0_, ...), custom_call_target="tpu_custom_call" | custom-call | flops 268435456 | bytes 8388608 | tf_op jit(solution)/shard_map/tasks2/pallas_call | solution.py:119
  (16 shorter events, 0.1 us)
Async XLA Ops:
  1.4 30.3 %collective-permute-start = (bf16[128,128]{1,0:T(8,128)(2,1)S(1)}, bf16[128,128]{1,0:T(8,128)(2,1)S(1)}, u32[]{:S(2)}, u32[]{:S(2)}) collective-permute-start(bf16[128,128]{1,0:T(8,128)(2,1)S(1)} %get-tuple-element.10), channel_id=1, source_target_pairs={{0,8},{1,9},{2,10},{3,11},{4,12},{5,13},{6,14},{7,15},{8,16},{9,17... | collective-permute-start | bytes 98312 | tf_op jit(solution)/shard_map/ppermute | solution.py:37
  11.1 20.7 %collective-permute-start.1 = (bf16[128,128]{1,0:T(8,128)(2,1)S(1)}, bf16[128,128]{1,0:T(8,128)(2,1)S(1)}, u32[]{:S(2)}, u32[]{:S(2)}) collective-permute-start(bf16[128,128]{1,0:T(8,128)(2,1)S(1)} %get-tuple-element.10), channel_id=1, source_target_pairs={{0,16},{1,17},{2,18},{3,19},{4,20},{5,21},{6,22},{7,23},{8,24},{9,... | collective-permute-start | bytes 98312 | tf_op jit(solution)/shard_map/ppermute | solution.py:37
  26.5 8.6 %collective-permute-start.2 = (bf16[128,128]{1,0:T(8,128)(2,1)S(1)}, bf16[128,128]{1,0:T(8,128)(2,1)S(1)}, u32[]{:S(2)}, u32[]{:S(2)}) collective-permute-start(bf16[128,128]{1,0:T(8,128)(2,1)S(1)} %get-tuple-element.10), channel_id=1, source_target_pairs={{0,24},{1,25},{2,26},{3,27},{4,28},{5,29},{6,30},{7,31},{8,0},{9,1... | collective-permute-start | bytes 98312 | tf_op jit(solution)/shard_map/ppermute | solution.py:37
  35.1 11.6 %collective-permute-start.3 = (bf16[4,128,128]{2,1,0:T(8,128)(2,1)S(1)}, bf16[4,128,128]{2,1,0:T(8,128)(2,1)S(1)}, u32[]{:S(2)}, u32[]{:S(2)}) collective-permute-start(bf16[4,128,128]{2,1,0:T(8,128)(2,1)S(1)} %pad_maximum_fusion), channel_id=1, source_target_pairs={{0,2},{1,3},{2,4},{3,5},{4,6},{5,7},{6,0},{7,1},{8,10},{9,11},{10,... | collective-permute-start | bytes 393224 | tf_op jit(solution)/shard_map/ppermute | solution.py:37
  38.7 12.2 %collective-permute-start.4 = (bf16[4,128,128]{2,1,0:T(8,128)(2,1)S(1)}, bf16[4,128,128]{2,1,0:T(8,128)(2,1)S(1)}, u32[]{:S(2)}, u32[]{:S(2)}) collective-permute-start(bf16[4,128,128]{2,1,0:T(8,128)(2,1)S(1)} %pad_maximum_fusion), channel_id=1, source_target_pairs={{0,4},{1,5},{2,6},{3,7},{4,0},{5,1},{6,2},{7,3},{8,12},{9,13},{10,... | collective-permute-start | bytes 393224 | tf_op jit(solution)/shard_map/ppermute | solution.py:37
  44.0 7.5 %collective-permute-start.5 = (bf16[4,128,128]{2,1,0:T(8,128)(2,1)S(1)}, bf16[4,128,128]{2,1,0:T(8,128)(2,1)S(1)}, u32[]{:S(2)}, u32[]{:S(2)}) collective-permute-start(bf16[4,128,128]{2,1,0:T(8,128)(2,1)S(1)} %pad_maximum_fusion), channel_id=1, source_target_pairs={{0,6},{1,7},{2,0},{3,1},{4,2},{5,3},{6,4},{7,5},{8,14},{9,15},{10,... | collective-permute-start | bytes 393224 | tf_op jit(solution)/shard_map/ppermute | solution.py:37
  51.5 16.0 %collective-permute-start.7 = (bf16[16,128,128]{2,1,0:T(8,128)(2,1)S(1)}, bf16[16,128,128]{2,1,0:T(8,128)(2,1)S(1)}, u32[]{:S(2)}, u32[]{:S(2)}) collective-permute-start(bf16[16,128,128]{2,1,0:T(8,128)(2,1)S(1)} %constant_dynamic-update-slice_fusion.rest_0_), channel_id=1, source_target_pairs={{0,32},{1,33},{2,34},{3,35},{4,36},{5,37},{6,38},{7,39},{8,40},{9,... | collective-permute-start | bytes 1572872 | tf_op jit(solution)/shard_map/ppermute | solution.py:37
  55.4 23.9 %collective-permute-start.8 = (bf16[16,128,128]{2,1,0:T(8,128)(2,1)S(1)}, bf16[16,128,128]{2,1,0:T(8,128)(2,1)S(1)}, u32[]{:S(2)}, u32[]{:S(2)}) collective-permute-start(bf16[16,128,128]{2,1,0:T(8,128)(2,1)S(1)} %constant_dynamic-update-slice_fusion.rest_0_), channel_id=1, source_target_pairs={{0,64},{1,65},{2,66},{3,67},{4,68},{5,69},{6,70},{7,71},{8,72},{9,... | collective-permute-start | bytes 1572872 | tf_op jit(solution)/shard_map/ppermute | solution.py:37
  59.9 24.1 %collective-permute-start.9 = (bf16[16,128,128]{2,1,0:T(8,128)(2,1)S(1)}, bf16[16,128,128]{2,1,0:T(8,128)(2,1)S(1)}, u32[]{:S(2)}, u32[]{:S(2)}) collective-permute-start(bf16[16,128,128]{2,1,0:T(8,128)(2,1)S(1)} %constant_dynamic-update-slice_fusion.rest_0_), channel_id=1, source_target_pairs={{0,96},{1,97},{2,98},{3,99},{4,100},{5,101},{6,102},{7,103},{8,104... | collective-permute-start | bytes 1572872 | tf_op jit(solution)/shard_map/ppermute | solution.py:37
  62.9 28.9 %collective-permute-start.6 = (bf16[16,128,128]{2,1,0:T(8,128)(2,1)S(1)}, bf16[16,128,128]{2,1,0:T(8,128)(2,1)S(1)}, u32[]{:S(2)}, u32[]{:S(2)}) collective-permute-start(bf16[16,128,128]{2,1,0:T(8,128)(2,1)S(1)} %constant_dynamic-update-slice_fusion.rest_0_), channel_id=1, source_target_pairs={{0,1},{1,0},{2,3},{3,2},{4,5},{5,4},{6,7},{7,6},{8,9},{9,8},{10,11... | collective-permute-start | bytes 1572872 | tf_op jit(solution)/shard_map/ppermute | solution.py:37
  67.5 37.1 %collective-permute-start.10 = (bf16[16,128,128]{2,1,0:T(8,128)(2,1)S(1)}, bf16[16,128,128]{2,1,0:T(8,128)(2,1)S(1)}, u32[]{:S(2)}, u32[]{:S(2)}) collective-permute-start(bf16[16,128,128]{2,1,0:T(8,128)(2,1)S(1)} %collective-permute-done.7.rest_0_), channel_id=1, source_target_pairs={{0,1},{1,0},{2,3},{3,2},{4,5},{5,4},{6,7},{7,6},{8,9},{9,8},{10,11... | collective-permute-start | bytes 1572872 | tf_op jit(solution)/shard_map/ppermute | solution.py:37
  79.3 25.4 %collective-permute-start.11 = (bf16[16,128,128]{2,1,0:T(8,128)(2,1)S(1)}, bf16[16,128,128]{2,1,0:T(8,128)(2,1)}, u32[]{:S(2)}, u32[]{:S(2)}) collective-permute-start(bf16[16,128,128]{2,1,0:T(8,128)(2,1)S(1)} %collective-permute-done.8.rest_1_), channel_id=1, source_target_pairs={{0,1},{1,0},{2,3},{3,2},{4,5},{5,4},{6,7},{7,6},{8,9},{9,8},{10,11... | collective-permute-start | bytes 1572872 | tf_op jit(solution)/shard_map/ppermute | solution.py:37
  84.0 20.7 %collective-permute-start.12 = (bf16[16,128,128]{2,1,0:T(8,128)(2,1)S(1)}, bf16[16,128,128]{2,1,0:T(8,128)(2,1)}, u32[]{:S(2)}, u32[]{:S(2)}) collective-permute-start(bf16[16,128,128]{2,1,0:T(8,128)(2,1)S(1)} %collective-permute-done.9.rest_2_), channel_id=1, source_target_pairs={{0,1},{1,0},{2,3},{3,2},{4,5},{5,4},{6,7},{7,6},{8,9},{9,8},{10,11... | collective-permute-start | bytes 1572872 | tf_op jit(solution)/shard_map/ppermute | solution.py:37
  91.9 2.5 %copy-start = (bf16[160,128,128]{2,1,0:T(8,128)(2,1)S(1)}, bf16[160,128,128]{2,1,0:T(8,128)(2,1)}, u32[]{:S(2)}) copy-start(bf16[160,128,128]{2,1,0:T(8,128)(2,1)} %own_tiles.5) | copy-start | bytes 15728644
  94.4 1.2 %copy-start.1 = (bf16[32,128,128]{2,1,0:T(8,128)(2,1)S(1)}, bf16[32,128,128]{2,1,0:T(8,128)(2,1)}, u32[]{:S(2)}) copy-start(bf16[32,128,128]{2,1,0:T(8,128)(2,1)} %help_tiles.5) | copy-start | bytes 3145732
  95.6 0.7 copy-start.2
  96.3 0.6 copy-start.3

commit v2 on v0

v2 whole, which is shorter than its diff:
```python
import functools

import jax
import jax.numpy as jnp
import numpy as np
from jax import lax
from jax.experimental import pallas as pl
from jax.experimental.pallas import tpu as pltpu
from jax.sharding import PartitionSpec as P

TILE = 128
OB = 4
NY, NZH, NZL, NC = 4, 4, 4, 2
LINE = NZH * NZL
PIECES = NC * NY
WIDE = 4


def split_col(i):
    return i // (LINE * NC), (i // (NZL * NC)) % NZH, (i // NC) % NZL, i % NC


def join_col(y, zh, zl, c):
    return ((y * NZH + zh) * NZL + zl) * NC + c


def shift(dy=0, dzh=0, dzl=0, dc=0):
    pairs = []
    for i in range(NY * LINE * NC):
        y, zh, zl, c = split_col(i)
        j = join_col((y + dy) % NY, (zh + dzh) % NZH, (zl + dzl) % NZL, (c + dc) % NC)
        pairs.append((i, j))
    return pairs


def move(x, **d):
    return lax.ppermute(x, "col", shift(**d))


def prep_kernel(own_k, own_out, own_live, help_k, help_out, help_live, table, own_tiles, help_tiles,
                lists, counts, tiles, sems, *held):
    n_own, n_help = own_k.shape[0], help_k.shape[0]
    cap = lists.shape[0] // PIECES
    loads = []
    for j, ref in enumerate((own_k, own_out, own_live, help_k, help_out, help_live, table)):
        loads.append(pltpu.make_async_copy(ref, held[j], sems.at[2 + j]))
        loads[j].start()
    own_k, own_out, own_live, help_k, help_out, help_live, table = held
    fetch_own = pltpu.make_async_copy(own_tiles, tiles.at[pl.ds(0, n_own)], sems.at[0])
    fetch_help = pltpu.make_async_copy(help_tiles, tiles.at[pl.ds(n_own, n_help)], sems.at[1])
    fetch_own.start()
    fetch_help.start()
    for p in range(PIECES):
        counts[p] = 0
    for load in loads:
        load.wait()

    def scan(ks, outs, live, base):
        def step(s, carry):
            code = table[ks[s]]
            p = code // LINE
            n = counts[p]
            lists[p * cap + n] = ((s + base) * LINE + code % LINE) * 8 + outs[s]
            counts[p] = n + live[s]
            return carry

        lax.fori_loop(0, ks.shape[0], step, 0)

    scan(own_k, own_out, own_live, 0)
    scan(help_k, help_out, help_live, n_own)
    for p in range(PIECES):
        for w in range(WIDE):
            lists[p * cap + counts[p] + w] = OB
    fetch_own.wait()
    fetch_help.wait()


def task_kernel(ids, last, lists, counts, tiles, acc_in, *rest):
    pieces, out, acc = rest[:len(ids)], rest[-2], rest[-1]
    cap = lists.shape[0] // PIECES
    acc[pl.ds(0, OB)] = acc_in[...]
    for p, amps in zip(ids, pieces):

        def step(g, carry, p=p, amps=amps):
            outs, prods = [], []
            for w in range(WIDE):
                entry = lists[p * cap + g * WIDE + w]
                outs.append(entry % 8)
                a = amps[(entry // 8) % LINE]
                b = tiles[entry // (8 * LINE)]
                prods.append(jnp.dot(a, b, preferred_element_type=jnp.float32))
            for w in range(WIDE):
                acc[outs[w]] += prods[w]
            return carry

        lax.fori_loop(0, (counts[p] + WIDE - 1) // WIDE, step, 0)
    if last:
        for o in range(OB):
            out[:, o * TILE:(o + 1) * TILE] = acc[o].astype(out.dtype)
    else:
        out[...] = acc[pl.ds(0, OB)]


def run_tasks(ids, pieces, acc_in, last, lists, counts, tiles):
    if last:
        out_shape = jax.ShapeDtypeStruct((TILE, OB * TILE), jnp.bfloat16)
    else:
        out_shape = jax.ShapeDtypeStruct((OB, TILE, TILE), jnp.float32)
    smem = pl.BlockSpec(memory_space=pltpu.SMEM)
    vmem = pl.BlockSpec(memory_space=pltpu.VMEM)
    n = tiles.shape[0] * len(ids) // PIECES
    return pl.pallas_call(
        functools.partial(task_kernel, ids, last),
        out_shape=out_shape,
        in_specs=[smem, smem, vmem, vmem] + [vmem] * len(pieces),
        out_specs=vmem,
        scratch_shapes=[pltpu.VMEM((OB + 1, TILE, TILE), jnp.float32)],
        compiler_params=pltpu.CompilerParams(vmem_limit_bytes=24 << 20),
        cost_estimate=pl.CostEstimate(flops=n * 20 * TILE ** 3, bytes_accessed=8 << 20, transcendentals=0),
        name="tasks" + "".join(str(p) for p in ids),
    )(lists, counts, tiles, acc_in, *pieces)


def prepare(own_tiles, own_k, own_out, own_live, help_tiles, help_k, help_out, help_live):
    me = lax.axis_index("col")
    y, zh, zl, c = split_col(me)
    ky, kzh, kzl, kc = split_col(jnp.arange(NY * LINE * NC, dtype=jnp.int32))
    dy, dzh, dzl, dc = (y - ky) % NY, (zh - kzh) % NZH, (zl - kzl) % NZL, (c - kc) % NC
    table = ((dc * NY + dy) * NZL + dzl) * NZH + dzh
    n = own_k.shape[0] + help_k.shape[0]
    smem = pl.BlockSpec(memory_space=pltpu.SMEM)
    hbm = pl.BlockSpec(memory_space=pltpu.HBM)
    scalars = (own_k, own_out, own_live, help_k, help_out, help_live, table)
    return pl.pallas_call(
        prep_kernel,
        out_shape=(
            jax.ShapeDtypeStruct((PIECES * (n + 8),), jnp.int32),
            jax.ShapeDtypeStruct((PIECES,), jnp.int32),
            pltpu.VMEM((n, TILE, TILE), jnp.bfloat16),
        ),
        in_specs=[hbm] * 9,
        out_specs=(smem, smem, pl.BlockSpec(memory_space=pltpu.VMEM)),
        scratch_shapes=[pltpu.SemaphoreType.DMA((2 + len(scalars),))]
        + [pltpu.SMEM(v.shape, jnp.int32) for v in scalars],
        name="prep",
        compiler_params=pltpu.CompilerParams(vmem_limit_bytes=24 << 20),
        cost_estimate=pl.CostEstimate(flops=0, bytes_accessed=8 << 20, transcendentals=0),
    )(*[pltpu.with_memory_space_constraint(v, pltpu.HBM) for v in (*scalars, own_tiles, help_tiles)])


def shards(
    amplitudes,
    amp_kept,
    own_tiles,
    own_k,
    own_out,
    own_live,
    help_tiles,
    help_k,
    help_out,
    help_live,
):
    kept = amplitudes * amp_kept.astype(jnp.bfloat16)
    far = [kept] + [move(kept, dzh=k) for k in (1, 2, 3)]
    lists, counts, tiles = prepare(
        own_tiles, own_k, own_out, own_live, help_tiles, help_k, help_out, help_live)
    first = jnp.stack(far)
    line = jnp.concatenate([first] + [move(first, dzl=k) for k in (1, 2, 3)])
    ys = {k: move(line, dy=k) for k in (1, 3, 2)}
    line_c = move(line, dc=1)
    tasks = functools.partial(run_tasks, lists=lists, counts=counts, tiles=tiles)
    acc = jnp.zeros((OB, TILE, TILE), jnp.float32)
    acc = tasks((0, NY), [line, line_c], acc, False)
    ys[1], acc = lax.optimization_barrier((ys[1], acc))
    ys_c = {k: move(ys[k], dc=1) for k in (1, 3, 2)}
    acc = tasks((1, 3, 2), [ys[1], ys[3], ys[2]], acc, False)
    return tasks((NY + 1, NY + 3, NY + 2), [ys_c[1], ys_c[3], ys_c[2]], acc, True)


def solution(mesh):
    return jax.shard_map(
        shards,
        mesh=mesh,
        in_specs=(
            P("row", "col"),
            P("row", "col"),
            P("col", None, None),
            P("col"),
            P("col"),
            P("col"),
            P("col", None, None),
            P("col"),
            P("col"),
            P("col"),
        ),
        out_specs=P("row", "col"),
        check_vma=False,
    )
```

time: 392 us -> 99.2 us (0.25)
  the two profiles are of different devices: /device:TPU:9 before, /device:TPU:25 now
where the time goes in v2:
time: 99.2 us; the launch traced here: 98.7 us
  starting transfers between devices  70.8 us (71%)
  Pallas kernels  16.7 us (17%)
  waiting for transfers between devices  8.75 us (9%)
  other arithmetic  1.32 us (1%)
    ppermute x13, starting transfers between devices, move(): return lax.ppermute(x, 'col', shift(**d))  70.8 us
    pallas_call x3, Pallas kernels, run_tasks(): pl.pallas_call(functools.partial(task_kernel, ids, last), out_shape=out_s...  11.8 us
    ppermute x13, waiting for transfers between devices, move(): return lax.ppermute(x, 'col', shift(**d))  8.75 us
    pallas_call x1, Pallas kernels, prepare(): pl.pallas_call(prep_kernel, out_shape=(jax.ShapeDtypeStruct((PIECES * (n...  4.9 us
  transfers between devices with their start and end apart: 13, of which 2 were waited for; matrix products, arithmetic and copies ran while one was open for 1% of the time, Pallas kernels for 12%

profile of v2, /device:TPU:25, one launch (start us, length us, event | category | flops | bytes accessed | tf_op | source)
XLA Modules:
  0.0 98.7 jit_solution(10444017256902969146)
XLA Ops:
  0.7 0.8 constant_dynamic-update-slice_fusion.6
  1.4 8.8 %collective-permute-start = (bf16[128,128]{1,0:T(8,128)(2,1)S(1)}, bf16[128,128]{1,0:T(8,128)(2,1)S(1)}, u32[]{:S(2)}, u32[]{:S(2)}) collective-permute-start(bf16[128,128]{1,0:T(8,128)(2,1)S(1)} %get-tuple-element.16), channel_id=1, source_target_pairs={{0,8},{1,9},{2,10},{3,11},{4,12},{5,13},{6,14},{7,15},{8,16},{9,17... | collective-permute-start | bytes 98312 | tf_op jit(solution)/shard_map/ppermute | solution.py:37
  10.3 15.4 %collective-permute-start.1 = (bf16[128,128]{1,0:T(8,128)(2,1)S(1)}, bf16[128,128]{1,0:T(8,128)(2,1)S(1)}, u32[]{:S(2)}, u32[]{:S(2)}) collective-permute-start(bf16[128,128]{1,0:T(8,128)(2,1)S(1)} %get-tuple-element.16), channel_id=1, source_target_pairs={{0,16},{1,17},{2,18},{3,19},{4,20},{5,21},{6,22},{7,23},{8,24},{9,... | collective-permute-start | bytes 98312 | tf_op jit(solution)/shard_map/ppermute | solution.py:37
  25.7 5.2 %collective-permute-start.2 = (bf16[128,128]{1,0:T(8,128)(2,1)S(1)}, bf16[128,128]{1,0:T(8,128)(2,1)S(1)}, u32[]{:S(2)}, u32[]{:S(2)}) collective-permute-start(bf16[128,128]{1,0:T(8,128)(2,1)S(1)} %get-tuple-element.16), channel_id=1, source_target_pairs={{0,24},{1,25},{2,26},{3,27},{4,28},{5,29},{6,30},{7,31},{8,0},{9,1... | collective-permute-start | bytes 98312 | tf_op jit(solution)/shard_map/ppermute | solution.py:37
  30.9 0.0 collective-permute-done
  30.9 0.0 collective-permute-done.1
  30.9 3.4 %collective-permute-done.2 = bf16[128,128]{1,0:T(8,128)(2,1)S(1)} collective-permute-done((bf16[128,128]{1,0:T(8,128)(2,1)S(1)}, bf16[128,128]{1,0:T(8,128)(2,1)S(1)}, u32[]{:S(2)}, u32[]{:S(2)}) %collective-permute-start.2) | collective-permute-done | bytes 32800 | tf_op jit(solution)/shard_map/ppermute | solution.py:37
  34.3 3.6 %collective-permute-start.3 = (bf16[4,128,128]{2,1,0:T(8,128)(2,1)S(1)}, bf16[4,128,128]{2,1,0:T(8,128)(2,1)S(1)}, u32[]{:S(2)}, u32[]{:S(2)}) collective-permute-start(bf16[4,128,128]{2,1,0:T(8,128)(2,1)S(1)} %pad_maximum_fusion), channel_id=1, source_target_pairs={{0,2},{1,3},{2,4},{3,5},{4,6},{5,7},{6,0},{7,1},{8,10},{9,11},{10,... | collective-permute-start | bytes 393224 | tf_op jit(solution)/shard_map/ppermute | solution.py:37
  37.9 5.3 %collective-permute-start.4 = (bf16[4,128,128]{2,1,0:T(8,128)(2,1)S(1)}, bf16[4,128,128]{2,1,0:T(8,128)(2,1)S(1)}, u32[]{:S(2)}, u32[]{:S(2)}) collective-permute-start(bf16[4,128,128]{2,1,0:T(8,128)(2,1)S(1)} %pad_maximum_fusion), channel_id=1, source_target_pairs={{0,4},{1,5},{2,6},{3,7},{4,0},{5,1},{6,2},{7,3},{8,12},{9,13},{10,... | collective-permute-start | bytes 393224 | tf_op jit(solution)/shard_map/ppermute | solution.py:37
  43.2 2.6 %collective-permute-start.5 = (bf16[4,128,128]{2,1,0:T(8,128)(2,1)S(1)}, bf16[4,128,128]{2,1,0:T(8,128)(2,1)S(1)}, u32[]{:S(2)}, u32[]{:S(2)}) collective-permute-start(bf16[4,128,128]{2,1,0:T(8,128)(2,1)S(1)} %pad_maximum_fusion), channel_id=1, source_target_pairs={{0,6},{1,7},{2,0},{3,1},{4,2},{5,3},{6,4},{7,5},{8,14},{9,15},{10,... | collective-permute-start | bytes 393224 | tf_op jit(solution)/shard_map/ppermute | solution.py:37
  45.9 0.0 collective-permute-done.3
  45.9 5.4 %collective-permute-done.4 = bf16[4,128,128]{2,1,0:T(8,128)(2,1)S(1)} collective-permute-done((bf16[4,128,128]{2,1,0:T(8,128)(2,1)S(1)}, bf16[4,128,128]{2,1,0:T(8,128)(2,1)S(1)}, u32[]{:S(2)}, u32[]{:S(2)}) %collective-permute-start.4) | collective-permute-done | bytes 131104 | tf_op jit(solution)/shard_map/ppermute | solution.py:37
  51.3 0.0 collective-permute-done.5
  51.3 3.8 %collective-permute-start.7 = (bf16[16,128,128]{2,1,0:T(8,128)(2,1)S(1)}, bf16[16,128,128]{2,1,0:T(8,128)(2,1)S(1)}, u32[]{:S(2)}, u32[]{:S(2)}) collective-permute-start(bf16[16,128,128]{2,1,0:T(8,128)(2,1)S(1)} %constant_dynamic-update-slice_fusion.rest_0_), channel_id=1, source_target_pairs={{0,1},{1,0},{2,3},{3,2},{4,5},{5,4},{6,7},{7,6},{8,9},{9,8},{10,11... | collective-permute-start | bytes 1572872 | tf_op jit(solution)/shard_map/ppermute | solution.py:37
  55.1 2.0 %collective-permute-start.6 = (bf16[16,128,128]{2,1,0:T(8,128)(2,1)S(1)}, bf16[16,128,128]{2,1,0:T(8,128)(2,1)S(1)}, u32[]{:S(2)}, u32[]{:S(2)}) collective-permute-start(bf16[16,128,128]{2,1,0:T(8,128)(2,1)S(1)} %constant_dynamic-update-slice_fusion.rest_0_), channel_id=1, source_target_pairs={{0,32},{1,33},{2,34},{3,35},{4,36},{5,37},{6,38},{7,39},{8,40},{9,... | collective-permute-start | bytes 1572872 | tf_op jit(solution)/shard_map/ppermute | solution.py:37
  57.1 3.3 %collective-permute-start.8 = (bf16[16,128,128]{2,1,0:T(8,128)(2,1)S(1)}, bf16[16,128,128]{2,1,0:T(8,128)(2,1)S(1)}, u32[]{:S(2)}, u32[]{:S(2)}) collective-permute-start(bf16[16,128,128]{2,1,0:T(8,128)(2,1)S(1)} %constant_dynamic-update-slice_fusion.rest_0_), channel_id=1, source_target_pairs={{0,96},{1,97},{2,98},{3,99},{4,100},{5,101},{6,102},{7,103},{8,104... | collective-permute-start | bytes 1572872 | tf_op jit(solution)/shard_map/ppermute | solution.py:37
  60.4 2.9 %collective-permute-start.9 = (bf16[16,128,128]{2,1,0:T(8,128)(2,1)S(1)}, bf16[16,128,128]{2,1,0:T(8,128)(2,1)S(1)}, u32[]{:S(2)}, u32[]{:S(2)}) collective-permute-start(bf16[16,128,128]{2,1,0:T(8,128)(2,1)S(1)} %constant_dynamic-update-slice_fusion.rest_0_), channel_id=1, source_target_pairs={{0,64},{1,65},{2,66},{3,67},{4,68},{5,69},{6,70},{7,71},{8,72},{9,... | collective-permute-start | bytes 1572872 | tf_op jit(solution)/shard_map/ppermute | solution.py:37
  63.3 0.5 fusion.2.table
  63.9 4.9 %prep.1 = (s32[1600]{0:T(1024)S(1)}, s32[8]{0:T(128)S(1)}, bf16[192,128,128]{2,1,0:T(8,128)(2,1)S(1)}) custom-call(s32[160]{0:T(256)} %own_k.1, s32[160]{0:T(256)} %own_out.1, s32[160]{0:T(256)} %own_live.1, s32[32]{0:T(128)} %help_k.1, s32[32]{0:T(128)} %help_out.1, s32[32]{0:T(128)} %help_live.1, s32[128]{0:T(128)} %fusion.2.table, ...), custom_call_target="tpu_custom_call" | custom-call | bytes 8388608 | tf_op jit(solution)/shard_map/prep/pallas_call | solution.py:134
  68.8 0.0 collective-permute-done.7.rest_1_
  68.8 2.8 %tasks04.1.acc_in = f32[4,128,128]{2,1,0:T(8,128)S(1)} custom-call(s32[1600]{0:T(1024)S(1)} %get-tuple-element.10.lists, s32[8]{0:T(128)S(1)} %get-tuple-element.11.counts, bf16[192,128,128]{2,1,0:T(8,128)(2,1)S(1)} %get-tuple-element.12.tiles, f32[4,128,128]{2,1,0:T(8,128)S(1)} %broadcast_in_dim.3.acc_in, ...), custom_call_target="tpu_custom_call" | custom-call | flops 2013265920 | bytes 8388608 | tf_op jit(solution)/shard_map/tasks04/pallas_call | solution.py:112
  71.6 0.0 collective-permute-done.6.rest_0_
  71.6 2.2 %collective-permute-start.10 = (bf16[16,128,128]{2,1,0:T(8,128)(2,1)S(1)}, bf16[16,128,128]{2,1,0:T(8,128)(2,1)S(1)}, u32[]{:S(2)}, u32[]{:S(2)}) collective-permute-start(bf16[16,128,128]{2,1,0:T(8,128)(2,1)S(1)} %collective-permute-done.6.rest_0_), channel_id=1, source_target_pairs={{0,1},{1,0},{2,3},{3,2},{4,5},{5,4},{6,7},{7,6},{8,9},{9,8},{10,11... | collective-permute-start | bytes 1572872 | tf_op jit(solution)/shard_map/ppermute | solution.py:37
  73.8 0.0 collective-permute-done.8.rest_1_
  73.8 13.9 %collective-permute-start.11 = (bf16[16,128,128]{2,1,0:T(8,128)(2,1)S(1)}, bf16[16,128,128]{2,1,0:T(8,128)(2,1)S(1)}, u32[]{:S(2)}, u32[]{:S(2)}) collective-permute-start(bf16[16,128,128]{2,1,0:T(8,128)(2,1)S(1)} %collective-permute-done.8.rest_1_), channel_id=1, source_target_pairs={{0,1},{1,0},{2,3},{3,2},{4,5},{5,4},{6,7},{7,6},{8,9},{9,8},{10,11... | collective-permute-start | bytes 1572872 | tf_op jit(solution)/shard_map/ppermute | solution.py:37
  87.7 0.0 collective-permute-done.9.rest_2_
  87.7 1.9 %collective-permute-start.12 = (bf16[16,128,128]{2,1,0:T(8,128)(2,1)S(1)}, bf16[16,128,128]{2,1,0:T(8,128)(2,1)S(1)}, u32[]{:S(2)}, u32[]{:S(2)}) collective-permute-start(bf16[16,128,128]{2,1,0:T(8,128)(2,1)S(1)} %collective-permute-done.9.rest_2_), channel_id=1, source_target_pairs={{0,1},{1,0},{2,3},{3,2},{4,5},{5,4},{6,7},{7,6},{8,9},{9,8},{10,11... | collective-permute-start | bytes 1572872 | tf_op jit(solution)/shard_map/ppermute | solution.py:37
  89.6 4.2 %tasks132.1.acc_in = f32[4,128,128]{2,1,0:T(8,128)S(1)} custom-call(s32[1600]{0:T(1024)S(1)} %get-tuple-element.10.lists, s32[8]{0:T(128)S(1)} %get-tuple-element.11.counts, bf16[192,128,128]{2,1,0:T(8,128)(2,1)S(1)} %get-tuple-element.12.tiles, f32[4,128,128]{2,1,0:T(8,128)S(1)} %tasks04.1.acc_in, bf16[16,128,128]{2,1,0:T(8,128)(2,1)S(1)} %collective-permute-done.6.rest_0_, ...), custom_call_target="tpu_custom_call" | custom-call | flops 3019898880 | bytes 8388608 | tf_op jit(solution)/shard_map/tasks132/pallas_call | solution.py:112
  93.8 0.0 collective-permute-done.10.rest_0_
  93.8 0.0 collective-permute-done.11.rest_1_
  93.8 0.0 collective-permute-done.12.rest_2_
  93.8 4.8 %tasks576.1 = bf16[128,512]{1,0:T(8,128)(2,1)} custom-call(s32[1600]{0:T(1024)S(1)} %get-tuple-element.10.lists, s32[8]{0:T(128)S(1)} %get-tuple-element.11.counts, bf16[192,128,128]{2,1,0:T(8,128)(2,1)S(1)} %get-tuple-element.12.tiles, f32[4,128,128]{2,1,0:T(8,128)S(1)} %tasks132.1.acc_in, bf16[16,128,128]{2,1,0:T(8,128)(2,1)S(1)} %collective-permute-done.10.rest_0_, ...), custom_call_target="tpu_custom_call" | custom-call | flops 3019898880 | bytes 8388608 | tf_op jit(solution)/shard_map/tasks576/pallas_call | solution.py:112
  (8 shorter events, 0.1 us)
Async XLA Ops:
  1.4 29.5 %collective-permute-start = (bf16[128,128]{1,0:T(8,128)(2,1)S(1)}, bf16[128,128]{1,0:T(8,128)(2,1)S(1)}, u32[]{:S(2)}, u32[]{:S(2)}) collective-permute-start(bf16[128,128]{1,0:T(8,128)(2,1)S(1)} %get-tuple-element.16), channel_id=1, source_target_pairs={{0,8},{1,9},{2,10},{3,11},{4,12},{5,13},{6,14},{7,15},{8,16},{9,17... | collective-permute-start | bytes 98312 | tf_op jit(solution)/shard_map/ppermute | solution.py:37
  10.3 20.7 %collective-permute-start.1 = (bf16[128,128]{1,0:T(8,128)(2,1)S(1)}, bf16[128,128]{1,0:T(8,128)(2,1)S(1)}, u32[]{:S(2)}, u32[]{:S(2)}) collective-permute-start(bf16[128,128]{1,0:T(8,128)(2,1)S(1)} %get-tuple-element.16), channel_id=1, source_target_pairs={{0,16},{1,17},{2,18},{3,19},{4,20},{5,21},{6,22},{7,23},{8,24},{9,... | collective-permute-start | bytes 98312 | tf_op jit(solution)/shard_map/ppermute | solution.py:37
  25.7 8.6 %collective-permute-start.2 = (bf16[128,128]{1,0:T(8,128)(2,1)S(1)}, bf16[128,128]{1,0:T(8,128)(2,1)S(1)}, u32[]{:S(2)}, u32[]{:S(2)}) collective-permute-start(bf16[128,128]{1,0:T(8,128)(2,1)S(1)} %get-tuple-element.16), channel_id=1, source_target_pairs={{0,24},{1,25},{2,26},{3,27},{4,28},{5,29},{6,30},{7,31},{8,0},{9,1... | collective-permute-start | bytes 98312 | tf_op jit(solution)/shard_map/ppermute | solution.py:37
  34.3 11.6 %collective-permute-start.3 = (bf16[4,128,128]{2,1,0:T(8,128)(2,1)S(1)}, bf16[4,128,128]{2,1,0:T(8,128)(2,1)S(1)}, u32[]{:S(2)}, u32[]{:S(2)}) collective-permute-start(bf16[4,128,128]{2,1,0:T(8,128)(2,1)S(1)} %pad_maximum_fusion), channel_id=1, source_target_pairs={{0,2},{1,3},{2,4},{3,5},{4,6},{5,7},{6,0},{7,1},{8,10},{9,11},{10,... | collective-permute-start | bytes 393224 | tf_op jit(solution)/shard_map/ppermute | solution.py:37
  37.9 13.4 %collective-permute-start.4 = (bf16[4,128,128]{2,1,0:T(8,128)(2,1)S(1)}, bf16[4,128,128]{2,1,0:T(8,128)(2,1)S(1)}, u32[]{:S(2)}, u32[]{:S(2)}) collective-permute-start(bf16[4,128,128]{2,1,0:T(8,128)(2,1)S(1)} %pad_maximum_fusion), channel_id=1, source_target_pairs={{0,4},{1,5},{2,6},{3,7},{4,0},{5,1},{6,2},{7,3},{8,12},{9,13},{10,... | collective-permute-start | bytes 393224 | tf_op jit(solution)/shard_map/ppermute | solution.py:37
  43.2 8.1 %collective-permute-start.5 = (bf16[4,128,128]{2,1,0:T(8,128)(2,1)S(1)}, bf16[4,128,128]{2,1,0:T(8,128)(2,1)S(1)}, u32[]{:S(2)}, u32[]{:S(2)}) collective-permute-start(bf16[4,128,128]{2,1,0:T(8,128)(2,1)S(1)} %pad_maximum_fusion), channel_id=1, source_target_pairs={{0,6},{1,7},{2,0},{3,1},{4,2},{5,3},{6,4},{7,5},{8,14},{9,15},{10,... | collective-permute-start | bytes 393224 | tf_op jit(solution)/shard_map/ppermute | solution.py:37
  51.3 17.4 %collective-permute-start.7 = (bf16[16,128,128]{2,1,0:T(8,128)(2,1)S(1)}, bf16[16,128,128]{2,1,0:T(8,128)(2,1)S(1)}, u32[]{:S(2)}, u32[]{:S(2)}) collective-permute-start(bf16[16,128,128]{2,1,0:T(8,128)(2,1)S(1)} %constant_dynamic-update-slice_fusion.rest_0_), channel_id=1, source_target_pairs={{0,1},{1,0},{2,3},{3,2},{4,5},{5,4},{6,7},{7,6},{8,9},{9,8},{10,11... | collective-permute-start | bytes 1572872 | tf_op jit(solution)/shard_map/ppermute | solution.py:37
  55.1 16.5 %collective-permute-start.6 = (bf16[16,128,128]{2,1,0:T(8,128)(2,1)S(1)}, bf16[16,128,128]{2,1,0:T(8,128)(2,1)S(1)}, u32[]{:S(2)}, u32[]{:S(2)}) collective-permute-start(bf16[16,128,128]{2,1,0:T(8,128)(2,1)S(1)} %constant_dynamic-update-slice_fusion.rest_0_), channel_id=1, source_target_pairs={{0,32},{1,33},{2,34},{3,35},{4,36},{5,37},{6,38},{7,39},{8,40},{9,... | collective-permute-start | bytes 1572872 | tf_op jit(solution)/shard_map/ppermute | solution.py:37
  57.1 16.7 %collective-permute-start.8 = (bf16[16,128,128]{2,1,0:T(8,128)(2,1)S(1)}, bf16[16,128,128]{2,1,0:T(8,128)(2,1)S(1)}, u32[]{:S(2)}, u32[]{:S(2)}) collective-permute-start(bf16[16,128,128]{2,1,0:T(8,128)(2,1)S(1)} %constant_dynamic-update-slice_fusion.rest_0_), channel_id=1, source_target_pairs={{0,96},{1,97},{2,98},{3,99},{4,100},{5,101},{6,102},{7,103},{8,104... | collective-permute-start | bytes 1572872 | tf_op jit(solution)/shard_map/ppermute | solution.py:37
  60.4 27.3 %collective-permute-start.9 = (bf16[16,128,128]{2,1,0:T(8,128)(2,1)S(1)}, bf16[16,128,128]{2,1,0:T(8,128)(2,1)S(1)}, u32[]{:S(2)}, u32[]{:S(2)}) collective-permute-start(bf16[16,128,128]{2,1,0:T(8,128)(2,1)S(1)} %constant_dynamic-update-slice_fusion.rest_0_), channel_id=1, source_target_pairs={{0,64},{1,65},{2,66},{3,67},{4,68},{5,69},{6,70},{7,71},{8,72},{9,... | collective-permute-start | bytes 1572872 | tf_op jit(solution)/shard_map/ppermute | solution.py:37
  71.6 22.2 %collective-permute-start.10 = (bf16[16,128,128]{2,1,0:T(8,128)(2,1)S(1)}, bf16[16,128,128]{2,1,0:T(8,128)(2,1)S(1)}, u32[]{:S(2)}, u32[]{:S(2)}) collective-permute-start(bf16[16,128,128]{2,1,0:T(8,128)(2,1)S(1)} %collective-permute-done.6.rest_0_), channel_id=1, source_target_pairs={{0,1},{1,0},{2,3},{3,2},{4,5},{5,4},{6,7},{7,6},{8,9},{9,8},{10,11... | collective-permute-start | bytes 1572872 | tf_op jit(solution)/shard_map/ppermute | solution.py:37
  73.8 20.0 %collective-permute-start.11 = (bf16[16,128,128]{2,1,0:T(8,128)(2,1)S(1)}, bf16[16,128,128]{2,1,0:T(8,128)(2,1)S(1)}, u32[]{:S(2)}, u32[]{:S(2)}) collective-permute-start(bf16[16,128,128]{2,1,0:T(8,128)(2,1)S(1)} %collective-permute-done.8.rest_1_), channel_id=1, source_target_pairs={{0,1},{1,0},{2,3},{3,2},{4,5},{5,4},{6,7},{7,6},{8,9},{9,8},{10,11... | collective-permute-start | bytes 1572872 | tf_op jit(solution)/shard_map/ppermute | solution.py:37
  87.7 6.1 %collective-permute-start.12 = (bf16[16,128,128]{2,1,0:T(8,128)(2,1)S(1)}, bf16[16,128,128]{2,1,0:T(8,128)(2,1)S(1)}, u32[]{:S(2)}, u32[]{:S(2)}) collective-permute-start(bf16[16,128,128]{2,1,0:T(8,128)(2,1)S(1)} %collective-permute-done.9.rest_2_), channel_id=1, source_target_pairs={{0,1},{1,0},{2,3},{3,2},{4,5},{5,4},{6,7},{7,6},{8,9},{9,8},{10,11... | collective-permute-start | bytes 1572872 | tf_op jit(solution)/shard_map/ppermute | solution.py:37

commit v3 on v2

--- a/solution.py
+++ b/solution.py
@@ -11,30 +11,19 @@
 TILE = 128
 OB = 4
 NY, NZH, NZL, NC = 4, 4, 4, 2
+COLS = NY * NZH * NZL * NC
 LINE = NZH * NZL
 PIECES = NC * NY
 WIDE = 4
-
-
-def split_col(i):
-    return i // (LINE * NC), (i // (NZL * NC)) % NZH, (i // NC) % NZL, i % NC
-
-
-def join_col(y, zh, zl, c):
-    return ((y * NZH + zh) * NZL + zl) * NC + c
-
-
-def shift(dy=0, dzh=0, dzl=0, dc=0):
-    pairs = []
-    for i in range(NY * LINE * NC):
-        y, zh, zl, c = split_col(i)
-        j = join_col((y + dy) % NY, (zh + dzh) % NZH, (zl + dzl) % NZL, (c + dc) % NC)
-        pairs.append((i, j))
-    return pairs
-
-
-def move(x, **d):
-    return lax.ppermute(x, "col", shift(**d))
+PACK = 10
+REST = LINE - PACK
+META = 16
+ABSENT, LATER = 99, 50
+
+
+def move(x, y=0, zh=0, zl=0, c=0):
+    mask = ((y * NZH + zh) * NZL + zl) * NC + c
+    return lax.ppermute(x, "col", [(i, i ^ mask) for i in range(COLS)])
 
 
 def prep_kernel(own_k, own_out, own_live, help_k, help_out, help_live, table, own_tiles, help_tiles,
@@ -75,58 +64,141 @@
     fetch_help.wait()
 
 
-def task_kernel(ids, last, lists, counts, tiles, acc_in, *rest):
-    pieces, out, acc = rest[:len(ids)], rest[-2], rest[-1]
+def pack_kernel(*refs):
+    groups, (head, tail) = refs[:NZL], refs[NZL:NZL + 2]
+    gone_v, gone_s, sem = refs[NZL + 2:]
+    lane = lax.broadcasted_iota(jnp.int32, (8, TILE), 1)
+    gone = jnp.zeros((8, TILE), jnp.int32)
+    for slot in range(LINE):
+        row = groups[slot // NZH][slot % NZH, pl.ds(0, 16), :].astype(jnp.float32)[:1]
+        gone = jnp.where((lane == slot) & (row == jnp.inf), 1, gone)
+    gone_v[...] = gone
+    copy = pltpu.make_async_copy(gone_v, gone_s, sem.at[0])
+    copy.start()
+    copy.wait()
+    lane = lax.broadcasted_iota(jnp.int32, (META, TILE), 1)
+    places = jnp.full((META, TILE), ABSENT, jnp.int32)
+    n = jnp.int32(0)
+    for slot in range(LINE):
+        here = gone_s[0, slot] == 0
+        tile = groups[slot // NZH].at[slot % NZH]
+
+        @pl.when(here & (n < PACK))
+        def _():
+            head[pl.ds(pl.multiple_of(n * TILE, TILE), TILE), :] = tile[...]
+
+        @pl.when(here & (n >= PACK))
+        def _():
+            tail[pl.ds(pl.multiple_of((n - PACK) * TILE, TILE), TILE), :] = tile[...]
+
+        places = jnp.where(lane == slot, jnp.where(here, n, ABSENT), places)
+        n = n + jnp.where(here, 1, 0)
+    late = (places >= PACK) & (places < ABSENT)
+    first = jnp.where(late, LATER, places)
+    first = jnp.where(lane == LINE, jnp.where(n > PACK, 1, 0), first)
+    second = jnp.where(late, places - PACK, ABSENT)
+    second = jnp.where(lane == LINE, 0, second)
+    head[pl.ds(PACK * TILE, META), :] = first.astype(jnp.float32).astype(head.dtype)
+    tail[pl.ds(REST * TILE, META), :] = second.astype(jnp.float32).astype(tail.dtype)
+
+
+def pack(groups):
+    vmem = pl.BlockSpec(memory_space=pltpu.VMEM)
+    return pl.pallas_call(
+        pack_kernel,
+        out_shape=(
+            jax.ShapeDtypeStruct((PACK * TILE + META, TILE), jnp.bfloat16),
+            jax.ShapeDtypeStruct((REST * TILE + META, TILE), jnp.bfloat16),
+        ),
+        in_specs=[vmem] * len(groups),
+        out_specs=(vmem, vmem),
+        scratch_shapes=[
+            pltpu.VMEM((8, TILE), jnp.int32),
+            pltpu.SMEM((8, TILE), jnp.int32),
+            pltpu.SemaphoreType.DMA((1,)),
+        ],
+        name="pack",
+        compiler_params=pltpu.CompilerParams(vmem_limit_bytes=24 << 20),
+    )(*groups)
+
+
+def task_kernel(ids, places, last, lists, counts, tiles, acc_in, over_in, *rest):
+    pieces, rest = rest[:len(ids)], rest[len(ids):]
+    outs, (acc, meta_v, meta_s, picked, sem) = rest[:-5], rest[-5:]
     cap = lists.shape[0] // PIECES
+    for j, piece in enumerate(pieces):
+        meta = piece[pl.ds(places * TILE, META), :].astype(jnp.float32).astype(jnp.int32)
+        meta_v[pl.ds(j, 1), :] = meta[:1]
+    copy = pltpu.make_async_copy(meta_v, meta_s, sem.at[0])
+    copy.start()
     acc[pl.ds(0, OB)] = acc_in[...]
-    for p, amps in zip(ids, pieces):
-
-        def step(g, carry, p=p, amps=amps):
-            outs, prods = [], []
+    copy.wait()
+    over = over_in[0]
+    for j, (p, amps) in enumerate(zip(ids, pieces)):
+        over = over + meta_s[j, LINE]
+
+        def pick(e, n, p=p, j=j):
+            entry = lists[p * cap + e]
+            place = meta_s[j, (entry // 8) % LINE]
+            picked[n] = (entry // (8 * LINE)) * (8 * LINE) + place * 8 + entry % 8
+            return n + jnp.where(place < places, 1, 0)
+
+        n = lax.fori_loop(0, counts[p], pick, 0)
+        for w in range(WIDE):
+            picked[n + w] = OB
+
+        def step(g, carry, amps=amps):
+            outputs, prods = [], []
             for w in range(WIDE):
-                entry = lists[p * cap + g * WIDE + w]
-                outs.append(entry % 8)
-                a = amps[(entry // 8) % LINE]
+                entry = picked[g * WIDE + w]
+                outputs.append(entry % 8)
+                place = (entry // 8) % LINE
+                a = amps[pl.ds(pl.multiple_of(place * TILE, TILE), TILE), :]
                 b = tiles[entry // (8 * LINE)]
                 prods.append(jnp.dot(a, b, preferred_element_type=jnp.float32))
             for w in range(WIDE):
-                acc[outs[w]] += prods[w]
+                acc[outputs[w]] += prods[w]
             return carry
 
-        lax.fori_loop(0, (counts[p] + WIDE - 1) // WIDE, step, 0)
+        lax.fori_loop(0, (n + WIDE - 1) // WIDE, step, 0)
     if last:
         for o in range(OB):
-            out[:, o * TILE:(o + 1) * TILE] = acc[o].astype(out.dtype)
-    else:
-        out[...] = acc[pl.ds(0, OB)]
-
-
-def run_tasks(ids, pieces, acc_in, last, lists, counts, tiles):
-    if last:
-        out_shape = jax.ShapeDtypeStruct((TILE, OB * TILE), jnp.bfloat16)
-    else:
-        out_shape = jax.ShapeDtypeStruct((OB, TILE, TILE), jnp.float32)
+            outs[2][:, o * TILE:(o + 1) * TILE] = acc[o].astype(outs[2].dtype)
+    outs[0][...] = acc[pl.ds(0, OB)]
+    outs[1][0] = over
+
+
+def run_tasks(ids, pieces, acc_in, last, lists, counts, tiles, places=PACK):
     smem = pl.BlockSpec(memory_space=pltpu.SMEM)
     vmem = pl.BlockSpec(memory_space=pltpu.VMEM)
+    out_shape = [jax.ShapeDtypeStruct((OB, TILE, TILE), jnp.float32), jax.ShapeDtypeStruct((1,), jnp.int32)]
+    out_specs = [vmem, smem]
+    if last:
+        out_shape.append(jax.ShapeDtypeStruct((TILE, OB * TILE), jnp.bfloat16))
+        out_specs.append(vmem)
     n = tiles.shape[0] * len(ids) // PIECES
     return pl.pallas_call(
-        functools.partial(task_kernel, ids, last),
+        functools.partial(task_kernel, ids, places, last),
         out_shape=out_shape,
-        in_specs=[smem, smem, vmem, vmem] + [vmem] * len(pieces),
-        out_specs=vmem,
-        scratch_shapes=[pltpu.VMEM((OB + 1, TILE, TILE), jnp.float32)],
+        in_specs=[smem, smem, vmem, vmem, smem] + [vmem] * len(pieces),
+        out_specs=out_specs,
+        scratch_shapes=[
+            pltpu.VMEM((OB + 1, TILE, TILE), jnp.float32),
+            pltpu.VMEM((8, TILE), jnp.int32),
+            pltpu.SMEM((8, TILE), jnp.int32),
+            pltpu.SMEM((tiles.shape[0] + 8,), jnp.int32),
+            pltpu.SemaphoreType.DMA((1,)),
+        ],
         compiler_params=pltpu.CompilerParams(vmem_limit_bytes=24 << 20),
         cost_estimate=pl.CostEstimate(flops=n * 20 * TILE ** 3, bytes_accessed=8 << 20, transcendentals=0),
         name="tasks" + "".join(str(p) for p in ids),
-    )(lists, counts, tiles, acc_in, *pieces)
+    )(lists, counts, tiles, *acc_in, *pieces)
 
 
 def prepare(own_tiles, own_k, own_out, own_live, help_tiles, help_k, help_out, help_live):
-    me = lax.axis_index("col")
-    y, zh, zl, c = split_col(me)
-    ky, kzh, kzl, kc = split_col(jnp.arange(NY * LINE * NC, dtype=jnp.int32))
-    dy, dzh, dzl, dc = (y - ky) % NY, (zh - kzh) % NZH, (zl - kzl) % NZL, (c - kc) % NC
-    table = ((dc * NY + dy) * NZL + dzl) * NZH + dzh
+    apart = lax.axis_index("col") ^ jnp.arange(COLS, dtype=jnp.int32)
+    c, zl, zh, y = apart % NC, apart // NC % NZL, apart // (NC * NZL) % NZH, apart // (NC * LINE)
+    table = ((c * NY + y) * NZL + zl) * NZH + zh
     n = own_k.shape[0] + help_k.shape[0]
     smem = pl.BlockSpec(memory_space=pltpu.SMEM)
     hbm = pl.BlockSpec(memory_space=pltpu.HBM)
@@ -160,21 +232,27 @@
     help_out,
     help_live,
 ):
-    kept = amplitudes * amp_kept.astype(jnp.bfloat16)
-    far = [kept] + [move(kept, dzh=k) for k in (1, 2, 3)]
+    kept = jnp.where(amp_kept != 0, amplitudes * amp_kept.astype(jnp.bfloat16), jnp.inf).astype(jnp.bfloat16)
+    first = jnp.stack([kept] + [move(kept, zh=k) for k in (1, 2, 3)])
+    head, tail = pack([first] + [move(first, zl=k) for k in (1, 2, 3)])
     lists, counts, tiles = prepare(
         own_tiles, own_k, own_out, own_live, help_tiles, help_k, help_out, help_live)
-    first = jnp.stack(far)
-    line = jnp.concatenate([first] + [move(first, dzl=k) for k in (1, 2, 3)])
-    ys = {k: move(line, dy=k) for k in (1, 3, 2)}
-    line_c = move(line, dc=1)
     tasks = functools.partial(run_tasks, lists=lists, counts=counts, tiles=tiles)
-    acc = jnp.zeros((OB, TILE, TILE), jnp.float32)
-    acc = tasks((0, NY), [line, line_c], acc, False)
+    ys = {k: move(head, y=k) for k in (1, 3, 2)}
+    head_c = move(head, c=1)
+    acc = (jnp.zeros((OB, TILE, TILE), jnp.float32), jnp.zeros((1,), jnp.int32))
+    acc = tasks((0, NY), [head, head_c], acc, False)
     ys[1], acc = lax.optimization_barrier((ys[1], acc))
-    ys_c = {k: move(ys[k], dc=1) for k in (1, 3, 2)}
+    ys_c = {k: move(ys[k], c=1) for k in (1, 3, 2)}
     acc = tasks((1, 3, 2), [ys[1], ys[3], ys[2]], acc, False)
-    return tasks((NY + 1, NY + 3, NY + 2), [ys_c[1], ys_c[3], ys_c[2]], acc, True)
+    total, over, out = tasks((NY + 1, NY + 3, NY + 2), [ys_c[1], ys_c[3], ys_c[2]], acc, True)
+
+    def second_round(tail, total, over, out):
+        line = [tail] + [move(tail, y=k) for k in (1, 2, 3)]
+        pieces = line + [move(v, c=1) for v in line]
+        return tasks(tuple(range(PIECES)), pieces, (total, over), True, places=REST)[2]
+
+    return lax.cond(over[0] > 0, second_round, lambda tail, total, over, out: out, tail, total, over, out)
 
 
 def solution(mesh):

time: 99.2 us -> 107 us (1.079)
  the two profiles are of different devices: /device:TPU:25 before, /device:TPU:1 now
where the time goes in v3:
time: 107 us; the launch traced here: 106 us
  starting transfers between devices  60.7 us (57%)
  waiting for transfers between devices  23.1 us (22%)
  Pallas kernels  18.5 us (17%)
  other arithmetic  2.08 us (2%)
  between operations  1.51 us (1%)
    ppermute x13, starting transfers between devices, move(): return lax.ppermute(x, 'col', [(i, i ^ mask) for i in range(COLS)])  60.7 us
    ppermute x13, waiting for transfers between devices, move(): return lax.ppermute(x, 'col', [(i, i ^ mask) for i in range(COLS)])  23.1 us
    pallas_call x3, Pallas kernels, run_tasks(): pl.pallas_call(functools.partial(task_kernel, ids, places, last), out_sha...  12.7 us
    pallas_call x1, Pallas kernels, prepare(): pl.pallas_call(prep_kernel, out_shape=(jax.ShapeDtypeStruct((PIECES * (n...  4.9 us
  transfers between devices with their start and end apart: 13, of which 4 were waited for; matrix products, arithmetic and copies ran while one was open for 1% of the time, Pallas kernels for 12%

profile of v3, /device:TPU:1, one launch (start us, length us, event | category | flops | bytes accessed | tf_op | source)
XLA Modules:
  0.0 105.9 jit_solution(282519661464465152)
XLA Ops:
  0.7 0.8 multiply_select_fusion
  1.4 9.6 %collective-permute-start.7 = (bf16[128,128]{1,0:T(8,128)(2,1)S(1)}, bf16[128,128]{1,0:T(8,128)(2,1)S(1)}, u32[]{:S(2)}, u32[]{:S(2)}) collective-permute-start(bf16[128,128]{1,0:T(8,128)(2,1)S(1)} %multiply_select_fusion), channel_id=1, source_target_pairs={{0,8},{1,9},{2,10},{3,11},{4,12},{5,13},{6,14},{7,15},{8,0},{9,1},... | collective-permute-start | bytes 98312 | tf_op jit(solution)/shard_map/ppermute | solution.py:26
  11.1 15.4 %collective-permute-start.8 = (bf16[128,128]{1,0:T(8,128)(2,1)S(1)}, bf16[128,128]{1,0:T(8,128)(2,1)S(1)}, u32[]{:S(2)}, u32[]{:S(2)}) collective-permute-start(bf16[128,128]{1,0:T(8,128)(2,1)S(1)} %multiply_select_fusion), channel_id=1, source_target_pairs={{0,16},{1,17},{2,18},{3,19},{4,20},{5,21},{6,22},{7,23},{8,24},{9,... | collective-permute-start | bytes 98312 | tf_op jit(solution)/shard_map/ppermute | solution.py:26
  26.5 1.9 %collective-permute-start.9 = (bf16[128,128]{1,0:T(8,128)(2,1)S(1)}, bf16[128,128]{1,0:T(8,128)(2,1)S(1)}, u32[]{:S(2)}, u32[]{:S(2)}) collective-permute-start(bf16[128,128]{1,0:T(8,128)(2,1)S(1)} %multiply_select_fusion), channel_id=1, source_target_pairs={{0,24},{1,25},{2,26},{3,27},{4,28},{5,29},{6,30},{7,31},{8,16},{9,... | collective-permute-start | bytes 98312 | tf_op jit(solution)/shard_map/ppermute | solution.py:26
  28.4 0.8 fusion.7
  29.2 0.0 collective-permute-done.7
  29.2 0.0 collective-permute-done.8
  29.2 15.6 %collective-permute-done.9 = bf16[128,128]{1,0:T(8,128)(2,1)S(1)} collective-permute-done((bf16[128,128]{1,0:T(8,128)(2,1)S(1)}, bf16[128,128]{1,0:T(8,128)(2,1)S(1)}, u32[]{:S(2)}, u32[]{:S(2)}) %collective-permute-start.9) | collective-permute-done | bytes 32800 | tf_op jit(solution)/shard_map/ppermute | solution.py:26
  44.9 3.5 %collective-permute-start.10 = (bf16[4,128,128]{2,1,0:T(8,128)(2,1)S(1)}, bf16[4,128,128]{2,1,0:T(8,128)(2,1)S(1)}, u32[]{:S(2)}, u32[]{:S(2)}) collective-permute-start(bf16[4,128,128]{2,1,0:T(8,128)(2,1)S(1)} %pad_maximum_fusion.refs_0_), channel_id=1, source_target_pairs={{0,2},{1,3},{2,0},{3,1},{4,6},{5,7},{6,4},{7,5},{8,10},{9,11},{10,... | collective-permute-start | bytes 393224 | tf_op jit(solution)/shard_map/ppermute | solution.py:26
  48.4 4.9 %collective-permute-start.11 = (bf16[4,128,128]{2,1,0:T(8,128)(2,1)S(1)}, bf16[4,128,128]{2,1,0:T(8,128)(2,1)S(1)}, u32[]{:S(2)}, u32[]{:S(2)}) collective-permute-start(bf16[4,128,128]{2,1,0:T(8,128)(2,1)S(1)} %pad_maximum_fusion.refs_0_), channel_id=1, source_target_pairs={{0,4},{1,5},{2,6},{3,7},{4,0},{5,1},{6,2},{7,3},{8,12},{9,13},{10,... | collective-permute-start | bytes 393224 | tf_op jit(solution)/shard_map/ppermute | solution.py:26
  53.3 1.9 %collective-permute-start.12 = (bf16[4,128,128]{2,1,0:T(8,128)(2,1)S(1)}, bf16[4,128,128]{2,1,0:T(8,128)(2,1)S(1)}, u32[]{:S(2)}, u32[]{:S(2)}) collective-permute-start(bf16[4,128,128]{2,1,0:T(8,128)(2,1)S(1)} %pad_maximum_fusion.refs_0_), channel_id=1, source_target_pairs={{0,6},{1,7},{2,4},{3,5},{4,2},{5,3},{6,0},{7,1},{8,14},{9,15},{10,... | collective-permute-start | bytes 393224 | tf_op jit(solution)/shard_map/ppermute | solution.py:26
  55.2 0.0 collective-permute-done.10.refs_1_
  55.3 1.5 %collective-permute-done.11.refs_2_ = bf16[4,128,128]{2,1,0:T(8,128)(2,1)S(1)} collective-permute-done((bf16[4,128,128]{2,1,0:T(8,128)(2,1)S(1)}, bf16[4,128,128]{2,1,0:T(8,128)(2,1)S(1)}, u32[]{:S(2)}, u32[]{:S(2)}) %collective-permute-start.11) | collective-permute-done | bytes 131104 | tf_op jit(solution)/shard_map/ppermute | solution.py:26
  56.8 4.1 %collective-permute-done.12.refs_3_ = bf16[4,128,128]{2,1,0:T(8,128)(2,1)S(1)} collective-permute-done((bf16[4,128,128]{2,1,0:T(8,128)(2,1)S(1)}, bf16[4,128,128]{2,1,0:T(8,128)(2,1)S(1)}, u32[]{:S(2)}, u32[]{:S(2)}) %collective-permute-start.12) | collective-permute-done | bytes 131104 | tf_op jit(solution)/shard_map/ppermute | solution.py:26
  60.9 0.8 pack.1
  61.8 6.0 %collective-permute-start.14 = (bf16[1296,128]{1,0:T(8,128)(2,1)S(1)}, bf16[1296,128]{1,0:T(8,128)(2,1)S(1)}, u32[]{:S(2)}, u32[]{:S(2)}) collective-permute-start(bf16[1296,128]{1,0:T(8,128)(2,1)S(1)} %get-tuple-element.46.rest_0_), channel_id=1, source_target_pairs={{0,1},{1,0},{2,3},{3,2},{4,5},{5,4},{6,7},{7,6},{8,9},{9,8},{10,11... | collective-permute-start | bytes 995336 | tf_op jit(solution)/shard_map/ppermute | solution.py:26
  67.8 3.2 %collective-permute-start.13 = (bf16[1296,128]{1,0:T(8,128)(2,1)S(1)}, bf16[1296,128]{1,0:T(8,128)(2,1)S(1)}, u32[]{:S(2)}, u32[]{:S(2)}) collective-permute-start(bf16[1296,128]{1,0:T(8,128)(2,1)S(1)} %get-tuple-element.46.rest_0_), channel_id=1, source_target_pairs={{0,32},{1,33},{2,34},{3,35},{4,36},{5,37},{6,38},{7,39},{8,40},{9,... | collective-permute-start | bytes 995336 | tf_op jit(solution)/shard_map/ppermute | solution.py:26
  71.0 3.8 %collective-permute-start.15 = (bf16[1296,128]{1,0:T(8,128)(2,1)S(1)}, bf16[1296,128]{1,0:T(8,128)(2,1)S(1)}, u32[]{:S(2)}, u32[]{:S(2)}) collective-permute-start(bf16[1296,128]{1,0:T(8,128)(2,1)S(1)} %get-tuple-element.46.rest_0_), channel_id=1, source_target_pairs={{0,96},{1,97},{2,98},{3,99},{4,100},{5,101},{6,102},{7,103},{8,104... | collective-permute-start | bytes 995336 | tf_op jit(solution)/shard_map/ppermute | solution.py:26
  74.8 2.6 %collective-permute-start.16 = (bf16[1296,128]{1,0:T(8,128)(2,1)S(1)}, bf16[1296,128]{1,0:T(8,128)(2,1)S(1)}, u32[]{:S(2)}, u32[]{:S(2)}) collective-permute-start(bf16[1296,128]{1,0:T(8,128)(2,1)S(1)} %get-tuple-element.46.rest_0_), channel_id=1, source_target_pairs={{0,64},{1,65},{2,66},{3,67},{4,68},{5,69},{6,70},{7,71},{8,72},{9,... | collective-permute-start | bytes 995336 | tf_op jit(solution)/shard_map/ppermute | solution.py:26
  77.5 0.5 fusion.1.table
  78.0 4.9 %prep.1 = (s32[1600]{0:T(1024)S(1)}, s32[8]{0:T(128)S(1)}, bf16[192,128,128]{2,1,0:T(8,128)(2,1)S(1)}) custom-call(s32[160]{0:T(256)} %own_k.1, s32[160]{0:T(256)} %own_out.1, s32[160]{0:T(256)} %own_live.1, s32[32]{0:T(128)} %help_k.1, s32[32]{0:T(128)} %help_out.1, s32[32]{0:T(128)} %help_live.1, s32[128]{0:T(128)} %fusion.1.table, ...), custom_call_target="tpu_custom_call" | custom-call | bytes 8388608 | tf_op jit(solution)/shard_map/prep/pallas_call | solution.py:206
  82.9 0.0 collective-permute-done.14.rest_1_
  82.9 2.8 %tasks04.1 = (f32[4,128,128]{2,1,0:T(8,128)S(1)}, s32[1]{0:T(128)}) custom-call(s32[1600]{0:T(1024)S(1)} %get-tuple-element.43.lists, s32[8]{0:T(128)S(1)} %get-tuple-element.44.counts, bf16[192,128,128]{2,1,0:T(8,128)(2,1)S(1)} %get-tuple-element.45.tiles, f32[4,128,128]{2,1,0:T(8,128)S(1)} %broadcast_in_dim.20.acc_in, s32[1]{0:T(128)} %constant.78.clone.1.over_in, ...), custom_call_target="tpu_custom_call" | custom-call | flops 2013265920 | bytes 8388608 | tf_op jit(solution)/shard_map/tasks04/pallas_call | solution.py:180
  85.7 0.0 collective-permute-done.13.rest_0_
  85.7 2.8 %collective-permute-start.17 = (bf16[1296,128]{1,0:T(8,128)(2,1)S(1)}, bf16[1296,128]{1,0:T(8,128)(2,1)S(1)}, u32[]{:S(2)}, u32[]{:S(2)}) collective-permute-start(bf16[1296,128]{1,0:T(8,128)(2,1)S(1)} %collective-permute-done.13.rest_0_), channel_id=1, source_target_pairs={{0,1},{1,0},{2,3},{3,2},{4,5},{5,4},{6,7},{7,6},{8,9},{9,8},{10,11... | collective-permute-start | bytes 995336 | tf_op jit(solution)/shard_map/ppermute | solution.py:26
  88.5 1.8 %collective-permute-done.15.rest_1_ = bf16[1296,128]{1,0:T(8,128)(2,1)S(1)} collective-permute-done((bf16[1296,128]{1,0:T(8,128)(2,1)S(1)}, bf16[1296,128]{1,0:T(8,128)(2,1)S(1)}, u32[]{:S(2)}, u32[]{:S(2)}) %collective-permute-start.15) | collective-permute-done | bytes 331808 | tf_op jit(solution)/shard_map/ppermute | solution.py:26
  90.3 3.0 %collective-permute-start.18 = (bf16[1296,128]{1,0:T(8,128)(2,1)S(1)}, bf16[1296,128]{1,0:T(8,128)(2,1)S(1)}, u32[]{:S(2)}, u32[]{:S(2)}) collective-permute-start(bf16[1296,128]{1,0:T(8,128)(2,1)S(1)} %collective-permute-done.15.rest_1_), channel_id=1, source_target_pairs={{0,1},{1,0},{2,3},{3,2},{4,5},{5,4},{6,7},{7,6},{8,9},{9,8},{10,11... | collective-permute-start | bytes 995336 | tf_op jit(solution)/shard_map/ppermute | solution.py:26
  93.3 0.0 collective-permute-done.16.rest_2_
  93.3 1.9 %collective-permute-start.19 = (bf16[1296,128]{1,0:T(8,128)(2,1)S(1)}, bf16[1296,128]{1,0:T(8,128)(2,1)S(1)}, u32[]{:S(2)}, u32[]{:S(2)}) collective-permute-start(bf16[1296,128]{1,0:T(8,128)(2,1)S(1)} %collective-permute-done.16.rest_2_), channel_id=1, source_target_pairs={{0,1},{1,0},{2,3},{3,2},{4,5},{5,4},{6,7},{7,6},{8,9},{9,8},{10,11... | collective-permute-start | bytes 995336 | tf_op jit(solution)/shard_map/ppermute | solution.py:26
  95.3 4.7 %tasks132.1 = (f32[4,128,128]{2,1,0:T(8,128)S(1)}, s32[1]{0:T(128)}) custom-call(s32[1600]{0:T(1024)S(1)} %get-tuple-element.43.lists, s32[8]{0:T(128)S(1)} %get-tuple-element.44.counts, bf16[192,128,128]{2,1,0:T(8,128)(2,1)S(1)} %get-tuple-element.45.tiles, f32[4,128,128]{2,1,0:T(8,128)S(1)} %get-tuple-element.49.acc_in, s32[1]{0:T(128)} %get-tuple-element.50.over_in, ...), custom_call_target="tpu_custom_call" | custom-call | flops 3019898880 | bytes 8388608 | tf_op jit(solution)/shard_map/tasks132/pallas_call | solution.py:180
  100.0 0.0 collective-permute-done.18.rest_1_
  100.0 5.3 %tasks576.1 = (f32[4,128,128]{2,1,0:T(8,128)S(1)}, s32[1]{0:T(128)}, bf16[128,512]{1,0:T(8,128)(2,1)}) custom-call(s32[1600]{0:T(1024)S(1)} %get-tuple-element.43.lists, s32[8]{0:T(128)S(1)} %get-tuple-element.44.counts, bf16[192,128,128]{2,1,0:T(8,128)(2,1)S(1)} %get-tuple-element.45.tiles, f32[4,128,128]{2,1,0:T(8,128)S(1)} %get-tuple-element.52.acc_in, ...), custom_call_target="tpu_custom_call" | custom-call | flops 3019898880 | bytes 8388608 | tf_op jit(solution)/shard_map/tasks576/pallas_call | solution.py:180
  (5 shorter events, 0.0 us)
Async XLA Ops:
  1.4 27.8 %collective-permute-start.7 = (bf16[128,128]{1,0:T(8,128)(2,1)S(1)}, bf16[128,128]{1,0:T(8,128)(2,1)S(1)}, u32[]{:S(2)}, u32[]{:S(2)}) collective-permute-start(bf16[128,128]{1,0:T(8,128)(2,1)S(1)} %multiply_select_fusion), channel_id=1, source_target_pairs={{0,8},{1,9},{2,10},{3,11},{4,12},{5,13},{6,14},{7,15},{8,0},{9,1},... | collective-permute-start | bytes 98312 | tf_op jit(solution)/shard_map/ppermute | solution.py:26
  11.1 18.2 %collective-permute-start.8 = (bf16[128,128]{1,0:T(8,128)(2,1)S(1)}, bf16[128,128]{1,0:T(8,128)(2,1)S(1)}, u32[]{:S(2)}, u32[]{:S(2)}) collective-permute-start(bf16[128,128]{1,0:T(8,128)(2,1)S(1)} %multiply_select_fusion), channel_id=1, source_target_pairs={{0,16},{1,17},{2,18},{3,19},{4,20},{5,21},{6,22},{7,23},{8,24},{9,... | collective-permute-start | bytes 98312 | tf_op jit(solution)/shard_map/ppermute | solution.py:26
  26.5 18.3 %collective-permute-start.9 = (bf16[128,128]{1,0:T(8,128)(2,1)S(1)}, bf16[128,128]{1,0:T(8,128)(2,1)S(1)}, u32[]{:S(2)}, u32[]{:S(2)}) collective-permute-start(bf16[128,128]{1,0:T(8,128)(2,1)S(1)} %multiply_select_fusion), channel_id=1, source_target_pairs={{0,24},{1,25},{2,26},{3,27},{4,28},{5,29},{6,30},{7,31},{8,16},{9,... | collective-permute-start | bytes 98312 | tf_op jit(solution)/shard_map/ppermute | solution.py:26
  44.9 10.4 %collective-permute-start.10 = (bf16[4,128,128]{2,1,0:T(8,128)(2,1)S(1)}, bf16[4,128,128]{2,1,0:T(8,128)(2,1)S(1)}, u32[]{:S(2)}, u32[]{:S(2)}) collective-permute-start(bf16[4,128,128]{2,1,0:T(8,128)(2,1)S(1)} %pad_maximum_fusion.refs_0_), channel_id=1, source_target_pairs={{0,2},{1,3},{2,0},{3,1},{4,6},{5,7},{6,4},{7,5},{8,10},{9,11},{10,... | collective-permute-start | bytes 393224 | tf_op jit(solution)/shard_map/ppermute | solution.py:26
  48.4 8.4 %collective-permute-start.11 = (bf16[4,128,128]{2,1,0:T(8,128)(2,1)S(1)}, bf16[4,128,128]{2,1,0:T(8,128)(2,1)S(1)}, u32[]{:S(2)}, u32[]{:S(2)}) collective-permute-start(bf16[4,128,128]{2,1,0:T(8,128)(2,1)S(1)} %pad_maximum_fusion.refs_0_), channel_id=1, source_target_pairs={{0,4},{1,5},{2,6},{3,7},{4,0},{5,1},{6,2},{7,3},{8,12},{9,13},{10,... | collective-permute-start | bytes 393224 | tf_op jit(solution)/shard_map/ppermute | solution.py:26
  53.3 7.6 %collective-permute-start.12 = (bf16[4,128,128]{2,1,0:T(8,128)(2,1)S(1)}, bf16[4,128,128]{2,1,0:T(8,128)(2,1)S(1)}, u32[]{:S(2)}, u32[]{:S(2)}) collective-permute-start(bf16[4,128,128]{2,1,0:T(8,128)(2,1)S(1)} %pad_maximum_fusion.refs_0_), channel_id=1, source_target_pairs={{0,6},{1,7},{2,4},{3,5},{4,2},{5,3},{6,0},{7,1},{8,14},{9,15},{10,... | collective-permute-start | bytes 393224 | tf_op jit(solution)/shard_map/ppermute | solution.py:26
  61.8 21.1 %collective-permute-start.14 = (bf16[1296,128]{1,0:T(8,128)(2,1)S(1)}, bf16[1296,128]{1,0:T(8,128)(2,1)S(1)}, u32[]{:S(2)}, u32[]{:S(2)}) collective-permute-start(bf16[1296,128]{1,0:T(8,128)(2,1)S(1)} %get-tuple-element.46.rest_0_), channel_id=1, source_target_pairs={{0,1},{1,0},{2,3},{3,2},{4,5},{5,4},{6,7},{7,6},{8,9},{9,8},{10,11... | collective-permute-start | bytes 995336 | tf_op jit(solution)/shard_map/ppermute | solution.py:26
  67.8 17.9 %collective-permute-start.13 = (bf16[1296,128]{1,0:T(8,128)(2,1)S(1)}, bf16[1296,128]{1,0:T(8,128)(2,1)S(1)}, u32[]{:S(2)}, u32[]{:S(2)}) collective-permute-start(bf16[1296,128]{1,0:T(8,128)(2,1)S(1)} %get-tuple-element.46.rest_0_), channel_id=1, source_target_pairs={{0,32},{1,33},{2,34},{3,35},{4,36},{5,37},{6,38},{7,39},{8,40},{9,... | collective-permute-start | bytes 995336 | tf_op jit(solution)/shard_map/ppermute | solution.py:26
  71.0 19.3 %collective-permute-start.15 = (bf16[1296,128]{1,0:T(8,128)(2,1)S(1)}, bf16[1296,128]{1,0:T(8,128)(2,1)S(1)}, u32[]{:S(2)}, u32[]{:S(2)}) collective-permute-start(bf16[1296,128]{1,0:T(8,128)(2,1)S(1)} %get-tuple-element.46.rest_0_), channel_id=1, source_target_pairs={{0,96},{1,97},{2,98},{3,99},{4,100},{5,101},{6,102},{7,103},{8,104... | collective-permute-start | bytes 995336 | tf_op jit(solution)/shard_map/ppermute | solution.py:26
  74.8 18.5 %collective-permute-start.16 = (bf16[1296,128]{1,0:T(8,128)(2,1)S(1)}, bf16[1296,128]{1,0:T(8,128)(2,1)S(1)}, u32[]{:S(2)}, u32[]{:S(2)}) collective-permute-start(bf16[1296,128]{1,0:T(8,128)(2,1)S(1)} %get-tuple-element.46.rest_0_), channel_id=1, source_target_pairs={{0,64},{1,65},{2,66},{3,67},{4,68},{5,69},{6,70},{7,71},{8,72},{9,... | collective-permute-start | bytes 995336 | tf_op jit(solution)/shard_map/ppermute | solution.py:26
  85.7 14.2 %collective-permute-start.17 = (bf16[1296,128]{1,0:T(8,128)(2,1)S(1)}, bf16[1296,128]{1,0:T(8,128)(2,1)S(1)}, u32[]{:S(2)}, u32[]{:S(2)}) collective-permute-start(bf16[1296,128]{1,0:T(8,128)(2,1)S(1)} %collective-permute-done.13.rest_0_), channel_id=1, source_target_pairs={{0,1},{1,0},{2,3},{3,2},{4,5},{5,4},{6,7},{7,6},{8,9},{9,8},{10,11... | collective-permute-start | bytes 995336 | tf_op jit(solution)/shard_map/ppermute | solution.py:26
  90.3 9.7 %collective-permute-start.18 = (bf16[1296,128]{1,0:T(8,128)(2,1)S(1)}, bf16[1296,128]{1,0:T(8,128)(2,1)S(1)}, u32[]{:S(2)}, u32[]{:S(2)}) collective-permute-start(bf16[1296,128]{1,0:T(8,128)(2,1)S(1)} %collective-permute-done.15.rest_1_), channel_id=1, source_target_pairs={{0,1},{1,0},{2,3},{3,2},{4,5},{5,4},{6,7},{7,6},{8,9},{9,8},{10,11... | collective-permute-start | bytes 995336 | tf_op jit(solution)/shard_map/ppermute | solution.py:26
  93.3 6.7 %collective-permute-start.19 = (bf16[1296,128]{1,0:T(8,128)(2,1)S(1)}, bf16[1296,128]{1,0:T(8,128)(2,1)S(1)}, u32[]{:S(2)}, u32[]{:S(2)}) collective-permute-start(bf16[1296,128]{1,0:T(8,128)(2,1)S(1)} %collective-permute-done.16.rest_2_), channel_id=1, source_target_pairs={{0,1},{1,0},{2,3},{3,2},{4,5},{5,4},{6,7},{7,6},{8,9},{9,8},{10,11... | collective-permute-start | bytes 995336 | tf_op jit(solution)/shard_map/ppermute | solution.py:26

commit v4 on v3

--- a/solution.py
+++ b/solution.py
@@ -15,6 +15,7 @@
 LINE = NZH * NZL
 PIECES = NC * NY
 WIDE = 4
+SCAN = 8
 PACK = 10
 REST = LINE - PACK
 META = 16
@@ -22,8 +23,12 @@
 
 
 def move(x, y=0, zh=0, zl=0, c=0):
-    mask = ((y * NZH + zh) * NZL + zl) * NC + c
-    return lax.ppermute(x, "col", [(i, i ^ mask) for i in range(COLS)])
+    pairs = []
+    for i in range(COLS):
+        far, near = (i // (NC * NZL) + zh) % NZH, (i // NC + zl) % NZL
+        here = ((i // (NC * LINE) ^ y) * NZH + far) * NZL + near
+        pairs.append((i, here * NC + (i % NC ^ c)))
+    return lax.ppermute(x, "col", pairs)
 
 
 def prep_kernel(own_k, own_out, own_live, help_k, help_out, help_live, table, own_tiles, help_tiles,
@@ -47,9 +52,9 @@
     def scan(ks, outs, live, base):
         def step(s, carry):
             code = table[ks[s]]
-            p = code // LINE
+            p = code >> 4
             n = counts[p]
-            lists[p * cap + n] = ((s + base) * LINE + code % LINE) * 8 + outs[s]
+            lists[p * cap + n] = ((s + base) << 7) | ((code & 15) << 3) | outs[s]
             counts[p] = n + live[s]
             return carry
 
@@ -58,7 +63,7 @@
     scan(own_k, own_out, own_live, 0)
     scan(help_k, help_out, help_live, n_own)
     for p in range(PIECES):
-        for w in range(WIDE):
+        for w in range(SCAN):
             lists[p * cap + counts[p] + w] = OB
     fetch_own.wait()
     fetch_help.wait()
@@ -137,13 +142,18 @@
     for j, (p, amps) in enumerate(zip(ids, pieces)):
         over = over + meta_s[j, LINE]
 
-        def pick(e, n, p=p, j=j):
-            entry = lists[p * cap + e]
-            place = meta_s[j, (entry // 8) % LINE]
-            picked[n] = (entry // (8 * LINE)) * (8 * LINE) + place * 8 + entry % 8
-            return n + jnp.where(place < places, 1, 0)
-
-        n = lax.fori_loop(0, counts[p], pick, 0)
+        count = counts[p]
+
+        def pick(g, n, p=p, j=j, count=count):
+            for u in range(SCAN):
+                e = g * SCAN + u
+                entry = lists[p * cap + e]
+                place = meta_s[j, (entry >> 3) & 15]
+                picked[n] = (entry & ~127) | (place << 3) | (entry & 7)
+                n = n + jnp.where((place < places) & (e < count), 1, 0)
+            return n
+
+        n = lax.fori_loop(0, (count + SCAN - 1) >> 3, pick, 0)
         for w in range(WIDE):
             picked[n + w] = OB
 
@@ -151,16 +161,16 @@
             outputs, prods = [], []
             for w in range(WIDE):
                 entry = picked[g * WIDE + w]
-                outputs.append(entry % 8)
-                place = (entry // 8) % LINE
+                outputs.append(entry & 7)
+                place = (entry >> 3) & 15
                 a = amps[pl.ds(pl.multiple_of(place * TILE, TILE), TILE), :]
-                b = tiles[entry // (8 * LINE)]
+                b = tiles[entry >> 7]
                 prods.append(jnp.dot(a, b, preferred_element_type=jnp.float32))
             for w in range(WIDE):
                 acc[outputs[w]] += prods[w]
             return carry
 
-        lax.fori_loop(0, (n + WIDE - 1) // WIDE, step, 0)
+        lax.fori_loop(0, (n + WIDE - 1) >> 2, step, 0)
     if last:
         for o in range(OB):
             outs[2][:, o * TILE:(o + 1) * TILE] = acc[o].astype(outs[2].dtype)
@@ -190,14 +200,15 @@
             pltpu.SemaphoreType.DMA((1,)),
         ],
         compiler_params=pltpu.CompilerParams(vmem_limit_bytes=24 << 20),
-        cost_estimate=pl.CostEstimate(flops=n * 20 * TILE ** 3, bytes_accessed=8 << 20, transcendentals=0),
+        cost_estimate=pl.CostEstimate(flops=n * TILE ** 3, bytes_accessed=n * TILE, transcendentals=0),
         name="tasks" + "".join(str(p) for p in ids),
     )(lists, counts, tiles, *acc_in, *pieces)
 
 
 def prepare(own_tiles, own_k, own_out, own_live, help_tiles, help_k, help_out, help_live):
-    apart = lax.axis_index("col") ^ jnp.arange(COLS, dtype=jnp.int32)
-    c, zl, zh, y = apart % NC, apart // NC % NZL, apart // (NC * NZL) % NZH, apart // (NC * LINE)
+    me, k = lax.axis_index("col"), jnp.arange(COLS, dtype=jnp.int32)
+    c, y = (me ^ k) & 1, (me ^ k) >> 5
+    zl, zh = ((me >> 1) - (k >> 1)) & 3, ((me >> 3) - (k >> 3)) & 3
     table = ((c * NY + y) * NZL + zl) * NZH + zh
     n = own_k.shape[0] + help_k.shape[0]
     smem = pl.BlockSpec(memory_space=pltpu.SMEM)
@@ -237,11 +248,10 @@
     head, tail = pack([first] + [move(first, zl=k) for k in (1, 2, 3)])
     lists, counts, tiles = prepare(
         own_tiles, own_k, own_out, own_live, help_tiles, help_k, help_out, help_live)
+    ys = {k: move(head, y=k) for k in (1, 3, 2)}
     tasks = functools.partial(run_tasks, lists=lists, counts=counts, tiles=tiles)
-    ys = {k: move(head, y=k) for k in (1, 3, 2)}
-    head_c = move(head, c=1)
     acc = (jnp.zeros((OB, TILE, TILE), jnp.float32), jnp.zeros((1,), jnp.int32))
-    acc = tasks((0, NY), [head, head_c], acc, False)
+    acc = tasks((0, NY), [head, move(head, c=1)], acc, False)
     ys[1], acc = lax.optimization_barrier((ys[1], acc))
     ys_c = {k: move(ys[k], c=1) for k in (1, 3, 2)}
     acc = tasks((1, 3, 2), [ys[1], ys[3], ys[2]], acc, False)

time: 107 us -> 93.7 us (0.88)
  waiting for transfers between devices: 23.1 us -> 10.6 us
  Pallas kernels: 18.5 us -> 15.9 us
  starting transfers between devices: 60.7 us -> 63 us
    ppermute x13, waiting for transfers between devices: 23.1 us -> 10.6 us  [move(): return lax.ppermute(x, 'col', pairs)]
    ppermute x13, starting transfers between devices: 60.7 us -> 63 us  [move(): return lax.ppermute(x, 'col', pairs)]
    pallas_call x3, Pallas kernels: 12.7 us -> 11.1 us  [run_tasks(): pl.pallas_call(functools.partial(task_kernel, ids, places, last), out_sha...]
where the time goes in v4:
time: 93.7 us; the launch traced here: 93 us
  starting transfers between devices  63 us (67%)
  Pallas kernels  15.9 us (17%)
  waiting for transfers between devices  10.6 us (11%)
  other arithmetic  2.07 us (2%)
  between operations  1.51 us (2%)
    ppermute x13, starting transfers between devices, move(): return lax.ppermute(x, 'col', pairs)  63 us
    pallas_call x3, Pallas kernels, run_tasks(): pl.pallas_call(functools.partial(task_kernel, ids, places, last), out_sha...  11.1 us
    ppermute x13, waiting for transfers between devices, move(): return lax.ppermute(x, 'col', pairs)  10.6 us
    pallas_call x1, Pallas kernels, prepare(): pl.pallas_call(prep_kernel, out_shape=(jax.ShapeDtypeStruct((PIECES * (n...  3.9 us
  transfers between devices with their start and end apart: 13, of which 4 were waited for; matrix products, arithmetic and copies ran while one was open for 1% of the time, Pallas kernels for 12%

profile of v4, /device:TPU:1, one launch (start us, length us, event | category | flops | bytes accessed | tf_op | source)
XLA Modules:
  0.0 93.0 jit_solution(8012009296288051087)
XLA Ops:
  0.7 0.8 multiply_select_fusion
  1.4 9.6 %collective-permute-start.7 = (bf16[128,128]{1,0:T(8,128)(2,1)S(1)}, bf16[128,128]{1,0:T(8,128)(2,1)S(1)}, u32[]{:S(2)}, u32[]{:S(2)}) collective-permute-start(bf16[128,128]{1,0:T(8,128)(2,1)S(1)} %multiply_select_fusion), channel_id=1, source_target_pairs={{0,8},{1,9},{2,10},{3,11},{4,12},{5,13},{6,14},{7,15},{8,16},{9,17... | collective-permute-start | bytes 98312 | tf_op jit(solution)/shard_map/ppermute | solution.py:31
  11.1 15.4 %collective-permute-start.8 = (bf16[128,128]{1,0:T(8,128)(2,1)S(1)}, bf16[128,128]{1,0:T(8,128)(2,1)S(1)}, u32[]{:S(2)}, u32[]{:S(2)}) collective-permute-start(bf16[128,128]{1,0:T(8,128)(2,1)S(1)} %multiply_select_fusion), channel_id=1, source_target_pairs={{0,16},{1,17},{2,18},{3,19},{4,20},{5,21},{6,22},{7,23},{8,24},{9,... | collective-permute-start | bytes 98312 | tf_op jit(solution)/shard_map/ppermute | solution.py:31
  26.5 5.2 %collective-permute-start.9 = (bf16[128,128]{1,0:T(8,128)(2,1)S(1)}, bf16[128,128]{1,0:T(8,128)(2,1)S(1)}, u32[]{:S(2)}, u32[]{:S(2)}) collective-permute-start(bf16[128,128]{1,0:T(8,128)(2,1)S(1)} %multiply_select_fusion), channel_id=1, source_target_pairs={{0,24},{1,25},{2,26},{3,27},{4,28},{5,29},{6,30},{7,31},{8,0},{9,1... | collective-permute-start | bytes 98312 | tf_op jit(solution)/shard_map/ppermute | solution.py:31
  31.7 0.8 fusion
  32.5 0.0 collective-permute-done.7
  32.5 0.0 collective-permute-done.8
  32.5 2.6 %collective-permute-done.9 = bf16[128,128]{1,0:T(8,128)(2,1)S(1)} collective-permute-done((bf16[128,128]{1,0:T(8,128)(2,1)S(1)}, bf16[128,128]{1,0:T(8,128)(2,1)S(1)}, u32[]{:S(2)}, u32[]{:S(2)}) %collective-permute-start.9) | collective-permute-done | bytes 32800 | tf_op jit(solution)/shard_map/ppermute | solution.py:31
  35.1 3.6 %collective-permute-start.10 = (bf16[4,128,128]{2,1,0:T(8,128)(2,1)S(1)}, bf16[4,128,128]{2,1,0:T(8,128)(2,1)S(1)}, u32[]{:S(2)}, u32[]{:S(2)}) collective-permute-start(bf16[4,128,128]{2,1,0:T(8,128)(2,1)S(1)} %pad_maximum_fusion.refs_0_), channel_id=1, source_target_pairs={{0,2},{1,3},{2,4},{3,5},{4,6},{5,7},{6,0},{7,1},{8,10},{9,11},{10,... | collective-permute-start | bytes 393224 | tf_op jit(solution)/shard_map/ppermute | solution.py:31
  38.7 5.3 %collective-permute-start.11 = (bf16[4,128,128]{2,1,0:T(8,128)(2,1)S(1)}, bf16[4,128,128]{2,1,0:T(8,128)(2,1)S(1)}, u32[]{:S(2)}, u32[]{:S(2)}) collective-permute-start(bf16[4,128,128]{2,1,0:T(8,128)(2,1)S(1)} %pad_maximum_fusion.refs_0_), channel_id=1, source_target_pairs={{0,4},{1,5},{2,6},{3,7},{4,0},{5,1},{6,2},{7,3},{8,12},{9,13},{10,... | collective-permute-start | bytes 393224 | tf_op jit(solution)/shard_map/ppermute | solution.py:31
  44.0 2.6 %collective-permute-start.12 = (bf16[4,128,128]{2,1,0:T(8,128)(2,1)S(1)}, bf16[4,128,128]{2,1,0:T(8,128)(2,1)S(1)}, u32[]{:S(2)}, u32[]{:S(2)}) collective-permute-start(bf16[4,128,128]{2,1,0:T(8,128)(2,1)S(1)} %pad_maximum_fusion.refs_0_), channel_id=1, source_target_pairs={{0,6},{1,7},{2,0},{3,1},{4,2},{5,3},{6,4},{7,5},{8,14},{9,15},{10,... | collective-permute-start | bytes 393224 | tf_op jit(solution)/shard_map/ppermute | solution.py:31
  46.6 0.0 collective-permute-done.10.refs_1_
  46.7 4.2 %collective-permute-done.11.refs_2_ = bf16[4,128,128]{2,1,0:T(8,128)(2,1)S(1)} collective-permute-done((bf16[4,128,128]{2,1,0:T(8,128)(2,1)S(1)}, bf16[4,128,128]{2,1,0:T(8,128)(2,1)S(1)}, u32[]{:S(2)}, u32[]{:S(2)}) %collective-permute-start.11) | collective-permute-done | bytes 131104 | tf_op jit(solution)/shard_map/ppermute | solution.py:31
  50.9 0.6 collective-permute-done.12.refs_3_
  51.5 0.8 pack.1
  52.3 4.6 %collective-permute-start.14 = (bf16[1296,128]{1,0:T(8,128)(2,1)S(1)}, bf16[1296,128]{1,0:T(8,128)(2,1)S(1)}, u32[]{:S(2)}, u32[]{:S(2)}) collective-permute-start(bf16[1296,128]{1,0:T(8,128)(2,1)S(1)} %get-tuple-element.46.rest_0_), channel_id=1, source_target_pairs={{0,1},{1,0},{2,3},{3,2},{4,5},{5,4},{6,7},{7,6},{8,9},{9,8},{10,11... | collective-permute-start | bytes 995336 | tf_op jit(solution)/shard_map/ppermute | solution.py:31
  56.9 3.1 %collective-permute-start.13 = (bf16[1296,128]{1,0:T(8,128)(2,1)S(1)}, bf16[1296,128]{1,0:T(8,128)(2,1)S(1)}, u32[]{:S(2)}, u32[]{:S(2)}) collective-permute-start(bf16[1296,128]{1,0:T(8,128)(2,1)S(1)} %get-tuple-element.46.rest_0_), channel_id=1, source_target_pairs={{0,32},{1,33},{2,34},{3,35},{4,36},{5,37},{6,38},{7,39},{8,40},{9,... | collective-permute-start | bytes 995336 | tf_op jit(solution)/shard_map/ppermute | solution.py:31
  60.0 3.8 %collective-permute-start.15 = (bf16[1296,128]{1,0:T(8,128)(2,1)S(1)}, bf16[1296,128]{1,0:T(8,128)(2,1)S(1)}, u32[]{:S(2)}, u32[]{:S(2)}) collective-permute-start(bf16[1296,128]{1,0:T(8,128)(2,1)S(1)} %get-tuple-element.46.rest_0_), channel_id=1, source_target_pairs={{0,96},{1,97},{2,98},{3,99},{4,100},{5,101},{6,102},{7,103},{8,104... | collective-permute-start | bytes 995336 | tf_op jit(solution)/shard_map/ppermute | solution.py:31
  63.8 2.6 %collective-permute-start.16 = (bf16[1296,128]{1,0:T(8,128)(2,1)S(1)}, bf16[1296,128]{1,0:T(8,128)(2,1)S(1)}, u32[]{:S(2)}, u32[]{:S(2)}) collective-permute-start(bf16[1296,128]{1,0:T(8,128)(2,1)S(1)} %get-tuple-element.46.rest_0_), channel_id=1, source_target_pairs={{0,64},{1,65},{2,66},{3,67},{4,68},{5,69},{6,70},{7,71},{8,72},{9,... | collective-permute-start | bytes 995336 | tf_op jit(solution)/shard_map/ppermute | solution.py:31
  66.4 0.5 and_add_fusion.table
  66.9 3.9 %prep.1 = (s32[1600]{0:T(1024)S(1)}, s32[8]{0:T(128)S(1)}, bf16[192,128,128]{2,1,0:T(8,128)(2,1)S(1)}) custom-call(s32[160]{0:T(256)} %own_k.1, s32[160]{0:T(256)} %own_out.1, s32[160]{0:T(256)} %own_live.1, s32[32]{0:T(128)} %help_k.1, s32[32]{0:T(128)} %help_out.1, s32[32]{0:T(128)} %help_live.1, s32[128]{0:T(128)} %and_add_fusion.table, ...), custom_call_target="tpu_custom_call" | custom-call | bytes 8388608 | tf_op jit(solution)/shard_map/prep/pallas_call | solution.py:217
  70.9 0.0 collective-permute-done.14.rest_1_
  70.9 3.0 %tasks04.1 = (f32[4,128,128]{2,1,0:T(8,128)S(1)}, s32[1]{0:T(128)}) custom-call(s32[1600]{0:T(1024)S(1)} %get-tuple-element.43.lists, s32[8]{0:T(128)S(1)} %get-tuple-element.44.counts, bf16[192,128,128]{2,1,0:T(8,128)(2,1)S(1)} %get-tuple-element.45.tiles, f32[4,128,128]{2,1,0:T(8,128)S(1)} %broadcast_in_dim.20.acc_in, s32[1]{0:T(128)} %constant.7.clone.1.over_in, ...), custom_call_target="tpu_custom_call" | custom-call | flops 100663296 | bytes 6144 | tf_op jit(solution)/shard_map/tasks04/pallas_call | solution.py:190
  73.9 0.0 collective-permute-done.13.rest_0_
  73.9 2.2 %collective-permute-start.17 = (bf16[1296,128]{1,0:T(8,128)(2,1)S(1)}, bf16[1296,128]{1,0:T(8,128)(2,1)S(1)}, u32[]{:S(2)}, u32[]{:S(2)}) collective-permute-start(bf16[1296,128]{1,0:T(8,128)(2,1)S(1)} %collective-permute-done.13.rest_0_), channel_id=1, source_target_pairs={{0,1},{1,0},{2,3},{3,2},{4,5},{5,4},{6,7},{7,6},{8,9},{9,8},{10,11... | collective-permute-start | bytes 995336 | tf_op jit(solution)/shard_map/ppermute | solution.py:31
  76.2 3.1 %collective-permute-done.15.rest_1_ = bf16[1296,128]{1,0:T(8,128)(2,1)S(1)} collective-permute-done((bf16[1296,128]{1,0:T(8,128)(2,1)S(1)}, bf16[1296,128]{1,0:T(8,128)(2,1)S(1)}, u32[]{:S(2)}, u32[]{:S(2)}) %collective-permute-start.15) | collective-permute-done | bytes 331808 | tf_op jit(solution)/shard_map/ppermute | solution.py:31
  79.3 3.0 %collective-permute-start.18 = (bf16[1296,128]{1,0:T(8,128)(2,1)S(1)}, bf16[1296,128]{1,0:T(8,128)(2,1)S(1)}, u32[]{:S(2)}, u32[]{:S(2)}) collective-permute-start(bf16[1296,128]{1,0:T(8,128)(2,1)S(1)} %collective-permute-done.15.rest_1_), channel_id=1, source_target_pairs={{0,1},{1,0},{2,3},{3,2},{4,5},{5,4},{6,7},{7,6},{8,9},{9,8},{10,11... | collective-permute-start | bytes 995336 | tf_op jit(solution)/shard_map/ppermute | solution.py:31
  82.3 1.9 %collective-permute-start.19 = (bf16[1296,128]{1,0:T(8,128)(2,1)S(1)}, bf16[1296,128]{1,0:T(8,128)(2,1)S(1)}, u32[]{:S(2)}, u32[]{:S(2)}) collective-permute-start(bf16[1296,128]{1,0:T(8,128)(2,1)S(1)} %collective-permute-done.16.rest_2_), channel_id=1, source_target_pairs={{0,1},{1,0},{2,3},{3,2},{4,5},{5,4},{6,7},{7,6},{8,9},{9,8},{10,11... | collective-permute-start | bytes 995336 | tf_op jit(solution)/shard_map/ppermute | solution.py:31
  84.2 3.8 %tasks132.1 = (f32[4,128,128]{2,1,0:T(8,128)S(1)}, s32[1]{0:T(128)}) custom-call(s32[1600]{0:T(1024)S(1)} %get-tuple-element.43.lists, s32[8]{0:T(128)S(1)} %get-tuple-element.44.counts, bf16[192,128,128]{2,1,0:T(8,128)(2,1)S(1)} %get-tuple-element.45.tiles, f32[4,128,128]{2,1,0:T(8,128)S(1)} %get-tuple-element.49.acc_in, s32[1]{0:T(128)} %get-tuple-element.50.over_in, ...), custom_call_target="tpu_custom_call" | custom-call | flops 150994944 | bytes 9216 | tf_op jit(solution)/shard_map/tasks132/pallas_call | solution.py:190
  88.0 0.0 collective-permute-done.17.rest_0_
  88.0 0.0 collective-permute-done.19.rest_2_
  88.1 4.3 %tasks576.1 = (f32[4,128,128]{2,1,0:T(8,128)S(1)}, s32[1]{0:T(128)}, bf16[128,512]{1,0:T(8,128)(2,1)}) custom-call(s32[1600]{0:T(1024)S(1)} %get-tuple-element.43.lists, s32[8]{0:T(128)S(1)} %get-tuple-element.44.counts, bf16[192,128,128]{2,1,0:T(8,128)(2,1)S(1)} %get-tuple-element.45.tiles, f32[4,128,128]{2,1,0:T(8,128)S(1)} %get-tuple-element.52.acc_in, ...), custom_call_target="tpu_custom_call" | custom-call | flops 150994944 | bytes 9216 | tf_op jit(solution)/shard_map/tasks576/pallas_call | solution.py:190
  (5 shorter events, 0.0 us)
Async XLA Ops:
  1.4 31.1 %collective-permute-start.7 = (bf16[128,128]{1,0:T(8,128)(2,1)S(1)}, bf16[128,128]{1,0:T(8,128)(2,1)S(1)}, u32[]{:S(2)}, u32[]{:S(2)}) collective-permute-start(bf16[128,128]{1,0:T(8,128)(2,1)S(1)} %multiply_select_fusion), channel_id=1, source_target_pairs={{0,8},{1,9},{2,10},{3,11},{4,12},{5,13},{6,14},{7,15},{8,16},{9,17... | collective-permute-start | bytes 98312 | tf_op jit(solution)/shard_map/ppermute | solution.py:31
  11.1 21.4 %collective-permute-start.8 = (bf16[128,128]{1,0:T(8,128)(2,1)S(1)}, bf16[128,128]{1,0:T(8,128)(2,1)S(1)}, u32[]{:S(2)}, u32[]{:S(2)}) collective-permute-start(bf16[128,128]{1,0:T(8,128)(2,1)S(1)} %multiply_select_fusion), channel_id=1, source_target_pairs={{0,16},{1,17},{2,18},{3,19},{4,20},{5,21},{6,22},{7,23},{8,24},{9,... | collective-permute-start | bytes 98312 | tf_op jit(solution)/shard_map/ppermute | solution.py:31
  26.5 8.6 %collective-permute-start.9 = (bf16[128,128]{1,0:T(8,128)(2,1)S(1)}, bf16[128,128]{1,0:T(8,128)(2,1)S(1)}, u32[]{:S(2)}, u32[]{:S(2)}) collective-permute-start(bf16[128,128]{1,0:T(8,128)(2,1)S(1)} %multiply_select_fusion), channel_id=1, source_target_pairs={{0,24},{1,25},{2,26},{3,27},{4,28},{5,29},{6,30},{7,31},{8,0},{9,1... | collective-permute-start | bytes 98312 | tf_op jit(solution)/shard_map/ppermute | solution.py:31
  35.1 11.5 %collective-permute-start.10 = (bf16[4,128,128]{2,1,0:T(8,128)(2,1)S(1)}, bf16[4,128,128]{2,1,0:T(8,128)(2,1)S(1)}, u32[]{:S(2)}, u32[]{:S(2)}) collective-permute-start(bf16[4,128,128]{2,1,0:T(8,128)(2,1)S(1)} %pad_maximum_fusion.refs_0_), channel_id=1, source_target_pairs={{0,2},{1,3},{2,4},{3,5},{4,6},{5,7},{6,0},{7,1},{8,10},{9,11},{10,... | collective-permute-start | bytes 393224 | tf_op jit(solution)/shard_map/ppermute | solution.py:31
  38.7 12.2 %collective-permute-start.11 = (bf16[4,128,128]{2,1,0:T(8,128)(2,1)S(1)}, bf16[4,128,128]{2,1,0:T(8,128)(2,1)S(1)}, u32[]{:S(2)}, u32[]{:S(2)}) collective-permute-start(bf16[4,128,128]{2,1,0:T(8,128)(2,1)S(1)} %pad_maximum_fusion.refs_0_), channel_id=1, source_target_pairs={{0,4},{1,5},{2,6},{3,7},{4,0},{5,1},{6,2},{7,3},{8,12},{9,13},{10,... | collective-permute-start | bytes 393224 | tf_op jit(solution)/shard_map/ppermute | solution.py:31
  44.0 7.5 %collective-permute-start.12 = (bf16[4,128,128]{2,1,0:T(8,128)(2,1)S(1)}, bf16[4,128,128]{2,1,0:T(8,128)(2,1)S(1)}, u32[]{:S(2)}, u32[]{:S(2)}) collective-permute-start(bf16[4,128,128]{2,1,0:T(8,128)(2,1)S(1)} %pad_maximum_fusion.refs_0_), channel_id=1, source_target_pairs={{0,6},{1,7},{2,0},{3,1},{4,2},{5,3},{6,4},{7,5},{8,14},{9,15},{10,... | collective-permute-start | bytes 393224 | tf_op jit(solution)/shard_map/ppermute | solution.py:31
  52.3 18.5 %collective-permute-start.14 = (bf16[1296,128]{1,0:T(8,128)(2,1)S(1)}, bf16[1296,128]{1,0:T(8,128)(2,1)S(1)}, u32[]{:S(2)}, u32[]{:S(2)}) collective-permute-start(bf16[1296,128]{1,0:T(8,128)(2,1)S(1)} %get-tuple-element.46.rest_0_), channel_id=1, source_target_pairs={{0,1},{1,0},{2,3},{3,2},{4,5},{5,4},{6,7},{7,6},{8,9},{9,8},{10,11... | collective-permute-start | bytes 995336 | tf_op jit(solution)/shard_map/ppermute | solution.py:31
  56.9 17.0 %collective-permute-start.13 = (bf16[1296,128]{1,0:T(8,128)(2,1)S(1)}, bf16[1296,128]{1,0:T(8,128)(2,1)S(1)}, u32[]{:S(2)}, u32[]{:S(2)}) collective-permute-start(bf16[1296,128]{1,0:T(8,128)(2,1)S(1)} %get-tuple-element.46.rest_0_), channel_id=1, source_target_pairs={{0,32},{1,33},{2,34},{3,35},{4,36},{5,37},{6,38},{7,39},{8,40},{9,... | collective-permute-start | bytes 995336 | tf_op jit(solution)/shard_map/ppermute | solution.py:31
  60.0 19.3 %collective-permute-start.15 = (bf16[1296,128]{1,0:T(8,128)(2,1)S(1)}, bf16[1296,128]{1,0:T(8,128)(2,1)S(1)}, u32[]{:S(2)}, u32[]{:S(2)}) collective-permute-start(bf16[1296,128]{1,0:T(8,128)(2,1)S(1)} %get-tuple-element.46.rest_0_), channel_id=1, source_target_pairs={{0,96},{1,97},{2,98},{3,99},{4,100},{5,101},{6,102},{7,103},{8,104... | collective-permute-start | bytes 995336 | tf_op jit(solution)/shard_map/ppermute | solution.py:31
  63.8 18.5 %collective-permute-start.16 = (bf16[1296,128]{1,0:T(8,128)(2,1)S(1)}, bf16[1296,128]{1,0:T(8,128)(2,1)S(1)}, u32[]{:S(2)}, u32[]{:S(2)}) collective-permute-start(bf16[1296,128]{1,0:T(8,128)(2,1)S(1)} %get-tuple-element.46.rest_0_), channel_id=1, source_target_pairs={{0,64},{1,65},{2,66},{3,67},{4,68},{5,69},{6,70},{7,71},{8,72},{9,... | collective-permute-start | bytes 995336 | tf_op jit(solution)/shard_map/ppermute | solution.py:31
  73.9 14.1 %collective-permute-start.17 = (bf16[1296,128]{1,0:T(8,128)(2,1)S(1)}, bf16[1296,128]{1,0:T(8,128)(2,1)S(1)}, u32[]{:S(2)}, u32[]{:S(2)}) collective-permute-start(bf16[1296,128]{1,0:T(8,128)(2,1)S(1)} %collective-permute-done.13.rest_0_), channel_id=1, source_target_pairs={{0,1},{1,0},{2,3},{3,2},{4,5},{5,4},{6,7},{7,6},{8,9},{9,8},{10,11... | collective-permute-start | bytes 995336 | tf_op jit(solution)/shard_map/ppermute | solution.py:31
  79.3 8.8 %collective-permute-start.18 = (bf16[1296,128]{1,0:T(8,128)(2,1)S(1)}, bf16[1296,128]{1,0:T(8,128)(2,1)S(1)}, u32[]{:S(2)}, u32[]{:S(2)}) collective-permute-start(bf16[1296,128]{1,0:T(8,128)(2,1)S(1)} %collective-permute-done.15.rest_1_), channel_id=1, source_target_pairs={{0,1},{1,0},{2,3},{3,2},{4,5},{5,4},{6,7},{7,6},{8,9},{9,8},{10,11... | collective-permute-start | bytes 995336 | tf_op jit(solution)/shard_map/ppermute | solution.py:31
  82.3 5.8 %collective-permute-start.19 = (bf16[1296,128]{1,0:T(8,128)(2,1)S(1)}, bf16[1296,128]{1,0:T(8,128)(2,1)S(1)}, u32[]{:S(2)}, u32[]{:S(2)}) collective-permute-start(bf16[1296,128]{1,0:T(8,128)(2,1)S(1)} %collective-permute-done.16.rest_2_), channel_id=1, source_target_pairs={{0,1},{1,0},{2,3},{3,2},{4,5},{5,4},{6,7},{7,6},{8,9},{9,8},{10,11... | collective-permute-start | bytes 995336 | tf_op jit(solution)/shard_map/ppermute | solution.py:31

commit v5 on v4

--- a/solution.py
+++ b/solution.py
@@ -13,12 +13,14 @@
 NY, NZH, NZL, NC = 4, 4, 4, 2
 COLS = NY * NZH * NZL * NC
 LINE = NZH * NZL
-PIECES = NC * NY
-WIDE = 4
+PHASES = 3
+WIDE = 8
 SCAN = 8
 PACK = 10
 REST = LINE - PACK
 META = 16
+ROWS = PACK * 128 + META
+ORDER = (2, 1, 3)
 ABSENT, LATER = 99, 50
 
 
@@ -34,7 +36,7 @@
 def prep_kernel(own_k, own_out, own_live, help_k, help_out, help_live, table, own_tiles, help_tiles,
                 lists, counts, tiles, sems, *held):
     n_own, n_help = own_k.shape[0], help_k.shape[0]
-    cap = lists.shape[0] // PIECES
+    cap = lists.shape[0] // PHASES
     loads = []
     for j, ref in enumerate((own_k, own_out, own_live, help_k, help_out, help_live, table)):
         loads.append(pltpu.make_async_copy(ref, held[j], sems.at[2 + j]))
@@ -44,7 +46,7 @@
     fetch_help = pltpu.make_async_copy(help_tiles, tiles.at[pl.ds(n_own, n_help)], sems.at[1])
     fetch_own.start()
     fetch_help.start()
-    for p in range(PIECES):
+    for p in range(PHASES):
         counts[p] = 0
     for load in loads:
         load.wait()
@@ -52,9 +54,9 @@
     def scan(ks, outs, live, base):
         def step(s, carry):
             code = table[ks[s]]
-            p = code >> 4
+            p = code >> 6
             n = counts[p]
-            lists[p * cap + n] = ((s + base) << 7) | ((code & 15) << 3) | outs[s]
+            lists[p * cap + n] = ((s + base) << 9) | ((code & 63) << 3) | outs[s]
             counts[p] = n + live[s]
             return carry
 
@@ -62,7 +64,7 @@
 
     scan(own_k, own_out, own_live, 0)
     scan(help_k, help_out, help_live, n_own)
-    for p in range(PIECES):
+    for p in range(PHASES):
         for w in range(SCAN):
             lists[p * cap + counts[p] + w] = OB
     fetch_own.wait()
@@ -127,50 +129,56 @@
     )(*groups)
 
 
-def task_kernel(ids, places, last, lists, counts, tiles, acc_in, over_in, *rest):
-    pieces, rest = rest[:len(ids)], rest[len(ids):]
-    outs, (acc, meta_v, meta_s, picked, sem) = rest[:-5], rest[-5:]
-    cap = lists.shape[0] // PIECES
+def task_kernel(phase, places, last, lists, counts, tiles, acc_in, over_in, *rest):
+    outs, (acc, amps, meta_v, meta_s, picked, sem) = rest[:-6], rest[-6:]
+    n_pieces = len(outs) - (3 if last else 2)
+    pieces, outs = outs[:n_pieces], outs[n_pieces:]
+    cap = lists.shape[0] // PHASES
     for j, piece in enumerate(pieces):
         meta = piece[pl.ds(places * TILE, META), :].astype(jnp.float32).astype(jnp.int32)
         meta_v[pl.ds(j, 1), :] = meta[:1]
-    copy = pltpu.make_async_copy(meta_v, meta_s, sem.at[0])
+    copy = pltpu.make_async_copy(meta_v, meta_s, sem.at[n_pieces])
     copy.start()
+    gathers = []
+    for j, piece in enumerate(pieces):
+        gathers.append(pltpu.make_async_copy(piece, amps.at[pl.ds(j * ROWS, piece.shape[0])], sem.at[j]))
+        gathers[j].start()
     acc[pl.ds(0, OB)] = acc_in[...]
     copy.wait()
     over = over_in[0]
-    for j, (p, amps) in enumerate(zip(ids, pieces)):
+    for j in range(n_pieces):
         over = over + meta_s[j, LINE]
-
-        count = counts[p]
-
-        def pick(g, n, p=p, j=j, count=count):
-            for u in range(SCAN):
-                e = g * SCAN + u
-                entry = lists[p * cap + e]
-                place = meta_s[j, (entry >> 3) & 15]
-                picked[n] = (entry & ~127) | (place << 3) | (entry & 7)
-                n = n + jnp.where((place < places) & (e < count), 1, 0)
-            return n
-
-        n = lax.fori_loop(0, (count + SCAN - 1) >> 3, pick, 0)
+    count = counts[phase]
+
+    def pick(g, n):
+        for u in range(SCAN):
+            e = g * SCAN + u
+            entry = lists[phase * cap + e]
+            place = meta_s[(entry >> 7) & 3, (entry >> 3) & 15]
+            picked[n] = (entry & ~120) | ((place & 15) << 3)
+            n = n + jnp.where((place < places) & (e < count), 1, 0)
+        return n
+
+    n = lax.fori_loop(0, (count + SCAN - 1) >> 3, pick, 0)
+    for w in range(WIDE):
+        picked[n + w] = OB
+    for gather in gathers:
+        gather.wait()
+
+    def step(g, carry):
+        outputs, prods = [], []
         for w in range(WIDE):
-            picked[n + w] = OB
-
-        def step(g, carry, amps=amps):
-            outputs, prods = [], []
-            for w in range(WIDE):
-                entry = picked[g * WIDE + w]
-                outputs.append(entry & 7)
-                place = (entry >> 3) & 15
-                a = amps[pl.ds(pl.multiple_of(place * TILE, TILE), TILE), :]
-                b = tiles[entry >> 7]
-                prods.append(jnp.dot(a, b, preferred_element_type=jnp.float32))
-            for w in range(WIDE):
-                acc[outputs[w]] += prods[w]
-            return carry
-
-        lax.fori_loop(0, (n + WIDE - 1) >> 2, step, 0)
+            entry = picked[g * WIDE + w]
+            outputs.append(entry & 7)
+            row = ((entry >> 7) & 3) * ROWS + ((entry >> 3) & 15) * TILE
+            a = amps[pl.ds(pl.multiple_of(row, 16), TILE), :]
+            b = tiles[entry >> 9]
+            prods.append(jnp.dot(a, b, preferred_element_type=jnp.float32))
+        for w in range(WIDE):
+            acc[outputs[w]] += prods[w]
+        return carry
+
+    lax.fori_loop(0, (n + WIDE - 1) >> 3, step, 0)
     if last:
         for o in range(OB):
             outs[2][:, o * TILE:(o + 1) * TILE] = acc[o].astype(outs[2].dtype)
@@ -178,7 +186,7 @@
     outs[1][0] = over
 
 
-def run_tasks(ids, pieces, acc_in, last, lists, counts, tiles, places=PACK):
+def run_tasks(phase, pieces, acc_in, last, lists, counts, tiles, places=PACK):
     smem = pl.BlockSpec(memory_space=pltpu.SMEM)
     vmem = pl.BlockSpec(memory_space=pltpu.VMEM)
     out_shape = [jax.ShapeDtypeStruct((OB, TILE, TILE), jnp.float32), jax.ShapeDtypeStruct((1,), jnp.int32)]
@@ -186,22 +194,23 @@
     if last:
         out_shape.append(jax.ShapeDtypeStruct((TILE, OB * TILE), jnp.bfloat16))
         out_specs.append(vmem)
-    n = tiles.shape[0] * len(ids) // PIECES
+    n = tiles.shape[0] * len(pieces) // (NC * NY)
     return pl.pallas_call(
-        functools.partial(task_kernel, ids, places, last),
+        functools.partial(task_kernel, phase, places, last),
         out_shape=out_shape,
         in_specs=[smem, smem, vmem, vmem, smem] + [vmem] * len(pieces),
         out_specs=out_specs,
         scratch_shapes=[
             pltpu.VMEM((OB + 1, TILE, TILE), jnp.float32),
+            pltpu.VMEM((len(pieces) * ROWS, TILE), jnp.bfloat16),
             pltpu.VMEM((8, TILE), jnp.int32),
             pltpu.SMEM((8, TILE), jnp.int32),
-            pltpu.SMEM((tiles.shape[0] + 8,), jnp.int32),
-            pltpu.SemaphoreType.DMA((1,)),
+            pltpu.SMEM((tiles.shape[0] + 16,), jnp.int32),
+            pltpu.SemaphoreType.DMA((len(pieces) + 1,)),
         ],
         compiler_params=pltpu.CompilerParams(vmem_limit_bytes=24 << 20),
-        cost_estimate=pl.CostEstimate(flops=n * TILE ** 3, bytes_accessed=n * TILE, transcendentals=0),
-        name="tasks" + "".join(str(p) for p in ids),
+        cost_estimate=pl.CostEstimate(flops=n * 20 * TILE ** 3, bytes_accessed=8 << 20, transcendentals=0),
+        name=f"tasks{phase}",
     )(lists, counts, tiles, *acc_in, *pieces)
 
 
@@ -209,7 +218,9 @@
     me, k = lax.axis_index("col"), jnp.arange(COLS, dtype=jnp.int32)
     c, y = (me ^ k) & 1, (me ^ k) >> 5
     zl, zh = ((me >> 1) - (k >> 1)) & 3, ((me >> 3) - (k >> 3)) & 3
-    table = ((c * NY + y) * NZL + zl) * NZH + zh
+    rank = sum(jnp.where(y == k, j, 0) for j, k in enumerate(ORDER))
+    group = jnp.where(y == 0, c, (1 + c) * 4 + rank)
+    table = (group * NZL + zl) * NZH + zh
     n = own_k.shape[0] + help_k.shape[0]
     smem = pl.BlockSpec(memory_space=pltpu.SMEM)
     hbm = pl.BlockSpec(memory_space=pltpu.HBM)
@@ -217,8 +228,8 @@
     return pl.pallas_call(
         prep_kernel,
         out_shape=(
-            jax.ShapeDtypeStruct((PIECES * (n + 8),), jnp.int32),
-            jax.ShapeDtypeStruct((PIECES,), jnp.int32),
+            jax.ShapeDtypeStruct((PHASES * (n + 8),), jnp.int32),
+            jax.ShapeDtypeStruct((PHASES,), jnp.int32),
             pltpu.VMEM((n, TILE, TILE), jnp.bfloat16),
         ),
         in_specs=[hbm] * 9,
@@ -248,19 +259,20 @@
     head, tail = pack([first] + [move(first, zl=k) for k in (1, 2, 3)])
     lists, counts, tiles = prepare(
         own_tiles, own_k, own_out, own_live, help_tiles, help_k, help_out, help_live)
-    ys = {k: move(head, y=k) for k in (1, 3, 2)}
     tasks = functools.partial(run_tasks, lists=lists, counts=counts, tiles=tiles)
+    ys = [move(head, y=k) for k in ORDER]
     acc = (jnp.zeros((OB, TILE, TILE), jnp.float32), jnp.zeros((1,), jnp.int32))
-    acc = tasks((0, NY), [head, move(head, c=1)], acc, False)
-    ys[1], acc = lax.optimization_barrier((ys[1], acc))
-    ys_c = {k: move(ys[k], c=1) for k in (1, 3, 2)}
-    acc = tasks((1, 3, 2), [ys[1], ys[3], ys[2]], acc, False)
-    total, over, out = tasks((NY + 1, NY + 3, NY + 2), [ys_c[1], ys_c[3], ys_c[2]], acc, True)
+    acc = tasks(0, [head, move(head, c=1)], acc, False)
+    ys[0], acc = lax.optimization_barrier((ys[0], acc))
+    ys_c = [move(v, c=1) for v in ys]
+    acc = tasks(1, ys, acc, False)
+    total, over, out = tasks(2, ys_c, acc, True)
 
     def second_round(tail, total, over, out):
-        line = [tail] + [move(tail, y=k) for k in (1, 2, 3)]
-        pieces = line + [move(v, c=1) for v in line]
-        return tasks(tuple(range(PIECES)), pieces, (total, over), True, places=REST)[2]
+        ys = [move(tail, y=k) for k in ORDER]
+        acc = tasks(0, [tail, move(tail, c=1)], (total, over), False, places=REST)
+        acc = tasks(1, ys, acc, False, places=REST)
+        return tasks(2, [move(v, c=1) for v in ys], acc, True, places=REST)[2]
 
     return lax.cond(over[0] > 0, second_round, lambda tail, total, over, out: out, tail, total, over, out)
 

time: 93.7 us -> 90.3 us (0.964)
  Pallas kernels: 15.9 us -> 14.1 us
  waiting for transfers between devices: 10.6 us -> 9.23 us
    pallas_call x4, Pallas kernels: 15 us -> 13.3 us  [the longest x3 9.5 us: run_tasks(): pl.pallas_call(functools.partial(task_kernel, phase, places, last), out_s...]
    ppermute x13, waiting for transfers between devices: 10.6 us -> 9.23 us  [move(): return lax.ppermute(x, 'col', pairs)]
  transfers between devices with their start and end apart: 13 -> 13, of which waited for: 4 -> 4; matrix products, arithmetic and copies ran while one was open for 1% -> 1% of each run, Pallas kernels for 12% -> 10%
where the time goes in v5:
time: 90.3 us; the launch traced here: 89.7 us
  starting transfers between devices  62.6 us (69%)
  Pallas kernels  14.1 us (16%)
  waiting for transfers between devices  9.23 us (10%)
  other arithmetic  2.07 us (2%)
  between operations  1.56 us (2%)
    ppermute x13, starting transfers between devices, move(): return lax.ppermute(x, 'col', pairs)  62.6 us
    pallas_call x3, Pallas kernels, run_tasks(): pl.pallas_call(functools.partial(task_kernel, phase, places, last), out_s...  9.5 us
    ppermute x13, waiting for transfers between devices, move(): return lax.ppermute(x, 'col', pairs)  9.23 us
    pallas_call x1, Pallas kernels, prepare(): pl.pallas_call(prep_kernel, out_shape=(jax.ShapeDtypeStruct((PHASES * (n...  3.81 us
  transfers between devices with their start and end apart: 13, of which 4 were waited for; matrix products, arithmetic and copies ran while one was open for 1% of the time, Pallas kernels for 10%

profile of v5, /device:TPU:1, one launch (start us, length us, event | category | flops | bytes accessed | tf_op | source)
XLA Modules:
  0.0 89.7 jit_solution(2178138618594011277)
XLA Ops:
  0.7 0.8 multiply_select_fusion
  1.4 9.6 %collective-permute-start.7 = (bf16[128,128]{1,0:T(8,128)(2,1)S(1)}, bf16[128,128]{1,0:T(8,128)(2,1)S(1)}, u32[]{:S(2)}, u32[]{:S(2)}) collective-permute-start(bf16[128,128]{1,0:T(8,128)(2,1)S(1)} %multiply_select_fusion), channel_id=1, source_target_pairs={{0,8},{1,9},{2,10},{3,11},{4,12},{5,13},{6,14},{7,15},{8,16},{9,17... | collective-permute-start | bytes 98312 | tf_op jit(solution)/shard_map/ppermute | solution.py:33
  11.1 15.4 %collective-permute-start.8 = (bf16[128,128]{1,0:T(8,128)(2,1)S(1)}, bf16[128,128]{1,0:T(8,128)(2,1)S(1)}, u32[]{:S(2)}, u32[]{:S(2)}) collective-permute-start(bf16[128,128]{1,0:T(8,128)(2,1)S(1)} %multiply_select_fusion), channel_id=1, source_target_pairs={{0,16},{1,17},{2,18},{3,19},{4,20},{5,21},{6,22},{7,23},{8,24},{9,... | collective-permute-start | bytes 98312 | tf_op jit(solution)/shard_map/ppermute | solution.py:33
  26.5 5.2 %collective-permute-start.9 = (bf16[128,128]{1,0:T(8,128)(2,1)S(1)}, bf16[128,128]{1,0:T(8,128)(2,1)S(1)}, u32[]{:S(2)}, u32[]{:S(2)}) collective-permute-start(bf16[128,128]{1,0:T(8,128)(2,1)S(1)} %multiply_select_fusion), channel_id=1, source_target_pairs={{0,24},{1,25},{2,26},{3,27},{4,28},{5,29},{6,30},{7,31},{8,0},{9,1... | collective-permute-start | bytes 98312 | tf_op jit(solution)/shard_map/ppermute | solution.py:33
  31.7 0.8 fusion.4
  32.5 0.0 collective-permute-done.7
  32.5 0.0 collective-permute-done.8
  32.5 2.6 %collective-permute-done.9 = bf16[128,128]{1,0:T(8,128)(2,1)S(1)} collective-permute-done((bf16[128,128]{1,0:T(8,128)(2,1)S(1)}, bf16[128,128]{1,0:T(8,128)(2,1)S(1)}, u32[]{:S(2)}, u32[]{:S(2)}) %collective-permute-start.9) | collective-permute-done | bytes 32800 | tf_op jit(solution)/shard_map/ppermute | solution.py:33
  35.1 3.6 %collective-permute-start.10 = (bf16[4,128,128]{2,1,0:T(8,128)(2,1)S(1)}, bf16[4,128,128]{2,1,0:T(8,128)(2,1)S(1)}, u32[]{:S(2)}, u32[]{:S(2)}) collective-permute-start(bf16[4,128,128]{2,1,0:T(8,128)(2,1)S(1)} %pad_maximum_fusion.refs_0_), channel_id=1, source_target_pairs={{0,2},{1,3},{2,4},{3,5},{4,6},{5,7},{6,0},{7,1},{8,10},{9,11},{10,... | collective-permute-start | bytes 393224 | tf_op jit(solution)/shard_map/ppermute | solution.py:33
  38.7 5.3 %collective-permute-start.11 = (bf16[4,128,128]{2,1,0:T(8,128)(2,1)S(1)}, bf16[4,128,128]{2,1,0:T(8,128)(2,1)S(1)}, u32[]{:S(2)}, u32[]{:S(2)}) collective-permute-start(bf16[4,128,128]{2,1,0:T(8,128)(2,1)S(1)} %pad_maximum_fusion.refs_0_), channel_id=1, source_target_pairs={{0,4},{1,5},{2,6},{3,7},{4,0},{5,1},{6,2},{7,3},{8,12},{9,13},{10,... | collective-permute-start | bytes 393224 | tf_op jit(solution)/shard_map/ppermute | solution.py:33
  44.0 2.6 %collective-permute-start.12 = (bf16[4,128,128]{2,1,0:T(8,128)(2,1)S(1)}, bf16[4,128,128]{2,1,0:T(8,128)(2,1)S(1)}, u32[]{:S(2)}, u32[]{:S(2)}) collective-permute-start(bf16[4,128,128]{2,1,0:T(8,128)(2,1)S(1)} %pad_maximum_fusion.refs_0_), channel_id=1, source_target_pairs={{0,6},{1,7},{2,0},{3,1},{4,2},{5,3},{6,4},{7,5},{8,14},{9,15},{10,... | collective-permute-start | bytes 393224 | tf_op jit(solution)/shard_map/ppermute | solution.py:33
  46.6 0.0 collective-permute-done.10.refs_1_
  46.7 4.2 %collective-permute-done.11.refs_2_ = bf16[4,128,128]{2,1,0:T(8,128)(2,1)S(1)} collective-permute-done((bf16[4,128,128]{2,1,0:T(8,128)(2,1)S(1)}, bf16[4,128,128]{2,1,0:T(8,128)(2,1)S(1)}, u32[]{:S(2)}, u32[]{:S(2)}) %collective-permute-start.11) | collective-permute-done | bytes 131104 | tf_op jit(solution)/shard_map/ppermute | solution.py:33
  50.9 0.6 collective-permute-done.12.refs_3_
  51.5 0.8 pack.1
  52.3 4.6 %collective-permute-start.14 = (bf16[1296,128]{1,0:T(8,128)(2,1)S(1)}, bf16[1296,128]{1,0:T(8,128)(2,1)S(1)}, u32[]{:S(2)}, u32[]{:S(2)}) collective-permute-start(bf16[1296,128]{1,0:T(8,128)(2,1)S(1)} %get-tuple-element.50.rest_0_), channel_id=1, source_target_pairs={{0,1},{1,0},{2,3},{3,2},{4,5},{5,4},{6,7},{7,6},{8,9},{9,8},{10,11... | collective-permute-start | bytes 995336 | tf_op jit(solution)/shard_map/ppermute | solution.py:33
  56.9 4.7 %collective-permute-start.13 = (bf16[1296,128]{1,0:T(8,128)(2,1)S(1)}, bf16[1296,128]{1,0:T(8,128)(2,1)S(1)}, u32[]{:S(2)}, u32[]{:S(2)}) collective-permute-start(bf16[1296,128]{1,0:T(8,128)(2,1)S(1)} %get-tuple-element.50.rest_0_), channel_id=1, source_target_pairs={{0,64},{1,65},{2,66},{3,67},{4,68},{5,69},{6,70},{7,71},{8,72},{9,... | collective-permute-start | bytes 995336 | tf_op jit(solution)/shard_map/ppermute | solution.py:33
  61.6 2.3 %collective-permute-start.15 = (bf16[1296,128]{1,0:T(8,128)(2,1)S(1)}, bf16[1296,128]{1,0:T(8,128)(2,1)S(1)}, u32[]{:S(2)}, u32[]{:S(2)}) collective-permute-start(bf16[1296,128]{1,0:T(8,128)(2,1)S(1)} %get-tuple-element.50.rest_0_), channel_id=1, source_target_pairs={{0,32},{1,33},{2,34},{3,35},{4,36},{5,37},{6,38},{7,39},{8,40},{9,... | collective-permute-start | bytes 995336 | tf_op jit(solution)/shard_map/ppermute | solution.py:33
  63.9 2.3 %collective-permute-start.16 = (bf16[1296,128]{1,0:T(8,128)(2,1)S(1)}, bf16[1296,128]{1,0:T(8,128)(2,1)S(1)}, u32[]{:S(2)}, u32[]{:S(2)}) collective-permute-start(bf16[1296,128]{1,0:T(8,128)(2,1)S(1)} %get-tuple-element.50.rest_0_), channel_id=1, source_target_pairs={{0,96},{1,97},{2,98},{3,99},{4,100},{5,101},{6,102},{7,103},{8,104... | collective-permute-start | bytes 995336 | tf_op jit(solution)/shard_map/ppermute | solution.py:33
  66.2 0.5 and_add_fusion.table
  66.7 3.8 %prep.1 = (s32[600]{0:T(1024)S(1)}, s32[3]{0:T(128)S(1)}, bf16[192,128,128]{2,1,0:T(8,128)(2,1)S(1)}) custom-call(s32[160]{0:T(256)} %own_k.1, s32[160]{0:T(256)} %own_out.1, s32[160]{0:T(256)} %own_live.1, s32[32]{0:T(128)} %help_k.1, s32[32]{0:T(128)} %help_out.1, s32[32]{0:T(128)} %help_live.1, s32[128]{0:T(128)} %and_add_fusion.table, ...), custom_call_target="tpu_custom_call" | custom-call | bytes 8388608 | tf_op jit(solution)/shard_map/prep/pallas_call | solution.py:228
  70.5 0.0 collective-permute-done.14.rest_1_
  70.6 2.3 %tasks0.3 = (f32[4,128,128]{2,1,0:T(8,128)S(1)}, s32[1]{0:T(128)}) custom-call(s32[600]{0:T(1024)S(1)} %get-tuple-element.47.lists, s32[3]{0:T(128)S(1)} %get-tuple-element.48.counts, bf16[192,128,128]{2,1,0:T(8,128)(2,1)S(1)} %get-tuple-element.49.tiles, f32[4,128,128]{2,1,0:T(8,128)S(1)} %broadcast_in_dim.28.acc_in, s32[1]{0:T(128)} %constant.8.clone.1.over_in, ...), custom_call_target="tpu_custom_call" | custom-call | flops 2013265920 | bytes 8388608 | tf_op jit(solution)/shard_map/tasks0/pallas_call | solution.py:198
  72.8 0.0 collective-permute-done.13.rest_0_
  72.8 2.4 %collective-permute-start.17 = (bf16[1296,128]{1,0:T(8,128)(2,1)S(1)}, bf16[1296,128]{1,0:T(8,128)(2,1)S(1)}, u32[]{:S(2)}, u32[]{:S(2)}) collective-permute-start(bf16[1296,128]{1,0:T(8,128)(2,1)S(1)} %collective-permute-done.13.rest_0_), channel_id=1, source_target_pairs={{0,1},{1,0},{2,3},{3,2},{4,5},{5,4},{6,7},{7,6},{8,9},{9,8},{10,11... | collective-permute-start | bytes 995336 | tf_op jit(solution)/shard_map/ppermute | solution.py:33
  75.3 1.8 %collective-permute-done.15.rest_1_ = bf16[1296,128]{1,0:T(8,128)(2,1)S(1)} collective-permute-done((bf16[1296,128]{1,0:T(8,128)(2,1)S(1)}, bf16[1296,128]{1,0:T(8,128)(2,1)S(1)}, u32[]{:S(2)}, u32[]{:S(2)}) %collective-permute-start.15) | collective-permute-done | bytes 331808 | tf_op jit(solution)/shard_map/ppermute | solution.py:33
  77.0 2.7 %collective-permute-start.18 = (bf16[1296,128]{1,0:T(8,128)(2,1)S(1)}, bf16[1296,128]{1,0:T(8,128)(2,1)S(1)}, u32[]{:S(2)}, u32[]{:S(2)}) collective-permute-start(bf16[1296,128]{1,0:T(8,128)(2,1)S(1)} %collective-permute-done.15.rest_1_), channel_id=1, source_target_pairs={{0,1},{1,0},{2,3},{3,2},{4,5},{5,4},{6,7},{7,6},{8,9},{9,8},{10,11... | collective-permute-start | bytes 995336 | tf_op jit(solution)/shard_map/ppermute | solution.py:33
  79.8 1.9 %collective-permute-start.19 = (bf16[1296,128]{1,0:T(8,128)(2,1)S(1)}, bf16[1296,128]{1,0:T(8,128)(2,1)S(1)}, u32[]{:S(2)}, u32[]{:S(2)}) collective-permute-start(bf16[1296,128]{1,0:T(8,128)(2,1)S(1)} %collective-permute-done.16.rest_2_), channel_id=1, source_target_pairs={{0,1},{1,0},{2,3},{3,2},{4,5},{5,4},{6,7},{7,6},{8,9},{9,8},{10,11... | collective-permute-start | bytes 995336 | tf_op jit(solution)/shard_map/ppermute | solution.py:33
  81.7 3.3 %tasks1.3 = (f32[4,128,128]{2,1,0:T(8,128)S(1)}, s32[1]{0:T(128)}) custom-call(s32[600]{0:T(1024)S(1)} %get-tuple-element.47.lists, s32[3]{0:T(128)S(1)} %get-tuple-element.48.counts, bf16[192,128,128]{2,1,0:T(8,128)(2,1)S(1)} %get-tuple-element.49.tiles, f32[4,128,128]{2,1,0:T(8,128)S(1)} %get-tuple-element.53.acc_in, s32[1]{0:T(128)} %get-tuple-element.54.over_in, ...), custom_call_target="tpu_custom_call" | custom-call | flops 3019898880 | bytes 8388608 | tf_op jit(solution)/shard_map/tasks1/pallas_call | solution.py:198
  85.0 0.0 collective-permute-done.17.rest_0_
  85.0 0.0 collective-permute-done.18.rest_1_
  85.0 3.9 %tasks2.3 = (f32[4,128,128]{2,1,0:T(8,128)S(1)}, s32[1]{0:T(128)}, bf16[128,512]{1,0:T(8,128)(2,1)}) custom-call(s32[600]{0:T(1024)S(1)} %get-tuple-element.47.lists, s32[3]{0:T(128)S(1)} %get-tuple-element.48.counts, bf16[192,128,128]{2,1,0:T(8,128)(2,1)S(1)} %get-tuple-element.49.tiles, f32[4,128,128]{2,1,0:T(8,128)S(1)} %get-tuple-element.56.acc_in, ...), custom_call_target="tpu_custom_call" | custom-call | flops 3019898880 | bytes 8388608 | tf_op jit(solution)/shard_map/tasks2/pallas_call | solution.py:198
  (5 shorter events, 0.0 us)
Async XLA Ops:
  1.4 31.1 %collective-permute-start.7 = (bf16[128,128]{1,0:T(8,128)(2,1)S(1)}, bf16[128,128]{1,0:T(8,128)(2,1)S(1)}, u32[]{:S(2)}, u32[]{:S(2)}) collective-permute-start(bf16[128,128]{1,0:T(8,128)(2,1)S(1)} %multiply_select_fusion), channel_id=1, source_target_pairs={{0,8},{1,9},{2,10},{3,11},{4,12},{5,13},{6,14},{7,15},{8,16},{9,17... | collective-permute-start | bytes 98312 | tf_op jit(solution)/shard_map/ppermute | solution.py:33
  11.1 21.4 %collective-permute-start.8 = (bf16[128,128]{1,0:T(8,128)(2,1)S(1)}, bf16[128,128]{1,0:T(8,128)(2,1)S(1)}, u32[]{:S(2)}, u32[]{:S(2)}) collective-permute-start(bf16[128,128]{1,0:T(8,128)(2,1)S(1)} %multiply_select_fusion), channel_id=1, source_target_pairs={{0,16},{1,17},{2,18},{3,19},{4,20},{5,21},{6,22},{7,23},{8,24},{9,... | collective-permute-start | bytes 98312 | tf_op jit(solution)/shard_map/ppermute | solution.py:33
  26.5 8.6 %collective-permute-start.9 = (bf16[128,128]{1,0:T(8,128)(2,1)S(1)}, bf16[128,128]{1,0:T(8,128)(2,1)S(1)}, u32[]{:S(2)}, u32[]{:S(2)}) collective-permute-start(bf16[128,128]{1,0:T(8,128)(2,1)S(1)} %multiply_select_fusion), channel_id=1, source_target_pairs={{0,24},{1,25},{2,26},{3,27},{4,28},{5,29},{6,30},{7,31},{8,0},{9,1... | collective-permute-start | bytes 98312 | tf_op jit(solution)/shard_map/ppermute | solution.py:33
  35.1 11.5 %collective-permute-start.10 = (bf16[4,128,128]{2,1,0:T(8,128)(2,1)S(1)}, bf16[4,128,128]{2,1,0:T(8,128)(2,1)S(1)}, u32[]{:S(2)}, u32[]{:S(2)}) collective-permute-start(bf16[4,128,128]{2,1,0:T(8,128)(2,1)S(1)} %pad_maximum_fusion.refs_0_), channel_id=1, source_target_pairs={{0,2},{1,3},{2,4},{3,5},{4,6},{5,7},{6,0},{7,1},{8,10},{9,11},{10,... | collective-permute-start | bytes 393224 | tf_op jit(solution)/shard_map/ppermute | solution.py:33
  38.7 12.2 %collective-permute-start.11 = (bf16[4,128,128]{2,1,0:T(8,128)(2,1)S(1)}, bf16[4,128,128]{2,1,0:T(8,128)(2,1)S(1)}, u32[]{:S(2)}, u32[]{:S(2)}) collective-permute-start(bf16[4,128,128]{2,1,0:T(8,128)(2,1)S(1)} %pad_maximum_fusion.refs_0_), channel_id=1, source_target_pairs={{0,4},{1,5},{2,6},{3,7},{4,0},{5,1},{6,2},{7,3},{8,12},{9,13},{10,... | collective-permute-start | bytes 393224 | tf_op jit(solution)/shard_map/ppermute | solution.py:33
  44.0 7.5 %collective-permute-start.12 = (bf16[4,128,128]{2,1,0:T(8,128)(2,1)S(1)}, bf16[4,128,128]{2,1,0:T(8,128)(2,1)S(1)}, u32[]{:S(2)}, u32[]{:S(2)}) collective-permute-start(bf16[4,128,128]{2,1,0:T(8,128)(2,1)S(1)} %pad_maximum_fusion.refs_0_), channel_id=1, source_target_pairs={{0,6},{1,7},{2,0},{3,1},{4,2},{5,3},{6,4},{7,5},{8,14},{9,15},{10,... | collective-permute-start | bytes 393224 | tf_op jit(solution)/shard_map/ppermute | solution.py:33
  52.3 18.2 %collective-permute-start.14 = (bf16[1296,128]{1,0:T(8,128)(2,1)S(1)}, bf16[1296,128]{1,0:T(8,128)(2,1)S(1)}, u32[]{:S(2)}, u32[]{:S(2)}) collective-permute-start(bf16[1296,128]{1,0:T(8,128)(2,1)S(1)} %get-tuple-element.50.rest_0_), channel_id=1, source_target_pairs={{0,1},{1,0},{2,3},{3,2},{4,5},{5,4},{6,7},{7,6},{8,9},{9,8},{10,11... | collective-permute-start | bytes 995336 | tf_op jit(solution)/shard_map/ppermute | solution.py:33
  56.9 16.0 %collective-permute-start.13 = (bf16[1296,128]{1,0:T(8,128)(2,1)S(1)}, bf16[1296,128]{1,0:T(8,128)(2,1)S(1)}, u32[]{:S(2)}, u32[]{:S(2)}) collective-permute-start(bf16[1296,128]{1,0:T(8,128)(2,1)S(1)} %get-tuple-element.50.rest_0_), channel_id=1, source_target_pairs={{0,64},{1,65},{2,66},{3,67},{4,68},{5,69},{6,70},{7,71},{8,72},{9,... | collective-permute-start | bytes 995336 | tf_op jit(solution)/shard_map/ppermute | solution.py:33
  61.6 15.5 %collective-permute-start.15 = (bf16[1296,128]{1,0:T(8,128)(2,1)S(1)}, bf16[1296,128]{1,0:T(8,128)(2,1)S(1)}, u32[]{:S(2)}, u32[]{:S(2)}) collective-permute-start(bf16[1296,128]{1,0:T(8,128)(2,1)S(1)} %get-tuple-element.50.rest_0_), channel_id=1, source_target_pairs={{0,32},{1,33},{2,34},{3,35},{4,36},{5,37},{6,38},{7,39},{8,40},{9,... | collective-permute-start | bytes 995336 | tf_op jit(solution)/shard_map/ppermute | solution.py:33
  63.9 15.9 %collective-permute-start.16 = (bf16[1296,128]{1,0:T(8,128)(2,1)S(1)}, bf16[1296,128]{1,0:T(8,128)(2,1)S(1)}, u32[]{:S(2)}, u32[]{:S(2)}) collective-permute-start(bf16[1296,128]{1,0:T(8,128)(2,1)S(1)} %get-tuple-element.50.rest_0_), channel_id=1, source_target_pairs={{0,96},{1,97},{2,98},{3,99},{4,100},{5,101},{6,102},{7,103},{8,104... | collective-permute-start | bytes 995336 | tf_op jit(solution)/shard_map/ppermute | solution.py:33
  72.8 12.2 %collective-permute-start.17 = (bf16[1296,128]{1,0:T(8,128)(2,1)S(1)}, bf16[1296,128]{1,0:T(8,128)(2,1)S(1)}, u32[]{:S(2)}, u32[]{:S(2)}) collective-permute-start(bf16[1296,128]{1,0:T(8,128)(2,1)S(1)} %collective-permute-done.13.rest_0_), channel_id=1, source_target_pairs={{0,1},{1,0},{2,3},{3,2},{4,5},{5,4},{6,7},{7,6},{8,9},{9,8},{10,11... | collective-permute-start | bytes 995336 | tf_op jit(solution)/shard_map/ppermute | solution.py:33
  77.0 8.0 %collective-permute-start.18 = (bf16[1296,128]{1,0:T(8,128)(2,1)S(1)}, bf16[1296,128]{1,0:T(8,128)(2,1)S(1)}, u32[]{:S(2)}, u32[]{:S(2)}) collective-permute-start(bf16[1296,128]{1,0:T(8,128)(2,1)S(1)} %collective-permute-done.15.rest_1_), channel_id=1, source_target_pairs={{0,1},{1,0},{2,3},{3,2},{4,5},{5,4},{6,7},{7,6},{8,9},{9,8},{10,11... | collective-permute-start | bytes 995336 | tf_op jit(solution)/shard_map/ppermute | solution.py:33
  79.8 5.3 %collective-permute-start.19 = (bf16[1296,128]{1,0:T(8,128)(2,1)S(1)}, bf16[1296,128]{1,0:T(8,128)(2,1)S(1)}, u32[]{:S(2)}, u32[]{:S(2)}) collective-permute-start(bf16[1296,128]{1,0:T(8,128)(2,1)S(1)} %collective-permute-done.16.rest_2_), channel_id=1, source_target_pairs={{0,1},{1,0},{2,3},{3,2},{4,5},{5,4},{6,7},{7,6},{8,9},{9,8},{10,11... | collective-permute-start | bytes 995336 | tf_op jit(solution)/shard_map/ppermute | solution.py:33

commit v6 on v5

--- a/solution.py
+++ b/solution.py
@@ -19,7 +19,6 @@
 PACK = 10
 REST = LINE - PACK
 META = 16
-ROWS = PACK * 128 + META
 ORDER = (2, 1, 3)
 ABSENT, LATER = 99, 50
 
@@ -34,9 +33,9 @@
 
 
 def prep_kernel(own_k, own_out, own_live, help_k, help_out, help_live, table, own_tiles, help_tiles,
-                lists, counts, tiles, sems, *held):
+                lists, tiles, sems, *held):
     n_own, n_help = own_k.shape[0], help_k.shape[0]
-    cap = lists.shape[0] // PHASES
+    cap = n_own + n_help + SCAN
     loads = []
     for j, ref in enumerate((own_k, own_out, own_live, help_k, help_out, help_live, table)):
         loads.append(pltpu.make_async_copy(ref, held[j], sems.at[2 + j]))
@@ -47,7 +46,7 @@
     fetch_own.start()
     fetch_help.start()
     for p in range(PHASES):
-        counts[p] = 0
+        lists[PHASES * cap + p] = 0
     for load in loads:
         load.wait()
 
@@ -55,9 +54,9 @@
         def step(s, carry):
             code = table[ks[s]]
             p = code >> 6
-            n = counts[p]
+            n = lists[PHASES * cap + p]
             lists[p * cap + n] = ((s + base) << 9) | ((code & 63) << 3) | outs[s]
-            counts[p] = n + live[s]
+            lists[PHASES * cap + p] = n + live[s]
             return carry
 
         lax.fori_loop(0, ks.shape[0], step, 0)
@@ -65,8 +64,9 @@
     scan(own_k, own_out, own_live, 0)
     scan(help_k, help_out, help_live, n_own)
     for p in range(PHASES):
+        n = lists[PHASES * cap + p]
         for w in range(SCAN):
-            lists[p * cap + counts[p] + w] = OB
+            lists[p * cap + n + w] = OB
     fetch_own.wait()
     fetch_help.wait()
 
@@ -129,26 +129,25 @@
     )(*groups)
 
 
-def task_kernel(phase, places, last, lists, counts, tiles, acc_in, over_in, *rest):
-    outs, (acc, amps, meta_v, meta_s, picked, sem) = rest[:-6], rest[-6:]
+def task_kernel(phase, places, last, lists_v, tiles, acc_in, over_in, *rest):
+    outs, (acc, meta_v, meta_s, lists, picked, sem) = rest[:-6], rest[-6:]
     n_pieces = len(outs) - (3 if last else 2)
     pieces, outs = outs[:n_pieces], outs[n_pieces:]
-    cap = lists.shape[0] // PHASES
+    cap = tiles.shape[0] + SCAN
+    load = pltpu.make_async_copy(lists_v, lists, sem.at[0])
+    load.start()
+    over = over_in[...]
     for j, piece in enumerate(pieces):
         meta = piece[pl.ds(places * TILE, META), :].astype(jnp.float32).astype(jnp.int32)
         meta_v[pl.ds(j, 1), :] = meta[:1]
-    copy = pltpu.make_async_copy(meta_v, meta_s, sem.at[n_pieces])
+        over = over + meta[:8]
+    meta_v[pl.ds(n_pieces, 1), :] = over[:1]
+    copy = pltpu.make_async_copy(meta_v, meta_s, sem.at[1])
     copy.start()
-    gathers = []
-    for j, piece in enumerate(pieces):
-        gathers.append(pltpu.make_async_copy(piece, amps.at[pl.ds(j * ROWS, piece.shape[0])], sem.at[j]))
-        gathers[j].start()
     acc[pl.ds(0, OB)] = acc_in[...]
+    load.wait()
     copy.wait()
-    over = over_in[0]
-    for j in range(n_pieces):
-        over = over + meta_s[j, LINE]
-    count = counts[phase]
+    count = lists[PHASES * cap + phase]
 
     def pick(g, n):
         for u in range(SCAN):
@@ -162,16 +161,16 @@
     n = lax.fori_loop(0, (count + SCAN - 1) >> 3, pick, 0)
     for w in range(WIDE):
         picked[n + w] = OB
-    for gather in gathers:
-        gather.wait()
 
     def step(g, carry):
         outputs, prods = [], []
         for w in range(WIDE):
             entry = picked[g * WIDE + w]
             outputs.append(entry & 7)
-            row = ((entry >> 7) & 3) * ROWS + ((entry >> 3) & 15) * TILE
-            a = amps[pl.ds(pl.multiple_of(row, 16), TILE), :]
+            rows = pl.ds(pl.multiple_of(((entry >> 3) & 15) * TILE, TILE), TILE)
+            a = pieces[0][rows, :]
+            for j in range(1, n_pieces):
+                a = jnp.where(((entry >> 7) & 3) == j, pieces[j][rows, :], a)
             b = tiles[entry >> 9]
             prods.append(jnp.dot(a, b, preferred_element_type=jnp.float32))
         for w in range(WIDE):
@@ -183,14 +182,17 @@
         for o in range(OB):
             outs[2][:, o * TILE:(o + 1) * TILE] = acc[o].astype(outs[2].dtype)
     outs[0][...] = acc[pl.ds(0, OB)]
-    outs[1][0] = over
-
-
-def run_tasks(phase, pieces, acc_in, last, lists, counts, tiles, places=PACK):
+    if last:
+        outs[1][0] = meta_s[n_pieces, LINE]
+    else:
+        outs[1][...] = over
+
+
+def run_tasks(phase, pieces, acc_in, last, lists, tiles, places=PACK):
     smem = pl.BlockSpec(memory_space=pltpu.SMEM)
     vmem = pl.BlockSpec(memory_space=pltpu.VMEM)
-    out_shape = [jax.ShapeDtypeStruct((OB, TILE, TILE), jnp.float32), jax.ShapeDtypeStruct((1,), jnp.int32)]
-    out_specs = [vmem, smem]
+    out_shape = [jax.ShapeDtypeStruct((OB, TILE, TILE), jnp.float32), jax.ShapeDtypeStruct((1,) if last else (8, TILE), jnp.int32)]
+    out_specs = [vmem, smem if last else vmem]
     if last:
         out_shape.append(jax.ShapeDtypeStruct((TILE, OB * TILE), jnp.bfloat16))
         out_specs.append(vmem)
@@ -198,20 +200,20 @@
     return pl.pallas_call(
         functools.partial(task_kernel, phase, places, last),
         out_shape=out_shape,
-        in_specs=[smem, smem, vmem, vmem, smem] + [vmem] * len(pieces),
+        in_specs=[vmem] * (4 + len(pieces)),
         out_specs=out_specs,
         scratch_shapes=[
             pltpu.VMEM((OB + 1, TILE, TILE), jnp.float32),
-            pltpu.VMEM((len(pieces) * ROWS, TILE), jnp.bfloat16),
             pltpu.VMEM((8, TILE), jnp.int32),
             pltpu.SMEM((8, TILE), jnp.int32),
+            pltpu.SMEM(lists.shape, jnp.int32),
             pltpu.SMEM((tiles.shape[0] + 16,), jnp.int32),
-            pltpu.SemaphoreType.DMA((len(pieces) + 1,)),
+            pltpu.SemaphoreType.DMA((2,)),
         ],
         compiler_params=pltpu.CompilerParams(vmem_limit_bytes=24 << 20),
         cost_estimate=pl.CostEstimate(flops=n * 20 * TILE ** 3, bytes_accessed=8 << 20, transcendentals=0),
         name=f"tasks{phase}",
-    )(lists, counts, tiles, *acc_in, *pieces)
+    )(lists, tiles, *acc_in, *pieces)
 
 
 def prepare(own_tiles, own_k, own_out, own_live, help_tiles, help_k, help_out, help_live):
@@ -228,12 +230,11 @@
     return pl.pallas_call(
         prep_kernel,
         out_shape=(
-            jax.ShapeDtypeStruct((PHASES * (n + 8),), jnp.int32),
-            jax.ShapeDtypeStruct((PHASES,), jnp.int32),
+            jax.ShapeDtypeStruct((PHASES * (n + SCAN) + SCAN,), jnp.int32),
             pltpu.VMEM((n, TILE, TILE), jnp.bfloat16),
         ),
         in_specs=[hbm] * 9,
-        out_specs=(smem, smem, pl.BlockSpec(memory_space=pltpu.VMEM)),
+        out_specs=(smem, pl.BlockSpec(memory_space=pltpu.VMEM)),
         scratch_shapes=[pltpu.SemaphoreType.DMA((2 + len(scalars),))]
         + [pltpu.SMEM(v.shape, jnp.int32) for v in scalars],
         name="prep",
@@ -257,24 +258,26 @@
     kept = jnp.where(amp_kept != 0, amplitudes * amp_kept.astype(jnp.bfloat16), jnp.inf).astype(jnp.bfloat16)
     first = jnp.stack([kept] + [move(kept, zh=k) for k in (1, 2, 3)])
     head, tail = pack([first] + [move(first, zl=k) for k in (1, 2, 3)])
-    lists, counts, tiles = prepare(
+    lists, tiles = prepare(
         own_tiles, own_k, own_out, own_live, help_tiles, help_k, help_out, help_live)
-    tasks = functools.partial(run_tasks, lists=lists, counts=counts, tiles=tiles)
     ys = [move(head, y=k) for k in ORDER]
-    acc = (jnp.zeros((OB, TILE, TILE), jnp.float32), jnp.zeros((1,), jnp.int32))
-    acc = tasks(0, [head, move(head, c=1)], acc, False)
+    own_head, lists = lax.optimization_barrier((head, lists))
+    tasks = functools.partial(run_tasks, lists=lists, tiles=tiles)
+    acc = (jnp.zeros((OB, TILE, TILE), jnp.float32), jnp.zeros((8, TILE), jnp.int32))
+    acc = tasks(0, [head, move(own_head, c=1)], acc, False)
     ys[0], acc = lax.optimization_barrier((ys[0], acc))
     ys_c = [move(v, c=1) for v in ys]
-    acc = tasks(1, ys, acc, False)
-    total, over, out = tasks(2, ys_c, acc, True)
-
-    def second_round(tail, total, over, out):
+    acc_own = tasks(1, ys, acc, False)
+    total, over, out = tasks(2, ys_c, acc_own, True)
+
+    def second_round(tail, total, out):
         ys = [move(tail, y=k) for k in ORDER]
-        acc = tasks(0, [tail, move(tail, c=1)], (total, over), False, places=REST)
+        acc = (total, jnp.zeros((8, TILE), jnp.int32))
+        acc = tasks(0, [tail, move(tail, c=1)], acc, False, places=REST)
         acc = tasks(1, ys, acc, False, places=REST)
         return tasks(2, [move(v, c=1) for v in ys], acc, True, places=REST)[2]
 
-    return lax.cond(over[0] > 0, second_round, lambda tail, total, over, out: out, tail, total, over, out)
+    return lax.cond(over[0] > 0, second_round, lambda tail, total, out: out, tail, total, out)
 
 
 def solution(mesh):

time: 90.3 us -> 86.9 us (0.962)
  Pallas kernels: 14.1 us -> 9.18 us
    pallas_call x3, Pallas kernels: 9.5 us -> 4.45 us  [run_tasks(): pl.pallas_call(functools.partial(task_kernel, phase, places, last), out_s...]
  transfers between devices with their start and end apart: 13 -> 13, of which waited for: 4 -> 5; matrix products, arithmetic and copies ran while one was open for 1% -> 2% of each run, Pallas kernels for 10% -> 8%
where the time goes in v6:
time: 86.9 us; the launch traced here: 85.9 us
  starting transfers between devices  63.4 us (73%)
  waiting for transfers between devices  9.7 us (11%)
  Pallas kernels  9.18 us (11%)
  other arithmetic  2.07 us (2%)
  between operations  1.52 us (2%)
    ppermute x13, starting transfers between devices, move(): return lax.ppermute(x, 'col', pairs)  63.4 us
    ppermute x13, waiting for transfers between devices, move(): return lax.ppermute(x, 'col', pairs)  9.7 us
    pallas_call x3, Pallas kernels, run_tasks(): pl.pallas_call(functools.partial(task_kernel, phase, places, last), out_s...  4.45 us
    pallas_call x1, Pallas kernels, prepare(): pl.pallas_call(prep_kernel, out_shape=(jax.ShapeDtypeStruct((PHASES * (n...  3.91 us
  transfers between devices with their start and end apart: 13, of which 5 were waited for; matrix products, arithmetic and copies ran while one was open for 2% of the time, Pallas kernels for 8%

profile of v6, /device:TPU:1, one launch (start us, length us, event | category | flops | bytes accessed | tf_op | source)
XLA Modules:
  0.0 85.9 jit_solution(7616466529085237429)
XLA Ops:
  0.7 0.8 multiply_select_fusion
  1.4 9.6 %collective-permute-start.7 = (bf16[128,128]{1,0:T(8,128)(2,1)S(1)}, bf16[128,128]{1,0:T(8,128)(2,1)S(1)}, u32[]{:S(2)}, u32[]{:S(2)}) collective-permute-start(bf16[128,128]{1,0:T(8,128)(2,1)S(1)} %multiply_select_fusion), channel_id=1, source_target_pairs={{0,8},{1,9},{2,10},{3,11},{4,12},{5,13},{6,14},{7,15},{8,16},{9,17... | collective-permute-start | bytes 98312 | tf_op jit(solution)/shard_map/ppermute | solution.py:32
  11.1 15.4 %collective-permute-start.8 = (bf16[128,128]{1,0:T(8,128)(2,1)S(1)}, bf16[128,128]{1,0:T(8,128)(2,1)S(1)}, u32[]{:S(2)}, u32[]{:S(2)}) collective-permute-start(bf16[128,128]{1,0:T(8,128)(2,1)S(1)} %multiply_select_fusion), channel_id=1, source_target_pairs={{0,16},{1,17},{2,18},{3,19},{4,20},{5,21},{6,22},{7,23},{8,24},{9,... | collective-permute-start | bytes 98312 | tf_op jit(solution)/shard_map/ppermute | solution.py:32
  26.5 5.2 %collective-permute-start.9 = (bf16[128,128]{1,0:T(8,128)(2,1)S(1)}, bf16[128,128]{1,0:T(8,128)(2,1)S(1)}, u32[]{:S(2)}, u32[]{:S(2)}) collective-permute-start(bf16[128,128]{1,0:T(8,128)(2,1)S(1)} %multiply_select_fusion), channel_id=1, source_target_pairs={{0,24},{1,25},{2,26},{3,27},{4,28},{5,29},{6,30},{7,31},{8,0},{9,1... | collective-permute-start | bytes 98312 | tf_op jit(solution)/shard_map/ppermute | solution.py:32
  31.7 0.8 fusion.4
  32.5 0.0 collective-permute-done.7
  32.5 0.0 collective-permute-done.8
  32.5 2.6 %collective-permute-done.9 = bf16[128,128]{1,0:T(8,128)(2,1)S(1)} collective-permute-done((bf16[128,128]{1,0:T(8,128)(2,1)S(1)}, bf16[128,128]{1,0:T(8,128)(2,1)S(1)}, u32[]{:S(2)}, u32[]{:S(2)}) %collective-permute-start.9) | collective-permute-done | bytes 32800 | tf_op jit(solution)/shard_map/ppermute | solution.py:32
  35.1 3.6 %collective-permute-start.10 = (bf16[4,128,128]{2,1,0:T(8,128)(2,1)S(1)}, bf16[4,128,128]{2,1,0:T(8,128)(2,1)S(1)}, u32[]{:S(2)}, u32[]{:S(2)}) collective-permute-start(bf16[4,128,128]{2,1,0:T(8,128)(2,1)S(1)} %pad_maximum_fusion.refs_0_), channel_id=1, source_target_pairs={{0,2},{1,3},{2,4},{3,5},{4,6},{5,7},{6,0},{7,1},{8,10},{9,11},{10,... | collective-permute-start | bytes 393224 | tf_op jit(solution)/shard_map/ppermute | solution.py:32
  38.7 5.3 %collective-permute-start.11 = (bf16[4,128,128]{2,1,0:T(8,128)(2,1)S(1)}, bf16[4,128,128]{2,1,0:T(8,128)(2,1)S(1)}, u32[]{:S(2)}, u32[]{:S(2)}) collective-permute-start(bf16[4,128,128]{2,1,0:T(8,128)(2,1)S(1)} %pad_maximum_fusion.refs_0_), channel_id=1, source_target_pairs={{0,4},{1,5},{2,6},{3,7},{4,0},{5,1},{6,2},{7,3},{8,12},{9,13},{10,... | collective-permute-start | bytes 393224 | tf_op jit(solution)/shard_map/ppermute | solution.py:32
  44.0 2.6 %collective-permute-start.12 = (bf16[4,128,128]{2,1,0:T(8,128)(2,1)S(1)}, bf16[4,128,128]{2,1,0:T(8,128)(2,1)S(1)}, u32[]{:S(2)}, u32[]{:S(2)}) collective-permute-start(bf16[4,128,128]{2,1,0:T(8,128)(2,1)S(1)} %pad_maximum_fusion.refs_0_), channel_id=1, source_target_pairs={{0,6},{1,7},{2,0},{3,1},{4,2},{5,3},{6,4},{7,5},{8,14},{9,15},{10,... | collective-permute-start | bytes 393224 | tf_op jit(solution)/shard_map/ppermute | solution.py:32
  46.7 0.5 and_add_fusion.table
  47.2 3.9 %prep.1 = (s32[608]{0:T(1024)S(1)}, bf16[192,128,128]{2,1,0:T(8,128)(2,1)S(1)}) custom-call(s32[160]{0:T(256)} %own_k.1, s32[160]{0:T(256)} %own_out.1, s32[160]{0:T(256)} %own_live.1, s32[32]{0:T(128)} %help_k.1, s32[32]{0:T(128)} %help_out.1, s32[32]{0:T(128)} %help_live.1, s32[128]{0:T(128)} %and_add_fusion.table, bf16[160,128,128]{2,1,0:T(8,128)(2,1)} %own_tiles.1, ...), custom_call_target="tpu_custom_call" | custom-call | bytes 8388608 | tf_op jit(solution)/shard_map/prep/pallas_call | solution.py:230
  51.1 0.0 collective-permute-done.10.refs_1_
  51.1 0.0 collective-permute-done.11.refs_2_
  51.1 0.4 collective-permute-done.12.refs_3_
  51.5 0.8 pack.1
  52.3 4.6 %collective-permute-start.14 = (bf16[1296,128]{1,0:T(8,128)(2,1)S(1)}, bf16[1296,128]{1,0:T(8,128)(2,1)S(1)}, u32[]{:S(2)}, u32[]{:S(2)}) collective-permute-start(bf16[1296,128]{1,0:T(8,128)(2,1)S(1)} %get-tuple-element.46.rest_0_), channel_id=1, source_target_pairs={{0,1},{1,0},{2,3},{3,2},{4,5},{5,4},{6,7},{7,6},{8,9},{9,8},{10,11... | collective-permute-start | bytes 995336 | tf_op jit(solution)/shard_map/ppermute | solution.py:32
  56.9 4.8 %collective-permute-start.13 = (bf16[1296,128]{1,0:T(8,128)(2,1)S(1)}, bf16[1296,128]{1,0:T(8,128)(2,1)S(1)}, u32[]{:S(2)}, u32[]{:S(2)}) collective-permute-start(bf16[1296,128]{1,0:T(8,128)(2,1)S(1)} %get-tuple-element.46.rest_0_), channel_id=1, source_target_pairs={{0,64},{1,65},{2,66},{3,67},{4,68},{5,69},{6,70},{7,71},{8,72},{9,... | collective-permute-start | bytes 995336 | tf_op jit(solution)/shard_map/ppermute | solution.py:32
  61.7 2.3 %collective-permute-start.15 = (bf16[1296,128]{1,0:T(8,128)(2,1)S(1)}, bf16[1296,128]{1,0:T(8,128)(2,1)S(1)}, u32[]{:S(2)}, u32[]{:S(2)}) collective-permute-start(bf16[1296,128]{1,0:T(8,128)(2,1)S(1)} %get-tuple-element.46.rest_0_), channel_id=1, source_target_pairs={{0,32},{1,33},{2,34},{3,35},{4,36},{5,37},{6,38},{7,39},{8,40},{9,... | collective-permute-start | bytes 995336 | tf_op jit(solution)/shard_map/ppermute | solution.py:32
  64.0 2.3 %collective-permute-start.16 = (bf16[1296,128]{1,0:T(8,128)(2,1)S(1)}, bf16[1296,128]{1,0:T(8,128)(2,1)S(1)}, u32[]{:S(2)}, u32[]{:S(2)}) collective-permute-start(bf16[1296,128]{1,0:T(8,128)(2,1)S(1)} %get-tuple-element.46.rest_0_), channel_id=1, source_target_pairs={{0,96},{1,97},{2,98},{3,99},{4,100},{5,101},{6,102},{7,103},{8,104... | collective-permute-start | bytes 995336 | tf_op jit(solution)/shard_map/ppermute | solution.py:32
  66.3 0.0 collective-permute-done.14.rest_1_
  66.3 1.1 %tasks0.3 = (f32[4,128,128]{2,1,0:T(8,128)S(1)}, s32[8,128]{1,0:T(8,128)S(1)}) custom-call(s32[608]{0:T(1024)S(1)} %get-tuple-element.44.lists_v, bf16[192,128,128]{2,1,0:T(8,128)(2,1)S(1)} %get-tuple-element.45.tiles, f32[4,128,128]{2,1,0:T(8,128)S(1)} %broadcast_in_dim.28.acc_in, s32[8,128]{1,0:T(8,128)S(1)} %broadcast_6_over_in.2.over_in, ...), custom_call_target="tpu_custom_call" | custom-call | flops 2013265920 | bytes 8388608 | tf_op jit(solution)/shard_map/tasks0/pallas_call | solution.py:200
  67.4 2.3 %collective-permute-done.13.rest_0_ = bf16[1296,128]{1,0:T(8,128)(2,1)S(1)} collective-permute-done((bf16[1296,128]{1,0:T(8,128)(2,1)S(1)}, bf16[1296,128]{1,0:T(8,128)(2,1)S(1)}, u32[]{:S(2)}, u32[]{:S(2)}) %collective-permute-start.13) | collective-permute-done | bytes 331808 | tf_op jit(solution)/shard_map/ppermute | solution.py:32
  69.7 3.1 %collective-permute-start.17 = (bf16[1296,128]{1,0:T(8,128)(2,1)S(1)}, bf16[1296,128]{1,0:T(8,128)(2,1)S(1)}, u32[]{:S(2)}, u32[]{:S(2)}) collective-permute-start(bf16[1296,128]{1,0:T(8,128)(2,1)S(1)} %collective-permute-done.13.rest_0_), channel_id=1, source_target_pairs={{0,1},{1,0},{2,3},{3,2},{4,5},{5,4},{6,7},{7,6},{8,9},{9,8},{10,11... | collective-permute-start | bytes 995336 | tf_op jit(solution)/shard_map/ppermute | solution.py:32
  72.8 4.3 %collective-permute-done.15.rest_1_ = bf16[1296,128]{1,0:T(8,128)(2,1)S(1)} collective-permute-done((bf16[1296,128]{1,0:T(8,128)(2,1)S(1)}, bf16[1296,128]{1,0:T(8,128)(2,1)S(1)}, u32[]{:S(2)}, u32[]{:S(2)}) %collective-permute-start.15) | collective-permute-done | bytes 331808 | tf_op jit(solution)/shard_map/ppermute | solution.py:32
  77.1 2.7 %collective-permute-start.18 = (bf16[1296,128]{1,0:T(8,128)(2,1)S(1)}, bf16[1296,128]{1,0:T(8,128)(2,1)S(1)}, u32[]{:S(2)}, u32[]{:S(2)}) collective-permute-start(bf16[1296,128]{1,0:T(8,128)(2,1)S(1)} %collective-permute-done.15.rest_1_), channel_id=1, source_target_pairs={{0,1},{1,0},{2,3},{3,2},{4,5},{5,4},{6,7},{7,6},{8,9},{9,8},{10,11... | collective-permute-start | bytes 995336 | tf_op jit(solution)/shard_map/ppermute | solution.py:32
  79.8 1.9 %collective-permute-start.19 = (bf16[1296,128]{1,0:T(8,128)(2,1)S(1)}, bf16[1296,128]{1,0:T(8,128)(2,1)S(1)}, u32[]{:S(2)}, u32[]{:S(2)}) collective-permute-start(bf16[1296,128]{1,0:T(8,128)(2,1)S(1)} %collective-permute-done.16.rest_2_), channel_id=1, source_target_pairs={{0,1},{1,0},{2,3},{3,2},{4,5},{5,4},{6,7},{7,6},{8,9},{9,8},{10,11... | collective-permute-start | bytes 995336 | tf_op jit(solution)/shard_map/ppermute | solution.py:32
  81.8 1.5 %tasks1.3 = (f32[4,128,128]{2,1,0:T(8,128)S(1)}, s32[8,128]{1,0:T(8,128)S(1)}) custom-call(s32[608]{0:T(1024)S(1)} %get-tuple-element.44.lists_v, bf16[192,128,128]{2,1,0:T(8,128)(2,1)S(1)} %get-tuple-element.45.tiles, f32[4,128,128]{2,1,0:T(8,128)S(1)} %get-tuple-element.49.acc_in, s32[8,128]{1,0:T(8,128)S(1)} %get-tuple-element.50.over_in, ...), custom_call_target="tpu_custom_call" | custom-call | flops 3019898880 | bytes 8388608 | tf_op jit(solution)/shard_map/tasks1/pallas_call | solution.py:200
  83.3 0.0 collective-permute-done.17.rest_0_
  83.3 0.1 collective-permute-done.19.rest_2_
  83.4 1.9 %tasks2.3 = (f32[4,128,128]{2,1,0:T(8,128)S(1)}, s32[1]{0:T(128)}, bf16[128,512]{1,0:T(8,128)(2,1)}) custom-call(s32[608]{0:T(1024)S(1)} %get-tuple-element.44.lists_v, bf16[192,128,128]{2,1,0:T(8,128)(2,1)S(1)} %get-tuple-element.45.tiles, f32[4,128,128]{2,1,0:T(8,128)S(1)} %get-tuple-element.52.acc_in, s32[8,128]{1,0:T(8,128)S(1)} %get-tuple-element.53.over_in, ...), custom_call_target="tpu_custom_call" | custom-call | flops 3019898880 | bytes 8388608 | tf_op jit(solution)/shard_map/tasks2/pallas_call | solution.py:200
  (6 shorter events, 0.1 us)
Async XLA Ops:
  1.4 31.1 %collective-permute-start.7 = (bf16[128,128]{1,0:T(8,128)(2,1)S(1)}, bf16[128,128]{1,0:T(8,128)(2,1)S(1)}, u32[]{:S(2)}, u32[]{:S(2)}) collective-permute-start(bf16[128,128]{1,0:T(8,128)(2,1)S(1)} %multiply_select_fusion), channel_id=1, source_target_pairs={{0,8},{1,9},{2,10},{3,11},{4,12},{5,13},{6,14},{7,15},{8,16},{9,17... | collective-permute-start | bytes 98312 | tf_op jit(solution)/shard_map/ppermute | solution.py:32
  11.1 21.4 %collective-permute-start.8 = (bf16[128,128]{1,0:T(8,128)(2,1)S(1)}, bf16[128,128]{1,0:T(8,128)(2,1)S(1)}, u32[]{:S(2)}, u32[]{:S(2)}) collective-permute-start(bf16[128,128]{1,0:T(8,128)(2,1)S(1)} %multiply_select_fusion), channel_id=1, source_target_pairs={{0,16},{1,17},{2,18},{3,19},{4,20},{5,21},{6,22},{7,23},{8,24},{9,... | collective-permute-start | bytes 98312 | tf_op jit(solution)/shard_map/ppermute | solution.py:32
  26.5 8.6 %collective-permute-start.9 = (bf16[128,128]{1,0:T(8,128)(2,1)S(1)}, bf16[128,128]{1,0:T(8,128)(2,1)S(1)}, u32[]{:S(2)}, u32[]{:S(2)}) collective-permute-start(bf16[128,128]{1,0:T(8,128)(2,1)S(1)} %multiply_select_fusion), channel_id=1, source_target_pairs={{0,24},{1,25},{2,26},{3,27},{4,28},{5,29},{6,30},{7,31},{8,0},{9,1... | collective-permute-start | bytes 98312 | tf_op jit(solution)/shard_map/ppermute | solution.py:32
  35.1 16.0 %collective-permute-start.10 = (bf16[4,128,128]{2,1,0:T(8,128)(2,1)S(1)}, bf16[4,128,128]{2,1,0:T(8,128)(2,1)S(1)}, u32[]{:S(2)}, u32[]{:S(2)}) collective-permute-start(bf16[4,128,128]{2,1,0:T(8,128)(2,1)S(1)} %pad_maximum_fusion.refs_0_), channel_id=1, source_target_pairs={{0,2},{1,3},{2,4},{3,5},{4,6},{5,7},{6,0},{7,1},{8,10},{9,11},{10,... | collective-permute-start | bytes 393224 | tf_op jit(solution)/shard_map/ppermute | solution.py:32
  38.7 12.4 %collective-permute-start.11 = (bf16[4,128,128]{2,1,0:T(8,128)(2,1)S(1)}, bf16[4,128,128]{2,1,0:T(8,128)(2,1)S(1)}, u32[]{:S(2)}, u32[]{:S(2)}) collective-permute-start(bf16[4,128,128]{2,1,0:T(8,128)(2,1)S(1)} %pad_maximum_fusion.refs_0_), channel_id=1, source_target_pairs={{0,4},{1,5},{2,6},{3,7},{4,0},{5,1},{6,2},{7,3},{8,12},{9,13},{10,... | collective-permute-start | bytes 393224 | tf_op jit(solution)/shard_map/ppermute | solution.py:32
  44.0 7.5 %collective-permute-start.12 = (bf16[4,128,128]{2,1,0:T(8,128)(2,1)S(1)}, bf16[4,128,128]{2,1,0:T(8,128)(2,1)S(1)}, u32[]{:S(2)}, u32[]{:S(2)}) collective-permute-start(bf16[4,128,128]{2,1,0:T(8,128)(2,1)S(1)} %pad_maximum_fusion.refs_0_), channel_id=1, source_target_pairs={{0,6},{1,7},{2,0},{3,1},{4,2},{5,3},{6,4},{7,5},{8,14},{9,15},{10,... | collective-permute-start | bytes 393224 | tf_op jit(solution)/shard_map/ppermute | solution.py:32
  52.3 13.9 %collective-permute-start.14 = (bf16[1296,128]{1,0:T(8,128)(2,1)S(1)}, bf16[1296,128]{1,0:T(8,128)(2,1)S(1)}, u32[]{:S(2)}, u32[]{:S(2)}) collective-permute-start(bf16[1296,128]{1,0:T(8,128)(2,1)S(1)} %get-tuple-element.46.rest_0_), channel_id=1, source_target_pairs={{0,1},{1,0},{2,3},{3,2},{4,5},{5,4},{6,7},{7,6},{8,9},{9,8},{10,11... | collective-permute-start | bytes 995336 | tf_op jit(solution)/shard_map/ppermute | solution.py:32
  56.9 12.8 %collective-permute-start.13 = (bf16[1296,128]{1,0:T(8,128)(2,1)S(1)}, bf16[1296,128]{1,0:T(8,128)(2,1)S(1)}, u32[]{:S(2)}, u32[]{:S(2)}) collective-permute-start(bf16[1296,128]{1,0:T(8,128)(2,1)S(1)} %get-tuple-element.46.rest_0_), channel_id=1, source_target_pairs={{0,64},{1,65},{2,66},{3,67},{4,68},{5,69},{6,70},{7,71},{8,72},{9,... | collective-permute-start | bytes 995336 | tf_op jit(solution)/shard_map/ppermute | solution.py:32
  61.7 15.5 %collective-permute-start.15 = (bf16[1296,128]{1,0:T(8,128)(2,1)S(1)}, bf16[1296,128]{1,0:T(8,128)(2,1)S(1)}, u32[]{:S(2)}, u32[]{:S(2)}) collective-permute-start(bf16[1296,128]{1,0:T(8,128)(2,1)S(1)} %get-tuple-element.46.rest_0_), channel_id=1, source_target_pairs={{0,32},{1,33},{2,34},{3,35},{4,36},{5,37},{6,38},{7,39},{8,40},{9,... | collective-permute-start | bytes 995336 | tf_op jit(solution)/shard_map/ppermute | solution.py:32
  64.0 15.9 %collective-permute-start.16 = (bf16[1296,128]{1,0:T(8,128)(2,1)S(1)}, bf16[1296,128]{1,0:T(8,128)(2,1)S(1)}, u32[]{:S(2)}, u32[]{:S(2)}) collective-permute-start(bf16[1296,128]{1,0:T(8,128)(2,1)S(1)} %get-tuple-element.46.rest_0_), channel_id=1, source_target_pairs={{0,96},{1,97},{2,98},{3,99},{4,100},{5,101},{6,102},{7,103},{8,104... | collective-permute-start | bytes 995336 | tf_op jit(solution)/shard_map/ppermute | solution.py:32
  69.7 13.6 %collective-permute-start.17 = (bf16[1296,128]{1,0:T(8,128)(2,1)S(1)}, bf16[1296,128]{1,0:T(8,128)(2,1)S(1)}, u32[]{:S(2)}, u32[]{:S(2)}) collective-permute-start(bf16[1296,128]{1,0:T(8,128)(2,1)S(1)} %collective-permute-done.13.rest_0_), channel_id=1, source_target_pairs={{0,1},{1,0},{2,3},{3,2},{4,5},{5,4},{6,7},{7,6},{8,9},{9,8},{10,11... | collective-permute-start | bytes 995336 | tf_op jit(solution)/shard_map/ppermute | solution.py:32
  77.1 6.1 %collective-permute-start.18 = (bf16[1296,128]{1,0:T(8,128)(2,1)S(1)}, bf16[1296,128]{1,0:T(8,128)(2,1)S(1)}, u32[]{:S(2)}, u32[]{:S(2)}) collective-permute-start(bf16[1296,128]{1,0:T(8,128)(2,1)S(1)} %collective-permute-done.15.rest_1_), channel_id=1, source_target_pairs={{0,1},{1,0},{2,3},{3,2},{4,5},{5,4},{6,7},{7,6},{8,9},{9,8},{10,11... | collective-permute-start | bytes 995336 | tf_op jit(solution)/shard_map/ppermute | solution.py:32
  79.8 3.5 %collective-permute-start.19 = (bf16[1296,128]{1,0:T(8,128)(2,1)S(1)}, bf16[1296,128]{1,0:T(8,128)(2,1)S(1)}, u32[]{:S(2)}, u32[]{:S(2)}) collective-permute-start(bf16[1296,128]{1,0:T(8,128)(2,1)S(1)} %collective-permute-done.16.rest_2_), channel_id=1, source_target_pairs={{0,1},{1,0},{2,3},{3,2},{4,5},{5,4},{6,7},{7,6},{8,9},{9,8},{10,11... | collective-permute-start | bytes 995336 | tf_op jit(solution)/shard_map/ppermute | solution.py:32

commit v7 on v6

--- a/solution.py
+++ b/solution.py
@@ -19,7 +19,7 @@
 PACK = 10
 REST = LINE - PACK
 META = 16
-ORDER = (2, 1, 3)
+PLAN = (((0, 0), (0, 1), (2, 0)), ((1, 0), (3, 0), (2, 1)), ((1, 1), (3, 1)))
 ABSENT, LATER = 99, 50
 
 
@@ -220,9 +220,11 @@
     me, k = lax.axis_index("col"), jnp.arange(COLS, dtype=jnp.int32)
     c, y = (me ^ k) & 1, (me ^ k) >> 5
     zl, zh = ((me >> 1) - (k >> 1)) & 3, ((me >> 3) - (k >> 3)) & 3
-    rank = sum(jnp.where(y == k, j, 0) for j, k in enumerate(ORDER))
-    group = jnp.where(y == 0, c, (1 + c) * 4 + rank)
-    table = (group * NZL + zl) * NZH + zh
+    group = jnp.zeros_like(k)
+    for phase, places in enumerate(PLAN):
+        for j, (dy, dc) in enumerate(places):
+            group = jnp.where((y == dy) & (c == dc), phase * 4 + j, group)
+    table = (group * NZL + zl) * NZH + ((zh & 1) << 1 | zh >> 1)
     n = own_k.shape[0] + help_k.shape[0]
     smem = pl.BlockSpec(memory_space=pltpu.SMEM)
     hbm = pl.BlockSpec(memory_space=pltpu.HBM)
@@ -256,26 +258,30 @@
     help_live,
 ):
     kept = jnp.where(amp_kept != 0, amplitudes * amp_kept.astype(jnp.bfloat16), jnp.inf).astype(jnp.bfloat16)
-    first = jnp.stack([kept] + [move(kept, zh=k) for k in (1, 2, 3)])
+    first = jnp.stack([kept] + [move(kept, zh=k) for k in (2, 1, 3)])
     head, tail = pack([first] + [move(first, zl=k) for k in (1, 2, 3)])
     lists, tiles = prepare(
         own_tiles, own_k, own_out, own_live, help_tiles, help_k, help_out, help_live)
-    ys = [move(head, y=k) for k in ORDER]
-    own_head, lists = lax.optimization_barrier((head, lists))
+    acc = (jnp.zeros((OB, TILE, TILE), jnp.float32), jnp.zeros((8, TILE), jnp.int32))
+    ys = {k: move(head, y=k) for k in (2, 1, 3)}
+    head_for_c, lists = lax.optimization_barrier((head, lists))
+    head_c = move(head_for_c, c=1)
     tasks = functools.partial(run_tasks, lists=lists, tiles=tiles)
-    acc = (jnp.zeros((OB, TILE, TILE), jnp.float32), jnp.zeros((8, TILE), jnp.int32))
-    acc = tasks(0, [head, move(own_head, c=1)], acc, False)
-    ys[0], acc = lax.optimization_barrier((ys[0], acc))
-    ys_c = [move(v, c=1) for v in ys]
-    acc_own = tasks(1, ys, acc, False)
-    total, over, out = tasks(2, ys_c, acc_own, True)
+    ys[2], own_head = lax.optimization_barrier((ys[2], head))
+    y2c = move(ys[2], c=1)
+    acc = tasks(0, [own_head, head_c, ys[2]], acc, False)
+    ys[1], acc = lax.optimization_barrier((ys[1], acc))
+    y1c, y3c = move(ys[1], c=1), move(ys[3], c=1)
+    acc = tasks(1, [ys[1], ys[3], y2c], acc, False)
+    total, over, out = tasks(2, [y1c, y3c], acc, True)
 
     def second_round(tail, total, out):
-        ys = [move(tail, y=k) for k in ORDER]
         acc = (total, jnp.zeros((8, TILE), jnp.int32))
-        acc = tasks(0, [tail, move(tail, c=1)], acc, False, places=REST)
-        acc = tasks(1, ys, acc, False, places=REST)
-        return tasks(2, [move(v, c=1) for v in ys], acc, True, places=REST)[2]
+        parts = {(k, 0): move(tail, y=k) if k else tail for k in range(NY)}
+        parts.update({(k, 1): move(parts[k, 0], c=1) for k in range(NY)})
+        for phase, places in enumerate(PLAN):
+            acc = tasks(phase, [parts[v] for v in places], acc, phase == 2, places=REST)
+        return acc[2]
 
     return lax.cond(over[0] > 0, second_round, lambda tail, total, out: out, tail, total, out)
 

time: 86.9 us -> 86.3 us (level)
  waiting for transfers between devices: 9.7 us -> 4.88 us
  starting transfers between devices: 63.4 us -> 67.5 us
    ppermute x13, waiting for transfers between devices: 9.7 us -> 4.88 us  [move(): return lax.ppermute(x, 'col', pairs)]
    ppermute x13, starting transfers between devices: 63.4 us -> 67.5 us  [move(): return lax.ppermute(x, 'col', pairs)]
  transfers between devices with their start and end apart: 13 -> 13, of which waited for: 5 -> 4; matrix products, arithmetic and copies ran while one was open for 2% -> 2% of each run, Pallas kernels for 8% -> 8%
where the time goes in v7:
time: 86.3 us; the launch traced here: 85.1 us
  starting transfers between devices  67.5 us (78%)
  Pallas kernels  9.13 us (11%)
  waiting for transfers between devices  4.88 us (6%)
  other arithmetic  2.08 us (2%)
  between operations  1.51 us (2%)
    ppermute x13, starting transfers between devices, move(): return lax.ppermute(x, 'col', pairs)  67.5 us
    ppermute x13, waiting for transfers between devices, move(): return lax.ppermute(x, 'col', pairs)  4.88 us
    pallas_call x3, Pallas kernels, run_tasks(): pl.pallas_call(functools.partial(task_kernel, phase, places, last), out_s...  4.39 us
    pallas_call x1, Pallas kernels, prepare(): pl.pallas_call(prep_kernel, out_shape=(jax.ShapeDtypeStruct((PHASES * (n...  3.91 us
  transfers between devices with their start and end apart: 13, of which 4 were waited for; matrix products, arithmetic and copies ran while one was open for 2% of the time, Pallas kernels for 8%

profile of v7, /device:TPU:1, one launch (start us, length us, event | category | flops | bytes accessed | tf_op | source)
XLA Modules:
  0.0 85.1 jit_solution(7222781969436018162)
XLA Ops:
  0.7 0.8 multiply_select_fusion
  1.4 16.3 %collective-permute-start.7 = (bf16[128,128]{1,0:T(8,128)(2,1)S(1)}, bf16[128,128]{1,0:T(8,128)(2,1)S(1)}, u32[]{:S(2)}, u32[]{:S(2)}) collective-permute-start(bf16[128,128]{1,0:T(8,128)(2,1)S(1)} %multiply_select_fusion), channel_id=1, source_target_pairs={{0,16},{1,17},{2,18},{3,19},{4,20},{5,21},{6,22},{7,23},{8,24},{9,... | collective-permute-start | bytes 98312 | tf_op jit(solution)/shard_map/ppermute | solution.py:32
  17.7 8.8 %collective-permute-start.8 = (bf16[128,128]{1,0:T(8,128)(2,1)S(1)}, bf16[128,128]{1,0:T(8,128)(2,1)S(1)}, u32[]{:S(2)}, u32[]{:S(2)}) collective-permute-start(bf16[128,128]{1,0:T(8,128)(2,1)S(1)} %multiply_select_fusion), channel_id=1, source_target_pairs={{0,8},{1,9},{2,10},{3,11},{4,12},{5,13},{6,14},{7,15},{8,16},{9,17... | collective-permute-start | bytes 98312 | tf_op jit(solution)/shard_map/ppermute | solution.py:32
  26.5 10.0 %collective-permute-start.9 = (bf16[128,128]{1,0:T(8,128)(2,1)S(1)}, bf16[128,128]{1,0:T(8,128)(2,1)S(1)}, u32[]{:S(2)}, u32[]{:S(2)}) collective-permute-start(bf16[128,128]{1,0:T(8,128)(2,1)S(1)} %multiply_select_fusion), channel_id=1, source_target_pairs={{0,24},{1,25},{2,26},{3,27},{4,28},{5,29},{6,30},{7,31},{8,0},{9,1... | collective-permute-start | bytes 98312 | tf_op jit(solution)/shard_map/ppermute | solution.py:32
  36.5 0.8 fusion
  37.3 0.0 collective-permute-done.7
  37.3 0.0 collective-permute-done.8
  37.3 0.2 collective-permute-done.9
  37.5 3.5 %collective-permute-start.10 = (bf16[4,128,128]{2,1,0:T(8,128)(2,1)S(1)}, bf16[4,128,128]{2,1,0:T(8,128)(2,1)S(1)}, u32[]{:S(2)}, u32[]{:S(2)}) collective-permute-start(bf16[4,128,128]{2,1,0:T(8,128)(2,1)S(1)} %pad_maximum_fusion.refs_0_), channel_id=1, source_target_pairs={{0,2},{1,3},{2,4},{3,5},{4,6},{5,7},{6,0},{7,1},{8,10},{9,11},{10,... | collective-permute-start | bytes 393224 | tf_op jit(solution)/shard_map/ppermute | solution.py:32
  41.1 5.3 %collective-permute-start.11 = (bf16[4,128,128]{2,1,0:T(8,128)(2,1)S(1)}, bf16[4,128,128]{2,1,0:T(8,128)(2,1)S(1)}, u32[]{:S(2)}, u32[]{:S(2)}) collective-permute-start(bf16[4,128,128]{2,1,0:T(8,128)(2,1)S(1)} %pad_maximum_fusion.refs_0_), channel_id=1, source_target_pairs={{0,4},{1,5},{2,6},{3,7},{4,0},{5,1},{6,2},{7,3},{8,12},{9,13},{10,... | collective-permute-start | bytes 393224 | tf_op jit(solution)/shard_map/ppermute | solution.py:32
  46.4 2.3 %collective-permute-start.12 = (bf16[4,128,128]{2,1,0:T(8,128)(2,1)S(1)}, bf16[4,128,128]{2,1,0:T(8,128)(2,1)S(1)}, u32[]{:S(2)}, u32[]{:S(2)}) collective-permute-start(bf16[4,128,128]{2,1,0:T(8,128)(2,1)S(1)} %pad_maximum_fusion.refs_0_), channel_id=1, source_target_pairs={{0,6},{1,7},{2,0},{3,1},{4,2},{5,3},{6,4},{7,5},{8,14},{9,15},{10,... | collective-permute-start | bytes 393224 | tf_op jit(solution)/shard_map/ppermute | solution.py:32
  48.6 0.5 or_add_fusion.table
  49.2 3.9 %prep.1 = (s32[608]{0:T(1024)S(1)}, bf16[192,128,128]{2,1,0:T(8,128)(2,1)S(1)}) custom-call(s32[160]{0:T(256)} %own_k.1, s32[160]{0:T(256)} %own_out.1, s32[160]{0:T(256)} %own_live.1, s32[32]{0:T(128)} %help_k.1, s32[32]{0:T(128)} %help_out.1, s32[32]{0:T(128)} %help_live.1, s32[128]{0:T(128)} %or_add_fusion.table, bf16[160,128,128]{2,1,0:T(8,128)(2,1)} %own_tiles.1, ...), custom_call_target="tpu_custom_call" | custom-call | bytes 8388608 | tf_op jit(solution)/shard_map/prep/pallas_call | solution.py:232
  53.1 1.1 %collective-permute-done.11.refs_2_ = bf16[4,128,128]{2,1,0:T(8,128)(2,1)S(1)} collective-permute-done((bf16[4,128,128]{2,1,0:T(8,128)(2,1)S(1)}, bf16[4,128,128]{2,1,0:T(8,128)(2,1)S(1)}, u32[]{:S(2)}, u32[]{:S(2)}) %collective-permute-start.11) | collective-permute-done | bytes 131104 | tf_op jit(solution)/shard_map/ppermute | solution.py:32
  54.2 0.0 collective-permute-done.12.refs_3_
  54.2 0.8 pack.1
  55.1 4.7 %collective-permute-start.14 = (bf16[1296,128]{1,0:T(8,128)(2,1)S(1)}, bf16[1296,128]{1,0:T(8,128)(2,1)S(1)}, u32[]{:S(2)}, u32[]{:S(2)}) collective-permute-start(bf16[1296,128]{1,0:T(8,128)(2,1)S(1)} %get-tuple-element.49.rest_0_), channel_id=1, source_target_pairs={{0,64},{1,65},{2,66},{3,67},{4,68},{5,69},{6,70},{7,71},{8,72},{9,... | collective-permute-start | bytes 995336 | tf_op jit(solution)/shard_map/ppermute | solution.py:32
  59.8 4.2 %collective-permute-start.15 = (bf16[1296,128]{1,0:T(8,128)(2,1)S(1)}, bf16[1296,128]{1,0:T(8,128)(2,1)S(1)}, u32[]{:S(2)}, u32[]{:S(2)}) collective-permute-start(bf16[1296,128]{1,0:T(8,128)(2,1)S(1)} %get-tuple-element.49.rest_0_), channel_id=1, source_target_pairs={{0,1},{1,0},{2,3},{3,2},{4,5},{5,4},{6,7},{7,6},{8,9},{9,8},{10,11... | collective-permute-start | bytes 995336 | tf_op jit(solution)/shard_map/ppermute | solution.py:32
  63.9 2.3 %collective-permute-start.13 = (bf16[1296,128]{1,0:T(8,128)(2,1)S(1)}, bf16[1296,128]{1,0:T(8,128)(2,1)S(1)}, u32[]{:S(2)}, u32[]{:S(2)}) collective-permute-start(bf16[1296,128]{1,0:T(8,128)(2,1)S(1)} %get-tuple-element.49.rest_0_), channel_id=1, source_target_pairs={{0,32},{1,33},{2,34},{3,35},{4,36},{5,37},{6,38},{7,39},{8,40},{9,... | collective-permute-start | bytes 995336 | tf_op jit(solution)/shard_map/ppermute | solution.py:32
  66.2 2.3 %collective-permute-start.16 = (bf16[1296,128]{1,0:T(8,128)(2,1)S(1)}, bf16[1296,128]{1,0:T(8,128)(2,1)S(1)}, u32[]{:S(2)}, u32[]{:S(2)}) collective-permute-start(bf16[1296,128]{1,0:T(8,128)(2,1)S(1)} %get-tuple-element.49.rest_0_), channel_id=1, source_target_pairs={{0,96},{1,97},{2,98},{3,99},{4,100},{5,101},{6,102},{7,103},{8,104... | collective-permute-start | bytes 995336 | tf_op jit(solution)/shard_map/ppermute | solution.py:32
  68.5 0.0 collective-permute-done.14.rest_2_
  68.5 2.2 %collective-permute-start.17 = (bf16[1296,128]{1,0:T(8,128)(2,1)S(1)}, bf16[1296,128]{1,0:T(8,128)(2,1)S(1)}, u32[]{:S(2)}, u32[]{:S(2)}) collective-permute-start(bf16[1296,128]{1,0:T(8,128)(2,1)S(1)} %collective-permute-done.14.rest_2_), channel_id=1, source_target_pairs={{0,1},{1,0},{2,3},{3,2},{4,5},{5,4},{6,7},{7,6},{8,9},{9,8},{10,11... | collective-permute-start | bytes 995336 | tf_op jit(solution)/shard_map/ppermute | solution.py:32
  70.8 1.4 %tasks0.3 = (f32[4,128,128]{2,1,0:T(8,128)S(1)}, s32[8,128]{1,0:T(8,128)S(1)}) custom-call(s32[608]{0:T(1024)S(1)} %get-tuple-element.46.lists_v, bf16[192,128,128]{2,1,0:T(8,128)(2,1)S(1)} %get-tuple-element.47.tiles, f32[4,128,128]{2,1,0:T(8,128)S(1)} %broadcast_in_dim.41.acc_in, s32[8,128]{1,0:T(8,128)S(1)} %broadcast_8_over_in.2.over_in, ...), custom_call_target="tpu_custom_call" | custom-call | flops 3019898880 | bytes 8388608 | tf_op jit(solution)/shard_map/tasks0/pallas_call | solution.py:200
  72.2 3.0 %collective-permute-done.13.rest_0_ = bf16[1296,128]{1,0:T(8,128)(2,1)S(1)} collective-permute-done((bf16[1296,128]{1,0:T(8,128)(2,1)S(1)}, bf16[1296,128]{1,0:T(8,128)(2,1)S(1)}, u32[]{:S(2)}, u32[]{:S(2)}) %collective-permute-start.13) | collective-permute-done | bytes 331808 | tf_op jit(solution)/shard_map/ppermute | solution.py:32
  75.2 2.7 %collective-permute-start.18 = (bf16[1296,128]{1,0:T(8,128)(2,1)S(1)}, bf16[1296,128]{1,0:T(8,128)(2,1)S(1)}, u32[]{:S(2)}, u32[]{:S(2)}) collective-permute-start(bf16[1296,128]{1,0:T(8,128)(2,1)S(1)} %collective-permute-done.13.rest_0_), channel_id=1, source_target_pairs={{0,1},{1,0},{2,3},{3,2},{4,5},{5,4},{6,7},{7,6},{8,9},{9,8},{10,11... | collective-permute-start | bytes 995336 | tf_op jit(solution)/shard_map/ppermute | solution.py:32
  77.9 0.5 collective-permute-done.16.rest_1_
  78.4 3.0 %collective-permute-start.19 = (bf16[1296,128]{1,0:T(8,128)(2,1)S(1)}, bf16[1296,128]{1,0:T(8,128)(2,1)S(1)}, u32[]{:S(2)}, u32[]{:S(2)}) collective-permute-start(bf16[1296,128]{1,0:T(8,128)(2,1)S(1)} %collective-permute-done.16.rest_1_), channel_id=1, source_target_pairs={{0,1},{1,0},{2,3},{3,2},{4,5},{5,4},{6,7},{7,6},{8,9},{9,8},{10,11... | collective-permute-start | bytes 995336 | tf_op jit(solution)/shard_map/ppermute | solution.py:32
  81.5 0.0 collective-permute-done.17.rest_2_
  81.5 1.2 %tasks1.3 = (f32[4,128,128]{2,1,0:T(8,128)S(1)}, s32[8,128]{1,0:T(8,128)S(1)}) custom-call(s32[608]{0:T(1024)S(1)} %get-tuple-element.46.lists_v, bf16[192,128,128]{2,1,0:T(8,128)(2,1)S(1)} %get-tuple-element.47.tiles, f32[4,128,128]{2,1,0:T(8,128)S(1)} %get-tuple-element.53.acc_in, s32[8,128]{1,0:T(8,128)S(1)} %get-tuple-element.54.over_in, ...), custom_call_target="tpu_custom_call" | custom-call | flops 3019898880 | bytes 8388608 | tf_op jit(solution)/shard_map/tasks1/pallas_call | solution.py:200
  82.7 0.0 collective-permute-done.18.rest_0_
  82.7 0.0 collective-permute-done.19.rest_1_
  82.7 1.8 %tasks2.3 = (f32[4,128,128]{2,1,0:T(8,128)S(1)}, s32[1]{0:T(128)}, bf16[128,512]{1,0:T(8,128)(2,1)}) custom-call(s32[608]{0:T(1024)S(1)} %get-tuple-element.46.lists_v, bf16[192,128,128]{2,1,0:T(8,128)(2,1)S(1)} %get-tuple-element.47.tiles, f32[4,128,128]{2,1,0:T(8,128)S(1)} %get-tuple-element.56.acc_in, s32[8,128]{1,0:T(8,128)S(1)} %get-tuple-element.57.over_in, ...), custom_call_target="tpu_custom_call" | custom-call | flops 2013265920 | bytes 8388608 | tf_op jit(solution)/shard_map/tasks2/pallas_call | solution.py:200
  (6 shorter events, 0.1 us)
Async XLA Ops:
  1.4 35.9 %collective-permute-start.7 = (bf16[128,128]{1,0:T(8,128)(2,1)S(1)}, bf16[128,128]{1,0:T(8,128)(2,1)S(1)}, u32[]{:S(2)}, u32[]{:S(2)}) collective-permute-start(bf16[128,128]{1,0:T(8,128)(2,1)S(1)} %multiply_select_fusion), channel_id=1, source_target_pairs={{0,16},{1,17},{2,18},{3,19},{4,20},{5,21},{6,22},{7,23},{8,24},{9,... | collective-permute-start | bytes 98312 | tf_op jit(solution)/shard_map/ppermute | solution.py:32
  17.7 19.6 %collective-permute-start.8 = (bf16[128,128]{1,0:T(8,128)(2,1)S(1)}, bf16[128,128]{1,0:T(8,128)(2,1)S(1)}, u32[]{:S(2)}, u32[]{:S(2)}) collective-permute-start(bf16[128,128]{1,0:T(8,128)(2,1)S(1)} %multiply_select_fusion), channel_id=1, source_target_pairs={{0,8},{1,9},{2,10},{3,11},{4,12},{5,13},{6,14},{7,15},{8,16},{9,17... | collective-permute-start | bytes 98312 | tf_op jit(solution)/shard_map/ppermute | solution.py:32
  26.5 11.0 %collective-permute-start.9 = (bf16[128,128]{1,0:T(8,128)(2,1)S(1)}, bf16[128,128]{1,0:T(8,128)(2,1)S(1)}, u32[]{:S(2)}, u32[]{:S(2)}) collective-permute-start(bf16[128,128]{1,0:T(8,128)(2,1)S(1)} %multiply_select_fusion), channel_id=1, source_target_pairs={{0,24},{1,25},{2,26},{3,27},{4,28},{5,29},{6,30},{7,31},{8,0},{9,1... | collective-permute-start | bytes 98312 | tf_op jit(solution)/shard_map/ppermute | solution.py:32
  37.5 15.6 %collective-permute-start.10 = (bf16[4,128,128]{2,1,0:T(8,128)(2,1)S(1)}, bf16[4,128,128]{2,1,0:T(8,128)(2,1)S(1)}, u32[]{:S(2)}, u32[]{:S(2)}) collective-permute-start(bf16[4,128,128]{2,1,0:T(8,128)(2,1)S(1)} %pad_maximum_fusion.refs_0_), channel_id=1, source_target_pairs={{0,2},{1,3},{2,4},{3,5},{4,6},{5,7},{6,0},{7,1},{8,10},{9,11},{10,... | collective-permute-start | bytes 393224 | tf_op jit(solution)/shard_map/ppermute | solution.py:32
  41.1 13.1 %collective-permute-start.11 = (bf16[4,128,128]{2,1,0:T(8,128)(2,1)S(1)}, bf16[4,128,128]{2,1,0:T(8,128)(2,1)S(1)}, u32[]{:S(2)}, u32[]{:S(2)}) collective-permute-start(bf16[4,128,128]{2,1,0:T(8,128)(2,1)S(1)} %pad_maximum_fusion.refs_0_), channel_id=1, source_target_pairs={{0,4},{1,5},{2,6},{3,7},{4,0},{5,1},{6,2},{7,3},{8,12},{9,13},{10,... | collective-permute-start | bytes 393224 | tf_op jit(solution)/shard_map/ppermute | solution.py:32
  46.4 7.9 %collective-permute-start.12 = (bf16[4,128,128]{2,1,0:T(8,128)(2,1)S(1)}, bf16[4,128,128]{2,1,0:T(8,128)(2,1)S(1)}, u32[]{:S(2)}, u32[]{:S(2)}) collective-permute-start(bf16[4,128,128]{2,1,0:T(8,128)(2,1)S(1)} %pad_maximum_fusion.refs_0_), channel_id=1, source_target_pairs={{0,6},{1,7},{2,0},{3,1},{4,2},{5,3},{6,4},{7,5},{8,14},{9,15},{10,... | collective-permute-start | bytes 393224 | tf_op jit(solution)/shard_map/ppermute | solution.py:32
  55.1 13.5 %collective-permute-start.14 = (bf16[1296,128]{1,0:T(8,128)(2,1)S(1)}, bf16[1296,128]{1,0:T(8,128)(2,1)S(1)}, u32[]{:S(2)}, u32[]{:S(2)}) collective-permute-start(bf16[1296,128]{1,0:T(8,128)(2,1)S(1)} %get-tuple-element.49.rest_0_), channel_id=1, source_target_pairs={{0,64},{1,65},{2,66},{3,67},{4,68},{5,69},{6,70},{7,71},{8,72},{9,... | collective-permute-start | bytes 995336 | tf_op jit(solution)/shard_map/ppermute | solution.py:32
  59.8 11.0 %collective-permute-start.15 = (bf16[1296,128]{1,0:T(8,128)(2,1)S(1)}, bf16[1296,128]{1,0:T(8,128)(2,1)S(1)}, u32[]{:S(2)}, u32[]{:S(2)}) collective-permute-start(bf16[1296,128]{1,0:T(8,128)(2,1)S(1)} %get-tuple-element.49.rest_0_), channel_id=1, source_target_pairs={{0,1},{1,0},{2,3},{3,2},{4,5},{5,4},{6,7},{7,6},{8,9},{9,8},{10,11... | collective-permute-start | bytes 995336 | tf_op jit(solution)/shard_map/ppermute | solution.py:32
  63.9 11.3 %collective-permute-start.13 = (bf16[1296,128]{1,0:T(8,128)(2,1)S(1)}, bf16[1296,128]{1,0:T(8,128)(2,1)S(1)}, u32[]{:S(2)}, u32[]{:S(2)}) collective-permute-start(bf16[1296,128]{1,0:T(8,128)(2,1)S(1)} %get-tuple-element.49.rest_0_), channel_id=1, source_target_pairs={{0,32},{1,33},{2,34},{3,35},{4,36},{5,37},{6,38},{7,39},{8,40},{9,... | collective-permute-start | bytes 995336 | tf_op jit(solution)/shard_map/ppermute | solution.py:32
  66.2 12.2 %collective-permute-start.16 = (bf16[1296,128]{1,0:T(8,128)(2,1)S(1)}, bf16[1296,128]{1,0:T(8,128)(2,1)S(1)}, u32[]{:S(2)}, u32[]{:S(2)}) collective-permute-start(bf16[1296,128]{1,0:T(8,128)(2,1)S(1)} %get-tuple-element.49.rest_0_), channel_id=1, source_target_pairs={{0,96},{1,97},{2,98},{3,99},{4,100},{5,101},{6,102},{7,103},{8,104... | collective-permute-start | bytes 995336 | tf_op jit(solution)/shard_map/ppermute | solution.py:32
  68.5 12.9 %collective-permute-start.17 = (bf16[1296,128]{1,0:T(8,128)(2,1)S(1)}, bf16[1296,128]{1,0:T(8,128)(2,1)S(1)}, u32[]{:S(2)}, u32[]{:S(2)}) collective-permute-start(bf16[1296,128]{1,0:T(8,128)(2,1)S(1)} %collective-permute-done.14.rest_2_), channel_id=1, source_target_pairs={{0,1},{1,0},{2,3},{3,2},{4,5},{5,4},{6,7},{7,6},{8,9},{9,8},{10,11... | collective-permute-start | bytes 995336 | tf_op jit(solution)/shard_map/ppermute | solution.py:32
  75.2 7.4 %collective-permute-start.18 = (bf16[1296,128]{1,0:T(8,128)(2,1)S(1)}, bf16[1296,128]{1,0:T(8,128)(2,1)S(1)}, u32[]{:S(2)}, u32[]{:S(2)}) collective-permute-start(bf16[1296,128]{1,0:T(8,128)(2,1)S(1)} %collective-permute-done.13.rest_0_), channel_id=1, source_target_pairs={{0,1},{1,0},{2,3},{3,2},{4,5},{5,4},{6,7},{7,6},{8,9},{9,8},{10,11... | collective-permute-start | bytes 995336 | tf_op jit(solution)/shard_map/ppermute | solution.py:32
  78.4 4.3 %collective-permute-start.19 = (bf16[1296,128]{1,0:T(8,128)(2,1)S(1)}, bf16[1296,128]{1,0:T(8,128)(2,1)S(1)}, u32[]{:S(2)}, u32[]{:S(2)}) collective-permute-start(bf16[1296,128]{1,0:T(8,128)(2,1)S(1)} %collective-permute-done.16.rest_1_), channel_id=1, source_target_pairs={{0,1},{1,0},{2,3},{3,2},{4,5},{5,4},{6,7},{7,6},{8,9},{9,8},{10,11... | collective-permute-start | bytes 995336 | tf_op jit(solution)/shard_map/ppermute | solution.py:32

commit v8 on v7

--- a/solution.py
+++ b/solution.py
@@ -224,7 +224,7 @@
     for phase, places in enumerate(PLAN):
         for j, (dy, dc) in enumerate(places):
             group = jnp.where((y == dy) & (c == dc), phase * 4 + j, group)
-    table = (group * NZL + zl) * NZH + ((zh & 1) << 1 | zh >> 1)
+    table = (group * NZL + zl) * NZH + zh
     n = own_k.shape[0] + help_k.shape[0]
     smem = pl.BlockSpec(memory_space=pltpu.SMEM)
     hbm = pl.BlockSpec(memory_space=pltpu.HBM)
@@ -258,7 +258,7 @@
     help_live,
 ):
     kept = jnp.where(amp_kept != 0, amplitudes * amp_kept.astype(jnp.bfloat16), jnp.inf).astype(jnp.bfloat16)
-    first = jnp.stack([kept] + [move(kept, zh=k) for k in (2, 1, 3)])
+    first = jnp.stack([kept] + [move(kept, zh=k) for k in (1, 2, 3)])
     head, tail = pack([first] + [move(first, zl=k) for k in (1, 2, 3)])
     lists, tiles = prepare(
         own_tiles, own_k, own_out, own_live, help_tiles, help_k, help_out, help_live)

time: 86.3 us -> 85 us (0.985)
  starting transfers between devices: 67.5 us -> 63.9 us
  waiting for transfers between devices: 4.88 us -> 6.37 us
    ppermute x13, starting transfers between devices: 67.5 us -> 63.9 us  [move(): return lax.ppermute(x, 'col', pairs)]
    ppermute x13, waiting for transfers between devices: 4.88 us -> 6.37 us  [move(): return lax.ppermute(x, 'col', pairs)]
where the time goes in v8:
time: 85 us; the launch traced here: 83.5 us
  starting transfers between devices  63.9 us (75%)
  Pallas kernels  9.64 us (11%)
  waiting for transfers between devices  6.37 us (7%)
  other arithmetic  2.08 us (2%)
  between operations  1.52 us (2%)
    ppermute x13, starting transfers between devices, move(): return lax.ppermute(x, 'col', pairs)  63.9 us
    ppermute x13, waiting for transfers between devices, move(): return lax.ppermute(x, 'col', pairs)  6.37 us
    pallas_call x3, Pallas kernels, run_tasks(): pl.pallas_call(functools.partial(task_kernel, phase, places, last), out_s...  4.9 us
    pallas_call x1, Pallas kernels, prepare(): pl.pallas_call(prep_kernel, out_shape=(jax.ShapeDtypeStruct((PHASES * (n...  3.91 us
  transfers between devices with their start and end apart: 13, of which 4 were waited for; matrix products, arithmetic and copies ran while one was open for 2% of the time, Pallas kernels for 8%

profile of v8, /device:TPU:1, one launch (start us, length us, event | category | flops | bytes accessed | tf_op | source)
XLA Modules:
  0.0 83.5 jit_solution(14440813079765706821)
XLA Ops:
  0.7 0.8 multiply_select_fusion
  1.4 9.6 %collective-permute-start.7 = (bf16[128,128]{1,0:T(8,128)(2,1)S(1)}, bf16[128,128]{1,0:T(8,128)(2,1)S(1)}, u32[]{:S(2)}, u32[]{:S(2)}) collective-permute-start(bf16[128,128]{1,0:T(8,128)(2,1)S(1)} %multiply_select_fusion), channel_id=1, source_target_pairs={{0,8},{1,9},{2,10},{3,11},{4,12},{5,13},{6,14},{7,15},{8,16},{9,17... | collective-permute-start | bytes 98312 | tf_op jit(solution)/shard_map/ppermute | solution.py:32
  11.1 15.4 %collective-permute-start.8 = (bf16[128,128]{1,0:T(8,128)(2,1)S(1)}, bf16[128,128]{1,0:T(8,128)(2,1)S(1)}, u32[]{:S(2)}, u32[]{:S(2)}) collective-permute-start(bf16[128,128]{1,0:T(8,128)(2,1)S(1)} %multiply_select_fusion), channel_id=1, source_target_pairs={{0,16},{1,17},{2,18},{3,19},{4,20},{5,21},{6,22},{7,23},{8,24},{9,... | collective-permute-start | bytes 98312 | tf_op jit(solution)/shard_map/ppermute | solution.py:32
  26.5 5.2 %collective-permute-start.9 = (bf16[128,128]{1,0:T(8,128)(2,1)S(1)}, bf16[128,128]{1,0:T(8,128)(2,1)S(1)}, u32[]{:S(2)}, u32[]{:S(2)}) collective-permute-start(bf16[128,128]{1,0:T(8,128)(2,1)S(1)} %multiply_select_fusion), channel_id=1, source_target_pairs={{0,24},{1,25},{2,26},{3,27},{4,28},{5,29},{6,30},{7,31},{8,0},{9,1... | collective-permute-start | bytes 98312 | tf_op jit(solution)/shard_map/ppermute | solution.py:32
  31.7 0.8 fusion
  32.5 0.0 collective-permute-done.7
  32.5 0.0 collective-permute-done.8
  32.5 2.6 %collective-permute-done.9 = bf16[128,128]{1,0:T(8,128)(2,1)S(1)} collective-permute-done((bf16[128,128]{1,0:T(8,128)(2,1)S(1)}, bf16[128,128]{1,0:T(8,128)(2,1)S(1)}, u32[]{:S(2)}, u32[]{:S(2)}) %collective-permute-start.9) | collective-permute-done | bytes 32800 | tf_op jit(solution)/shard_map/ppermute | solution.py:32
  35.1 3.6 %collective-permute-start.10 = (bf16[4,128,128]{2,1,0:T(8,128)(2,1)S(1)}, bf16[4,128,128]{2,1,0:T(8,128)(2,1)S(1)}, u32[]{:S(2)}, u32[]{:S(2)}) collective-permute-start(bf16[4,128,128]{2,1,0:T(8,128)(2,1)S(1)} %pad_maximum_fusion.refs_0_), channel_id=1, source_target_pairs={{0,2},{1,3},{2,4},{3,5},{4,6},{5,7},{6,0},{7,1},{8,10},{9,11},{10,... | collective-permute-start | bytes 393224 | tf_op jit(solution)/shard_map/ppermute | solution.py:32
  38.7 5.3 %collective-permute-start.11 = (bf16[4,128,128]{2,1,0:T(8,128)(2,1)S(1)}, bf16[4,128,128]{2,1,0:T(8,128)(2,1)S(1)}, u32[]{:S(2)}, u32[]{:S(2)}) collective-permute-start(bf16[4,128,128]{2,1,0:T(8,128)(2,1)S(1)} %pad_maximum_fusion.refs_0_), channel_id=1, source_target_pairs={{0,4},{1,5},{2,6},{3,7},{4,0},{5,1},{6,2},{7,3},{8,12},{9,13},{10,... | collective-permute-start | bytes 393224 | tf_op jit(solution)/shard_map/ppermute | solution.py:32
  44.0 2.6 %collective-permute-start.12 = (bf16[4,128,128]{2,1,0:T(8,128)(2,1)S(1)}, bf16[4,128,128]{2,1,0:T(8,128)(2,1)S(1)}, u32[]{:S(2)}, u32[]{:S(2)}) collective-permute-start(bf16[4,128,128]{2,1,0:T(8,128)(2,1)S(1)} %pad_maximum_fusion.refs_0_), channel_id=1, source_target_pairs={{0,6},{1,7},{2,0},{3,1},{4,2},{5,3},{6,4},{7,5},{8,14},{9,15},{10,... | collective-permute-start | bytes 393224 | tf_op jit(solution)/shard_map/ppermute | solution.py:32
  46.7 0.5 and_add_fusion.table
  47.2 3.9 %prep.1 = (s32[608]{0:T(1024)S(1)}, bf16[192,128,128]{2,1,0:T(8,128)(2,1)S(1)}) custom-call(s32[160]{0:T(256)} %own_k.1, s32[160]{0:T(256)} %own_out.1, s32[160]{0:T(256)} %own_live.1, s32[32]{0:T(128)} %help_k.1, s32[32]{0:T(128)} %help_out.1, s32[32]{0:T(128)} %help_live.1, s32[128]{0:T(128)} %and_add_fusion.table, bf16[160,128,128]{2,1,0:T(8,128)(2,1)} %own_tiles.1, ...), custom_call_target="tpu_custom_call" | custom-call | bytes 8388608 | tf_op jit(solution)/shard_map/prep/pallas_call | solution.py:232
  51.1 0.0 collective-permute-done.10.refs_1_
  51.1 0.0 collective-permute-done.11.refs_2_
  51.1 0.4 collective-permute-done.12.refs_3_
  51.5 0.8 pack.1
  52.3 5.4 %collective-permute-start.14 = (bf16[1296,128]{1,0:T(8,128)(2,1)S(1)}, bf16[1296,128]{1,0:T(8,128)(2,1)S(1)}, u32[]{:S(2)}, u32[]{:S(2)}) collective-permute-start(bf16[1296,128]{1,0:T(8,128)(2,1)S(1)} %get-tuple-element.49.rest_0_), channel_id=1, source_target_pairs={{0,64},{1,65},{2,66},{3,67},{4,68},{5,69},{6,70},{7,71},{8,72},{9,... | collective-permute-start | bytes 995336 | tf_op jit(solution)/shard_map/ppermute | solution.py:32
  57.8 4.2 %collective-permute-start.15 = (bf16[1296,128]{1,0:T(8,128)(2,1)S(1)}, bf16[1296,128]{1,0:T(8,128)(2,1)S(1)}, u32[]{:S(2)}, u32[]{:S(2)}) collective-permute-start(bf16[1296,128]{1,0:T(8,128)(2,1)S(1)} %get-tuple-element.49.rest_0_), channel_id=1, source_target_pairs={{0,1},{1,0},{2,3},{3,2},{4,5},{5,4},{6,7},{7,6},{8,9},{9,8},{10,11... | collective-permute-start | bytes 995336 | tf_op jit(solution)/shard_map/ppermute | solution.py:32
  61.9 2.3 %collective-permute-start.13 = (bf16[1296,128]{1,0:T(8,128)(2,1)S(1)}, bf16[1296,128]{1,0:T(8,128)(2,1)S(1)}, u32[]{:S(2)}, u32[]{:S(2)}) collective-permute-start(bf16[1296,128]{1,0:T(8,128)(2,1)S(1)} %get-tuple-element.49.rest_0_), channel_id=1, source_target_pairs={{0,32},{1,33},{2,34},{3,35},{4,36},{5,37},{6,38},{7,39},{8,40},{9,... | collective-permute-start | bytes 995336 | tf_op jit(solution)/shard_map/ppermute | solution.py:32
  64.2 2.3 %collective-permute-start.16 = (bf16[1296,128]{1,0:T(8,128)(2,1)S(1)}, bf16[1296,128]{1,0:T(8,128)(2,1)S(1)}, u32[]{:S(2)}, u32[]{:S(2)}) collective-permute-start(bf16[1296,128]{1,0:T(8,128)(2,1)S(1)} %get-tuple-element.49.rest_0_), channel_id=1, source_target_pairs={{0,96},{1,97},{2,98},{3,99},{4,100},{5,101},{6,102},{7,103},{8,104... | collective-permute-start | bytes 995336 | tf_op jit(solution)/shard_map/ppermute | solution.py:32
  66.6 0.0 collective-permute-done.14.rest_2_
  66.6 2.2 %collective-permute-start.17 = (bf16[1296,128]{1,0:T(8,128)(2,1)S(1)}, bf16[1296,128]{1,0:T(8,128)(2,1)S(1)}, u32[]{:S(2)}, u32[]{:S(2)}) collective-permute-start(bf16[1296,128]{1,0:T(8,128)(2,1)S(1)} %collective-permute-done.14.rest_2_), channel_id=1, source_target_pairs={{0,1},{1,0},{2,3},{3,2},{4,5},{5,4},{6,7},{7,6},{8,9},{9,8},{10,11... | collective-permute-start | bytes 995336 | tf_op jit(solution)/shard_map/ppermute | solution.py:32
  68.8 0.0 collective-permute-done.15.rest_1_
  68.8 1.6 %tasks0.3 = (f32[4,128,128]{2,1,0:T(8,128)S(1)}, s32[8,128]{1,0:T(8,128)S(1)}) custom-call(s32[608]{0:T(1024)S(1)} %get-tuple-element.46.lists_v, bf16[192,128,128]{2,1,0:T(8,128)(2,1)S(1)} %get-tuple-element.47.tiles, f32[4,128,128]{2,1,0:T(8,128)S(1)} %broadcast_in_dim.41.acc_in, s32[8,128]{1,0:T(8,128)S(1)} %broadcast_8_over_in.2.over_in, ...), custom_call_target="tpu_custom_call" | custom-call | flops 3019898880 | bytes 8388608 | tf_op jit(solution)/shard_map/tasks0/pallas_call | solution.py:200
  70.4 2.9 %collective-permute-done.13.rest_0_ = bf16[1296,128]{1,0:T(8,128)(2,1)S(1)} collective-permute-done((bf16[1296,128]{1,0:T(8,128)(2,1)S(1)}, bf16[1296,128]{1,0:T(8,128)(2,1)S(1)}, u32[]{:S(2)}, u32[]{:S(2)}) %collective-permute-start.13) | collective-permute-done | bytes 331808 | tf_op jit(solution)/shard_map/ppermute | solution.py:32
  73.2 2.7 %collective-permute-start.18 = (bf16[1296,128]{1,0:T(8,128)(2,1)S(1)}, bf16[1296,128]{1,0:T(8,128)(2,1)S(1)}, u32[]{:S(2)}, u32[]{:S(2)}) collective-permute-start(bf16[1296,128]{1,0:T(8,128)(2,1)S(1)} %collective-permute-done.13.rest_0_), channel_id=1, source_target_pairs={{0,1},{1,0},{2,3},{3,2},{4,5},{5,4},{6,7},{7,6},{8,9},{9,8},{10,11... | collective-permute-start | bytes 995336 | tf_op jit(solution)/shard_map/ppermute | solution.py:32
  75.9 0.5 collective-permute-done.16.rest_1_
  76.5 3.0 %collective-permute-start.19 = (bf16[1296,128]{1,0:T(8,128)(2,1)S(1)}, bf16[1296,128]{1,0:T(8,128)(2,1)S(1)}, u32[]{:S(2)}, u32[]{:S(2)}) collective-permute-start(bf16[1296,128]{1,0:T(8,128)(2,1)S(1)} %collective-permute-done.16.rest_1_), channel_id=1, source_target_pairs={{0,1},{1,0},{2,3},{3,2},{4,5},{5,4},{6,7},{7,6},{8,9},{9,8},{10,11... | collective-permute-start | bytes 995336 | tf_op jit(solution)/shard_map/ppermute | solution.py:32
  79.5 1.5 %tasks1.3 = (f32[4,128,128]{2,1,0:T(8,128)S(1)}, s32[8,128]{1,0:T(8,128)S(1)}) custom-call(s32[608]{0:T(1024)S(1)} %get-tuple-element.46.lists_v, bf16[192,128,128]{2,1,0:T(8,128)(2,1)S(1)} %get-tuple-element.47.tiles, f32[4,128,128]{2,1,0:T(8,128)S(1)} %get-tuple-element.53.acc_in, s32[8,128]{1,0:T(8,128)S(1)} %get-tuple-element.54.over_in, ...), custom_call_target="tpu_custom_call" | custom-call | flops 3019898880 | bytes 8388608 | tf_op jit(solution)/shard_map/tasks1/pallas_call | solution.py:200
  81.0 0.0 collective-permute-done.19.rest_1_
  81.0 1.8 %tasks2.3 = (f32[4,128,128]{2,1,0:T(8,128)S(1)}, s32[1]{0:T(128)}, bf16[128,512]{1,0:T(8,128)(2,1)}) custom-call(s32[608]{0:T(1024)S(1)} %get-tuple-element.46.lists_v, bf16[192,128,128]{2,1,0:T(8,128)(2,1)S(1)} %get-tuple-element.47.tiles, f32[4,128,128]{2,1,0:T(8,128)S(1)} %get-tuple-element.56.acc_in, s32[8,128]{1,0:T(8,128)S(1)} %get-tuple-element.57.over_in, ...), custom_call_target="tpu_custom_call" | custom-call | flops 2013265920 | bytes 8388608 | tf_op jit(solution)/shard_map/tasks2/pallas_call | solution.py:200
  (6 shorter events, 0.1 us)
Async XLA Ops:
  1.4 31.1 %collective-permute-start.7 = (bf16[128,128]{1,0:T(8,128)(2,1)S(1)}, bf16[128,128]{1,0:T(8,128)(2,1)S(1)}, u32[]{:S(2)}, u32[]{:S(2)}) collective-permute-start(bf16[128,128]{1,0:T(8,128)(2,1)S(1)} %multiply_select_fusion), channel_id=1, source_target_pairs={{0,8},{1,9},{2,10},{3,11},{4,12},{5,13},{6,14},{7,15},{8,16},{9,17... | collective-permute-start | bytes 98312 | tf_op jit(solution)/shard_map/ppermute | solution.py:32
  11.1 21.4 %collective-permute-start.8 = (bf16[128,128]{1,0:T(8,128)(2,1)S(1)}, bf16[128,128]{1,0:T(8,128)(2,1)S(1)}, u32[]{:S(2)}, u32[]{:S(2)}) collective-permute-start(bf16[128,128]{1,0:T(8,128)(2,1)S(1)} %multiply_select_fusion), channel_id=1, source_target_pairs={{0,16},{1,17},{2,18},{3,19},{4,20},{5,21},{6,22},{7,23},{8,24},{9,... | collective-permute-start | bytes 98312 | tf_op jit(solution)/shard_map/ppermute | solution.py:32
  26.5 8.6 %collective-permute-start.9 = (bf16[128,128]{1,0:T(8,128)(2,1)S(1)}, bf16[128,128]{1,0:T(8,128)(2,1)S(1)}, u32[]{:S(2)}, u32[]{:S(2)}) collective-permute-start(bf16[128,128]{1,0:T(8,128)(2,1)S(1)} %multiply_select_fusion), channel_id=1, source_target_pairs={{0,24},{1,25},{2,26},{3,27},{4,28},{5,29},{6,30},{7,31},{8,0},{9,1... | collective-permute-start | bytes 98312 | tf_op jit(solution)/shard_map/ppermute | solution.py:32
  35.1 16.0 %collective-permute-start.10 = (bf16[4,128,128]{2,1,0:T(8,128)(2,1)S(1)}, bf16[4,128,128]{2,1,0:T(8,128)(2,1)S(1)}, u32[]{:S(2)}, u32[]{:S(2)}) collective-permute-start(bf16[4,128,128]{2,1,0:T(8,128)(2,1)S(1)} %pad_maximum_fusion.refs_0_), channel_id=1, source_target_pairs={{0,2},{1,3},{2,4},{3,5},{4,6},{5,7},{6,0},{7,1},{8,10},{9,11},{10,... | collective-permute-start | bytes 393224 | tf_op jit(solution)/shard_map/ppermute | solution.py:32
  38.7 12.4 %collective-permute-start.11 = (bf16[4,128,128]{2,1,0:T(8,128)(2,1)S(1)}, bf16[4,128,128]{2,1,0:T(8,128)(2,1)S(1)}, u32[]{:S(2)}, u32[]{:S(2)}) collective-permute-start(bf16[4,128,128]{2,1,0:T(8,128)(2,1)S(1)} %pad_maximum_fusion.refs_0_), channel_id=1, source_target_pairs={{0,4},{1,5},{2,6},{3,7},{4,0},{5,1},{6,2},{7,3},{8,12},{9,13},{10,... | collective-permute-start | bytes 393224 | tf_op jit(solution)/shard_map/ppermute | solution.py:32
  44.0 7.5 %collective-permute-start.12 = (bf16[4,128,128]{2,1,0:T(8,128)(2,1)S(1)}, bf16[4,128,128]{2,1,0:T(8,128)(2,1)S(1)}, u32[]{:S(2)}, u32[]{:S(2)}) collective-permute-start(bf16[4,128,128]{2,1,0:T(8,128)(2,1)S(1)} %pad_maximum_fusion.refs_0_), channel_id=1, source_target_pairs={{0,6},{1,7},{2,0},{3,1},{4,2},{5,3},{6,4},{7,5},{8,14},{9,15},{10,... | collective-permute-start | bytes 393224 | tf_op jit(solution)/shard_map/ppermute | solution.py:32
  52.3 14.2 %collective-permute-start.14 = (bf16[1296,128]{1,0:T(8,128)(2,1)S(1)}, bf16[1296,128]{1,0:T(8,128)(2,1)S(1)}, u32[]{:S(2)}, u32[]{:S(2)}) collective-permute-start(bf16[1296,128]{1,0:T(8,128)(2,1)S(1)} %get-tuple-element.49.rest_0_), channel_id=1, source_target_pairs={{0,64},{1,65},{2,66},{3,67},{4,68},{5,69},{6,70},{7,71},{8,72},{9,... | collective-permute-start | bytes 995336 | tf_op jit(solution)/shard_map/ppermute | solution.py:32
  57.8 11.0 %collective-permute-start.15 = (bf16[1296,128]{1,0:T(8,128)(2,1)S(1)}, bf16[1296,128]{1,0:T(8,128)(2,1)S(1)}, u32[]{:S(2)}, u32[]{:S(2)}) collective-permute-start(bf16[1296,128]{1,0:T(8,128)(2,1)S(1)} %get-tuple-element.49.rest_0_), channel_id=1, source_target_pairs={{0,1},{1,0},{2,3},{3,2},{4,5},{5,4},{6,7},{7,6},{8,9},{9,8},{10,11... | collective-permute-start | bytes 995336 | tf_op jit(solution)/shard_map/ppermute | solution.py:32
  61.9 11.3 %collective-permute-start.13 = (bf16[1296,128]{1,0:T(8,128)(2,1)S(1)}, bf16[1296,128]{1,0:T(8,128)(2,1)S(1)}, u32[]{:S(2)}, u32[]{:S(2)}) collective-permute-start(bf16[1296,128]{1,0:T(8,128)(2,1)S(1)} %get-tuple-element.49.rest_0_), channel_id=1, source_target_pairs={{0,32},{1,33},{2,34},{3,35},{4,36},{5,37},{6,38},{7,39},{8,40},{9,... | collective-permute-start | bytes 995336 | tf_op jit(solution)/shard_map/ppermute | solution.py:32
  64.2 12.2 %collective-permute-start.16 = (bf16[1296,128]{1,0:T(8,128)(2,1)S(1)}, bf16[1296,128]{1,0:T(8,128)(2,1)S(1)}, u32[]{:S(2)}, u32[]{:S(2)}) collective-permute-start(bf16[1296,128]{1,0:T(8,128)(2,1)S(1)} %get-tuple-element.49.rest_0_), channel_id=1, source_target_pairs={{0,96},{1,97},{2,98},{3,99},{4,100},{5,101},{6,102},{7,103},{8,104... | collective-permute-start | bytes 995336 | tf_op jit(solution)/shard_map/ppermute | solution.py:32
  66.6 12.9 %collective-permute-start.17 = (bf16[1296,128]{1,0:T(8,128)(2,1)S(1)}, bf16[1296,128]{1,0:T(8,128)(2,1)S(1)}, u32[]{:S(2)}, u32[]{:S(2)}) collective-permute-start(bf16[1296,128]{1,0:T(8,128)(2,1)S(1)} %collective-permute-done.14.rest_2_), channel_id=1, source_target_pairs={{0,1},{1,0},{2,3},{3,2},{4,5},{5,4},{6,7},{7,6},{8,9},{9,8},{10,11... | collective-permute-start | bytes 995336 | tf_op jit(solution)/shard_map/ppermute | solution.py:32
  73.2 7.8 %collective-permute-start.18 = (bf16[1296,128]{1,0:T(8,128)(2,1)S(1)}, bf16[1296,128]{1,0:T(8,128)(2,1)S(1)}, u32[]{:S(2)}, u32[]{:S(2)}) collective-permute-start(bf16[1296,128]{1,0:T(8,128)(2,1)S(1)} %collective-permute-done.13.rest_0_), channel_id=1, source_target_pairs={{0,1},{1,0},{2,3},{3,2},{4,5},{5,4},{6,7},{7,6},{8,9},{9,8},{10,11... | collective-permute-start | bytes 995336 | tf_op jit(solution)/shard_map/ppermute | solution.py:32
  76.5 4.6 %collective-permute-start.19 = (bf16[1296,128]{1,0:T(8,128)(2,1)S(1)}, bf16[1296,128]{1,0:T(8,128)(2,1)S(1)}, u32[]{:S(2)}, u32[]{:S(2)}) collective-permute-start(bf16[1296,128]{1,0:T(8,128)(2,1)S(1)} %collective-permute-done.16.rest_1_), channel_id=1, source_target_pairs={{0,1},{1,0},{2,3},{3,2},{4,5},{5,4},{6,7},{7,6},{8,9},{9,8},{10,11... | collective-permute-start | bytes 995336 | tf_op jit(solution)/shard_map/ppermute | solution.py:32

commit v9 on v8

--- a/solution.py
+++ b/solution.py
@@ -19,7 +19,7 @@
 PACK = 10
 REST = LINE - PACK
 META = 16
-PLAN = (((0, 0), (0, 1), (2, 0)), ((1, 0), (3, 0), (2, 1)), ((1, 1), (3, 1)))
+PLAN = (((0, 0), (2, 0)), ((1, 0), (3, 0), (2, 1), (0, 1)), ((1, 1), (3, 1)))
 ABSENT, LATER = 99, 50
 
 
@@ -259,20 +259,21 @@
 ):
     kept = jnp.where(amp_kept != 0, amplitudes * amp_kept.astype(jnp.bfloat16), jnp.inf).astype(jnp.bfloat16)
     first = jnp.stack([kept] + [move(kept, zh=k) for k in (1, 2, 3)])
-    head, tail = pack([first] + [move(first, zl=k) for k in (1, 2, 3)])
+    near = [first] + [move(first, zl=k) for k in (1, 2, 3)]
     lists, tiles = prepare(
         own_tiles, own_k, own_out, own_live, help_tiles, help_k, help_out, help_live)
+    near[3], lists = lax.optimization_barrier((near[3], lists))
+    head, tail = pack(near)
     acc = (jnp.zeros((OB, TILE, TILE), jnp.float32), jnp.zeros((8, TILE), jnp.int32))
     ys = {k: move(head, y=k) for k in (2, 1, 3)}
-    head_for_c, lists = lax.optimization_barrier((head, lists))
-    head_c = move(head_for_c, c=1)
+    head_c = move(head, c=1)
     tasks = functools.partial(run_tasks, lists=lists, tiles=tiles)
     ys[2], own_head = lax.optimization_barrier((ys[2], head))
     y2c = move(ys[2], c=1)
-    acc = tasks(0, [own_head, head_c, ys[2]], acc, False)
+    acc = tasks(0, [own_head, ys[2]], acc, False)
     ys[1], acc = lax.optimization_barrier((ys[1], acc))
     y1c, y3c = move(ys[1], c=1), move(ys[3], c=1)
-    acc = tasks(1, [ys[1], ys[3], y2c], acc, False)
+    acc = tasks(1, [ys[1], ys[3], y2c, head_c], acc, False)
     total, over, out = tasks(2, [y1c, y3c], acc, True)
 
     def second_round(tail, total, out):

time: 85 us -> 87.5 us (1.029)
  waiting for transfers between devices: 6.37 us -> 8.84 us
    ppermute x13, waiting for transfers between devices: 6.37 us -> 8.84 us  [move(): return lax.ppermute(x, 'col', pairs)]
  transfers between devices with their start and end apart: 13 -> 13, of which waited for: 4 -> 3; matrix products, arithmetic and copies ran while one was open for 2% -> 2% of each run, Pallas kernels for 8% -> 9%
where the time goes in v9:
time: 87.5 us; the launch traced here: 86.9 us
  starting transfers between devices  64 us (73%)
  Pallas kernels  10.4 us (12%)
  waiting for transfers between devices  8.84 us (10%)
  other arithmetic  2.08 us (2%)
  between operations  1.53 us (2%)
    ppermute x13, starting transfers between devices, move(): return lax.ppermute(x, 'col', pairs)  64 us
    ppermute x13, waiting for transfers between devices, move(): return lax.ppermute(x, 'col', pairs)  8.84 us
    pallas_call x3, Pallas kernels, run_tasks(): pl.pallas_call(functools.partial(task_kernel, phase, places, last), out_s...  5.7 us
    pallas_call x1, Pallas kernels, prepare(): pl.pallas_call(prep_kernel, out_shape=(jax.ShapeDtypeStruct((PHASES * (n...  3.91 us
  transfers between devices with their start and end apart: 13, of which 3 were waited for; matrix products, arithmetic and copies ran while one was open for 2% of the time, Pallas kernels for 9%

profile of v9, /device:TPU:1, one launch (start us, length us, event | category | flops | bytes accessed | tf_op | source)
XLA Modules:
  0.0 86.9 jit_solution(15483867369987481334)
XLA Ops:
  0.7 0.8 multiply_select_fusion
  1.4 9.6 %collective-permute-start.7 = (bf16[128,128]{1,0:T(8,128)(2,1)S(1)}, bf16[128,128]{1,0:T(8,128)(2,1)S(1)}, u32[]{:S(2)}, u32[]{:S(2)}) collective-permute-start(bf16[128,128]{1,0:T(8,128)(2,1)S(1)} %multiply_select_fusion), channel_id=1, source_target_pairs={{0,8},{1,9},{2,10},{3,11},{4,12},{5,13},{6,14},{7,15},{8,16},{9,17... | collective-permute-start | bytes 98312 | tf_op jit(solution)/shard_map/ppermute | solution.py:32
  11.1 15.4 %collective-permute-start.8 = (bf16[128,128]{1,0:T(8,128)(2,1)S(1)}, bf16[128,128]{1,0:T(8,128)(2,1)S(1)}, u32[]{:S(2)}, u32[]{:S(2)}) collective-permute-start(bf16[128,128]{1,0:T(8,128)(2,1)S(1)} %multiply_select_fusion), channel_id=1, source_target_pairs={{0,16},{1,17},{2,18},{3,19},{4,20},{5,21},{6,22},{7,23},{8,24},{9,... | collective-permute-start | bytes 98312 | tf_op jit(solution)/shard_map/ppermute | solution.py:32
  26.5 5.2 %collective-permute-start.9 = (bf16[128,128]{1,0:T(8,128)(2,1)S(1)}, bf16[128,128]{1,0:T(8,128)(2,1)S(1)}, u32[]{:S(2)}, u32[]{:S(2)}) collective-permute-start(bf16[128,128]{1,0:T(8,128)(2,1)S(1)} %multiply_select_fusion), channel_id=1, source_target_pairs={{0,24},{1,25},{2,26},{3,27},{4,28},{5,29},{6,30},{7,31},{8,0},{9,1... | collective-permute-start | bytes 98312 | tf_op jit(solution)/shard_map/ppermute | solution.py:32
  31.7 0.8 fusion
  32.5 0.0 collective-permute-done.7
  32.5 0.0 collective-permute-done.8
  32.5 2.6 %collective-permute-done.9 = bf16[128,128]{1,0:T(8,128)(2,1)S(1)} collective-permute-done((bf16[128,128]{1,0:T(8,128)(2,1)S(1)}, bf16[128,128]{1,0:T(8,128)(2,1)S(1)}, u32[]{:S(2)}, u32[]{:S(2)}) %collective-permute-start.9) | collective-permute-done | bytes 32800 | tf_op jit(solution)/shard_map/ppermute | solution.py:32
  35.1 6.7 %collective-permute-start.10 = (bf16[4,128,128]{2,1,0:T(8,128)(2,1)S(1)}, bf16[4,128,128]{2,1,0:T(8,128)(2,1)S(1)}, u32[]{:S(2)}, u32[]{:S(2)}) collective-permute-start(bf16[4,128,128]{2,1,0:T(8,128)(2,1)S(1)} %pad_maximum_fusion.refs_0_), channel_id=1, source_target_pairs={{0,6},{1,7},{2,0},{3,1},{4,2},{5,3},{6,4},{7,5},{8,14},{9,15},{10,... | collective-permute-start | bytes 393224 | tf_op jit(solution)/shard_map/ppermute | solution.py:32
  41.8 1.9 %collective-permute-start.11 = (bf16[4,128,128]{2,1,0:T(8,128)(2,1)S(1)}, bf16[4,128,128]{2,1,0:T(8,128)(2,1)S(1)}, u32[]{:S(2)}, u32[]{:S(2)}) collective-permute-start(bf16[4,128,128]{2,1,0:T(8,128)(2,1)S(1)} %pad_maximum_fusion.refs_0_), channel_id=1, source_target_pairs={{0,2},{1,3},{2,4},{3,5},{4,6},{5,7},{6,0},{7,1},{8,10},{9,11},{10,... | collective-permute-start | bytes 393224 | tf_op jit(solution)/shard_map/ppermute | solution.py:32
  43.7 2.2 %collective-permute-start.12 = (bf16[4,128,128]{2,1,0:T(8,128)(2,1)S(1)}, bf16[4,128,128]{2,1,0:T(8,128)(2,1)S(1)}, u32[]{:S(2)}, u32[]{:S(2)}) collective-permute-start(bf16[4,128,128]{2,1,0:T(8,128)(2,1)S(1)} %pad_maximum_fusion.refs_0_), channel_id=1, source_target_pairs={{0,4},{1,5},{2,6},{3,7},{4,0},{5,1},{6,2},{7,3},{8,12},{9,13},{10,... | collective-permute-start | bytes 393224 | tf_op jit(solution)/shard_map/ppermute | solution.py:32
  45.9 0.5 and_add_fusion.table
  46.5 3.9 %prep.1 = (s32[608]{0:T(1024)S(1)}, bf16[192,128,128]{2,1,0:T(8,128)(2,1)S(1)}) custom-call(s32[160]{0:T(256)} %own_k.1, s32[160]{0:T(256)} %own_out.1, s32[160]{0:T(256)} %own_live.1, s32[32]{0:T(128)} %help_k.1, s32[32]{0:T(128)} %help_out.1, s32[32]{0:T(128)} %help_live.1, s32[128]{0:T(128)} %and_add_fusion.table, bf16[160,128,128]{2,1,0:T(8,128)(2,1)} %own_tiles.1, ...), custom_call_target="tpu_custom_call" | custom-call | bytes 8388608 | tf_op jit(solution)/shard_map/prep/pallas_call | solution.py:232
  50.4 0.0 collective-permute-done.10.refs_3_
  50.4 0.0 collective-permute-done.11.refs_1_
  50.4 5.5 %collective-permute-done.12.refs_2_ = bf16[4,128,128]{2,1,0:T(8,128)(2,1)S(1)} collective-permute-done((bf16[4,128,128]{2,1,0:T(8,128)(2,1)S(1)}, bf16[4,128,128]{2,1,0:T(8,128)(2,1)S(1)}, u32[]{:S(2)}, u32[]{:S(2)}) %collective-permute-start.12) | collective-permute-done | bytes 131104 | tf_op jit(solution)/shard_map/ppermute | solution.py:32
  55.9 0.8 pack.1
  56.8 4.8 %collective-permute-start.14 = (bf16[1296,128]{1,0:T(8,128)(2,1)S(1)}, bf16[1296,128]{1,0:T(8,128)(2,1)S(1)}, u32[]{:S(2)}, u32[]{:S(2)}) collective-permute-start(bf16[1296,128]{1,0:T(8,128)(2,1)S(1)} %get-tuple-element.49.rest_0_), channel_id=1, source_target_pairs={{0,64},{1,65},{2,66},{3,67},{4,68},{5,69},{6,70},{7,71},{8,72},{9,... | collective-permute-start | bytes 995336 | tf_op jit(solution)/shard_map/ppermute | solution.py:32
  61.6 2.3 %collective-permute-start.13 = (bf16[1296,128]{1,0:T(8,128)(2,1)S(1)}, bf16[1296,128]{1,0:T(8,128)(2,1)S(1)}, u32[]{:S(2)}, u32[]{:S(2)}) collective-permute-start(bf16[1296,128]{1,0:T(8,128)(2,1)S(1)} %get-tuple-element.49.rest_0_), channel_id=1, source_target_pairs={{0,32},{1,33},{2,34},{3,35},{4,36},{5,37},{6,38},{7,39},{8,40},{9,... | collective-permute-start | bytes 995336 | tf_op jit(solution)/shard_map/ppermute | solution.py:32
  63.9 2.3 %collective-permute-start.15 = (bf16[1296,128]{1,0:T(8,128)(2,1)S(1)}, bf16[1296,128]{1,0:T(8,128)(2,1)S(1)}, u32[]{:S(2)}, u32[]{:S(2)}) collective-permute-start(bf16[1296,128]{1,0:T(8,128)(2,1)S(1)} %get-tuple-element.49.rest_0_), channel_id=1, source_target_pairs={{0,96},{1,97},{2,98},{3,99},{4,100},{5,101},{6,102},{7,103},{8,104... | collective-permute-start | bytes 995336 | tf_op jit(solution)/shard_map/ppermute | solution.py:32
  66.2 3.6 %collective-permute-start.17 = (bf16[1296,128]{1,0:T(8,128)(2,1)S(1)}, bf16[1296,128]{1,0:T(8,128)(2,1)S(1)}, u32[]{:S(2)}, u32[]{:S(2)}) collective-permute-start(bf16[1296,128]{1,0:T(8,128)(2,1)S(1)} %get-tuple-element.49.rest_0_), channel_id=1, source_target_pairs={{0,1},{1,0},{2,3},{3,2},{4,5},{5,4},{6,7},{7,6},{8,9},{9,8},{10,11... | collective-permute-start | bytes 995336 | tf_op jit(solution)/shard_map/ppermute | solution.py:32
  69.8 4.1 %collective-permute-start.16 = (bf16[1296,128]{1,0:T(8,128)(2,1)S(1)}, bf16[1296,128]{1,0:T(8,128)(2,1)S(1)}, u32[]{:S(2)}, u32[]{:S(2)}) collective-permute-start(bf16[1296,128]{1,0:T(8,128)(2,1)S(1)} %collective-permute-done.14.rest_1_), channel_id=1, source_target_pairs={{0,1},{1,0},{2,3},{3,2},{4,5},{5,4},{6,7},{7,6},{8,9},{9,8},{10,11... | collective-permute-start | bytes 995336 | tf_op jit(solution)/shard_map/ppermute | solution.py:32
  73.9 1.2 %tasks0.3 = (f32[4,128,128]{2,1,0:T(8,128)S(1)}, s32[8,128]{1,0:T(8,128)S(1)}) custom-call(s32[608]{0:T(1024)S(1)} %get-tuple-element.45.lists_v, bf16[192,128,128]{2,1,0:T(8,128)(2,1)S(1)} %get-tuple-element.46.tiles, f32[4,128,128]{2,1,0:T(8,128)S(1)} %broadcast_in_dim.44.acc_in, s32[8,128]{1,0:T(8,128)S(1)} %broadcast_8_over_in.2.over_in, ...), custom_call_target="tpu_custom_call" | custom-call | flops 2013265920 | bytes 8388608 | tf_op jit(solution)/shard_map/tasks0/pallas_call | solution.py:200
  75.2 0.7 collective-permute-done.13.rest_0_
  75.8 3.9 %collective-permute-start.18 = (bf16[1296,128]{1,0:T(8,128)(2,1)S(1)}, bf16[1296,128]{1,0:T(8,128)(2,1)S(1)}, u32[]{:S(2)}, u32[]{:S(2)}) collective-permute-start(bf16[1296,128]{1,0:T(8,128)(2,1)S(1)} %collective-permute-done.13.rest_0_), channel_id=1, source_target_pairs={{0,1},{1,0},{2,3},{3,2},{4,5},{5,4},{6,7},{7,6},{8,9},{9,8},{10,11... | collective-permute-start | bytes 995336 | tf_op jit(solution)/shard_map/ppermute | solution.py:32
  79.7 0.0 collective-permute-done.15.rest_1_
  79.8 1.9 %collective-permute-start.19 = (bf16[1296,128]{1,0:T(8,128)(2,1)S(1)}, bf16[1296,128]{1,0:T(8,128)(2,1)S(1)}, u32[]{:S(2)}, u32[]{:S(2)}) collective-permute-start(bf16[1296,128]{1,0:T(8,128)(2,1)S(1)} %collective-permute-done.15.rest_1_), channel_id=1, source_target_pairs={{0,1},{1,0},{2,3},{3,2},{4,5},{5,4},{6,7},{7,6},{8,9},{9,8},{10,11... | collective-permute-start | bytes 995336 | tf_op jit(solution)/shard_map/ppermute | solution.py:32
  81.7 0.0 collective-permute-done.16.rest_2_
  81.7 2.3 %tasks1.3 = (f32[4,128,128]{2,1,0:T(8,128)S(1)}, s32[8,128]{1,0:T(8,128)S(1)}) custom-call(s32[608]{0:T(1024)S(1)} %get-tuple-element.45.lists_v, bf16[192,128,128]{2,1,0:T(8,128)(2,1)S(1)} %get-tuple-element.46.tiles, f32[4,128,128]{2,1,0:T(8,128)S(1)} %get-tuple-element.53.acc_in, s32[8,128]{1,0:T(8,128)S(1)} %get-tuple-element.54.over_in, ...), custom_call_target="tpu_custom_call" | custom-call | flops 4026531840 | bytes 8388608 | tf_op jit(solution)/shard_map/tasks1/pallas_call | solution.py:200
  84.0 0.0 collective-permute-done.18.rest_0_
  84.0 0.0 collective-permute-done.19.rest_1_
  84.0 2.2 %tasks2.3 = (f32[4,128,128]{2,1,0:T(8,128)S(1)}, s32[1]{0:T(128)}, bf16[128,512]{1,0:T(8,128)(2,1)}) custom-call(s32[608]{0:T(1024)S(1)} %get-tuple-element.45.lists_v, bf16[192,128,128]{2,1,0:T(8,128)(2,1)S(1)} %get-tuple-element.46.tiles, f32[4,128,128]{2,1,0:T(8,128)S(1)} %get-tuple-element.56.acc_in, s32[8,128]{1,0:T(8,128)S(1)} %get-tuple-element.57.over_in, ...), custom_call_target="tpu_custom_call" | custom-call | flops 2013265920 | bytes 8388608 | tf_op jit(solution)/shard_map/tasks2/pallas_call | solution.py:200
  (6 shorter events, 0.1 us)
Async XLA Ops:
  1.4 31.1 %collective-permute-start.7 = (bf16[128,128]{1,0:T(8,128)(2,1)S(1)}, bf16[128,128]{1,0:T(8,128)(2,1)S(1)}, u32[]{:S(2)}, u32[]{:S(2)}) collective-permute-start(bf16[128,128]{1,0:T(8,128)(2,1)S(1)} %multiply_select_fusion), channel_id=1, source_target_pairs={{0,8},{1,9},{2,10},{3,11},{4,12},{5,13},{6,14},{7,15},{8,16},{9,17... | collective-permute-start | bytes 98312 | tf_op jit(solution)/shard_map/ppermute | solution.py:32
  11.1 21.4 %collective-permute-start.8 = (bf16[128,128]{1,0:T(8,128)(2,1)S(1)}, bf16[128,128]{1,0:T(8,128)(2,1)S(1)}, u32[]{:S(2)}, u32[]{:S(2)}) collective-permute-start(bf16[128,128]{1,0:T(8,128)(2,1)S(1)} %multiply_select_fusion), channel_id=1, source_target_pairs={{0,16},{1,17},{2,18},{3,19},{4,20},{5,21},{6,22},{7,23},{8,24},{9,... | collective-permute-start | bytes 98312 | tf_op jit(solution)/shard_map/ppermute | solution.py:32
  26.5 8.6 %collective-permute-start.9 = (bf16[128,128]{1,0:T(8,128)(2,1)S(1)}, bf16[128,128]{1,0:T(8,128)(2,1)S(1)}, u32[]{:S(2)}, u32[]{:S(2)}) collective-permute-start(bf16[128,128]{1,0:T(8,128)(2,1)S(1)} %multiply_select_fusion), channel_id=1, source_target_pairs={{0,24},{1,25},{2,26},{3,27},{4,28},{5,29},{6,30},{7,31},{8,0},{9,1... | collective-permute-start | bytes 98312 | tf_op jit(solution)/shard_map/ppermute | solution.py:32
  35.1 15.3 %collective-permute-start.10 = (bf16[4,128,128]{2,1,0:T(8,128)(2,1)S(1)}, bf16[4,128,128]{2,1,0:T(8,128)(2,1)S(1)}, u32[]{:S(2)}, u32[]{:S(2)}) collective-permute-start(bf16[4,128,128]{2,1,0:T(8,128)(2,1)S(1)} %pad_maximum_fusion.refs_0_), channel_id=1, source_target_pairs={{0,6},{1,7},{2,0},{3,1},{4,2},{5,3},{6,4},{7,5},{8,14},{9,15},{10,... | collective-permute-start | bytes 393224 | tf_op jit(solution)/shard_map/ppermute | solution.py:32
  41.8 8.6 %collective-permute-start.11 = (bf16[4,128,128]{2,1,0:T(8,128)(2,1)S(1)}, bf16[4,128,128]{2,1,0:T(8,128)(2,1)S(1)}, u32[]{:S(2)}, u32[]{:S(2)}) collective-permute-start(bf16[4,128,128]{2,1,0:T(8,128)(2,1)S(1)} %pad_maximum_fusion.refs_0_), channel_id=1, source_target_pairs={{0,2},{1,3},{2,4},{3,5},{4,6},{5,7},{6,0},{7,1},{8,10},{9,11},{10,... | collective-permute-start | bytes 393224 | tf_op jit(solution)/shard_map/ppermute | solution.py:32
  43.7 12.2 %collective-permute-start.12 = (bf16[4,128,128]{2,1,0:T(8,128)(2,1)S(1)}, bf16[4,128,128]{2,1,0:T(8,128)(2,1)S(1)}, u32[]{:S(2)}, u32[]{:S(2)}) collective-permute-start(bf16[4,128,128]{2,1,0:T(8,128)(2,1)S(1)} %pad_maximum_fusion.refs_0_), channel_id=1, source_target_pairs={{0,4},{1,5},{2,6},{3,7},{4,0},{5,1},{6,2},{7,3},{8,12},{9,13},{10,... | collective-permute-start | bytes 393224 | tf_op jit(solution)/shard_map/ppermute | solution.py:32
  56.8 13.0 %collective-permute-start.14 = (bf16[1296,128]{1,0:T(8,128)(2,1)S(1)}, bf16[1296,128]{1,0:T(8,128)(2,1)S(1)}, u32[]{:S(2)}, u32[]{:S(2)}) collective-permute-start(bf16[1296,128]{1,0:T(8,128)(2,1)S(1)} %get-tuple-element.49.rest_0_), channel_id=1, source_target_pairs={{0,64},{1,65},{2,66},{3,67},{4,68},{5,69},{6,70},{7,71},{8,72},{9,... | collective-permute-start | bytes 995336 | tf_op jit(solution)/shard_map/ppermute | solution.py:32
  61.6 14.2 %collective-permute-start.13 = (bf16[1296,128]{1,0:T(8,128)(2,1)S(1)}, bf16[1296,128]{1,0:T(8,128)(2,1)S(1)}, u32[]{:S(2)}, u32[]{:S(2)}) collective-permute-start(bf16[1296,128]{1,0:T(8,128)(2,1)S(1)} %get-tuple-element.49.rest_0_), channel_id=1, source_target_pairs={{0,32},{1,33},{2,34},{3,35},{4,36},{5,37},{6,38},{7,39},{8,40},{9,... | collective-permute-start | bytes 995336 | tf_op jit(solution)/shard_map/ppermute | solution.py:32
  63.9 15.8 %collective-permute-start.15 = (bf16[1296,128]{1,0:T(8,128)(2,1)S(1)}, bf16[1296,128]{1,0:T(8,128)(2,1)S(1)}, u32[]{:S(2)}, u32[]{:S(2)}) collective-permute-start(bf16[1296,128]{1,0:T(8,128)(2,1)S(1)} %get-tuple-element.49.rest_0_), channel_id=1, source_target_pairs={{0,96},{1,97},{2,98},{3,99},{4,100},{5,101},{6,102},{7,103},{8,104... | collective-permute-start | bytes 995336 | tf_op jit(solution)/shard_map/ppermute | solution.py:32
  66.2 15.5 %collective-permute-start.17 = (bf16[1296,128]{1,0:T(8,128)(2,1)S(1)}, bf16[1296,128]{1,0:T(8,128)(2,1)S(1)}, u32[]{:S(2)}, u32[]{:S(2)}) collective-permute-start(bf16[1296,128]{1,0:T(8,128)(2,1)S(1)} %get-tuple-element.49.rest_0_), channel_id=1, source_target_pairs={{0,1},{1,0},{2,3},{3,2},{4,5},{5,4},{6,7},{7,6},{8,9},{9,8},{10,11... | collective-permute-start | bytes 995336 | tf_op jit(solution)/shard_map/ppermute | solution.py:32
  69.8 11.9 %collective-permute-start.16 = (bf16[1296,128]{1,0:T(8,128)(2,1)S(1)}, bf16[1296,128]{1,0:T(8,128)(2,1)S(1)}, u32[]{:S(2)}, u32[]{:S(2)}) collective-permute-start(bf16[1296,128]{1,0:T(8,128)(2,1)S(1)} %collective-permute-done.14.rest_1_), channel_id=1, source_target_pairs={{0,1},{1,0},{2,3},{3,2},{4,5},{5,4},{6,7},{7,6},{8,9},{9,8},{10,11... | collective-permute-start | bytes 995336 | tf_op jit(solution)/shard_map/ppermute | solution.py:32
  75.8 8.2 %collective-permute-start.18 = (bf16[1296,128]{1,0:T(8,128)(2,1)S(1)}, bf16[1296,128]{1,0:T(8,128)(2,1)S(1)}, u32[]{:S(2)}, u32[]{:S(2)}) collective-permute-start(bf16[1296,128]{1,0:T(8,128)(2,1)S(1)} %collective-permute-done.13.rest_0_), channel_id=1, source_target_pairs={{0,1},{1,0},{2,3},{3,2},{4,5},{5,4},{6,7},{7,6},{8,9},{9,8},{10,11... | collective-permute-start | bytes 995336 | tf_op jit(solution)/shard_map/ppermute | solution.py:32
  79.8 4.3 %collective-permute-start.19 = (bf16[1296,128]{1,0:T(8,128)(2,1)S(1)}, bf16[1296,128]{1,0:T(8,128)(2,1)S(1)}, u32[]{:S(2)}, u32[]{:S(2)}) collective-permute-start(bf16[1296,128]{1,0:T(8,128)(2,1)S(1)} %collective-permute-done.15.rest_1_), channel_id=1, source_target_pairs={{0,1},{1,0},{2,3},{3,2},{4,5},{5,4},{6,7},{7,6},{8,9},{9,8},{10,11... | collective-permute-start | bytes 995336 | tf_op jit(solution)/shard_map/ppermute | solution.py:32

commit v10 on v8

--- a/solution.py
+++ b/solution.py
@@ -224,7 +224,7 @@
     for phase, places in enumerate(PLAN):
         for j, (dy, dc) in enumerate(places):
             group = jnp.where((y == dy) & (c == dc), phase * 4 + j, group)
-    table = (group * NZL + zl) * NZH + zh
+    table = (group * NZL + zl) * NZH + (zh ^ (zh >> 1))
     n = own_k.shape[0] + help_k.shape[0]
     smem = pl.BlockSpec(memory_space=pltpu.SMEM)
     hbm = pl.BlockSpec(memory_space=pltpu.HBM)
@@ -258,7 +258,7 @@
     help_live,
 ):
     kept = jnp.where(amp_kept != 0, amplitudes * amp_kept.astype(jnp.bfloat16), jnp.inf).astype(jnp.bfloat16)
-    first = jnp.stack([kept] + [move(kept, zh=k) for k in (1, 2, 3)])
+    first = jnp.stack([kept] + [move(kept, zh=k) for k in (1, 3, 2)])
     head, tail = pack([first] + [move(first, zl=k) for k in (1, 2, 3)])
     lists, tiles = prepare(
         own_tiles, own_k, own_out, own_live, help_tiles, help_k, help_out, help_live)

time: 85 us -> 91.1 us (1.072)
  waiting for transfers between devices: 6.37 us -> 12.2 us
  starting transfers between devices: 63.9 us -> 65.5 us
    ppermute x13, waiting for transfers between devices: 6.37 us -> 12.2 us  [move(): return lax.ppermute(x, 'col', pairs)]
    ppermute x13, starting transfers between devices: 63.9 us -> 65.5 us  [move(): return lax.ppermute(x, 'col', pairs)]
  transfers between devices with their start and end apart: 13 -> 13, of which waited for: 4 -> 4; matrix products, arithmetic and copies ran while one was open for 2% -> 1% of each run, Pallas kernels for 8% -> 7%
where the time goes in v10:
time: 91.1 us; the launch traced here: 90.1 us
  starting transfers between devices  65.5 us (72%)
  waiting for transfers between devices  12.2 us (13%)
  Pallas kernels  8.85 us (10%)
  other arithmetic  2.08 us (2%)
  between operations  1.52 us (2%)
    ppermute x13, starting transfers between devices, move(): return lax.ppermute(x, 'col', pairs)  65.5 us
    ppermute x13, waiting for transfers between devices, move(): return lax.ppermute(x, 'col', pairs)  12.2 us
    pallas_call x3, Pallas kernels, run_tasks(): pl.pallas_call(functools.partial(task_kernel, phase, places, last), out_s...  4.12 us
    pallas_call x1, Pallas kernels, prepare(): pl.pallas_call(prep_kernel, out_shape=(jax.ShapeDtypeStruct((PHASES * (n...  3.91 us
  transfers between devices with their start and end apart: 13, of which 4 were waited for; matrix products, arithmetic and copies ran while one was open for 1% of the time, Pallas kernels for 7%

profile of v10, /device:TPU:1, one launch (start us, length us, event | category | flops | bytes accessed | tf_op | source)
XLA Modules:
  0.0 90.1 jit_solution(1386610017037250186)
XLA Ops:
  0.7 0.8 multiply_select_fusion
  1.4 9.6 %collective-permute-start.7 = (bf16[128,128]{1,0:T(8,128)(2,1)S(1)}, bf16[128,128]{1,0:T(8,128)(2,1)S(1)}, u32[]{:S(2)}, u32[]{:S(2)}) collective-permute-start(bf16[128,128]{1,0:T(8,128)(2,1)S(1)} %multiply_select_fusion), channel_id=1, source_target_pairs={{0,8},{1,9},{2,10},{3,11},{4,12},{5,13},{6,14},{7,15},{8,16},{9,17... | collective-permute-start | bytes 98312 | tf_op jit(solution)/shard_map/ppermute | solution.py:32
  11.1 15.2 %collective-permute-start.8 = (bf16[128,128]{1,0:T(8,128)(2,1)S(1)}, bf16[128,128]{1,0:T(8,128)(2,1)S(1)}, u32[]{:S(2)}, u32[]{:S(2)}) collective-permute-start(bf16[128,128]{1,0:T(8,128)(2,1)S(1)} %multiply_select_fusion), channel_id=1, source_target_pairs={{0,24},{1,25},{2,26},{3,27},{4,28},{5,29},{6,30},{7,31},{8,0},{9,1... | collective-permute-start | bytes 98312 | tf_op jit(solution)/shard_map/ppermute | solution.py:32
  26.2 2.2 %collective-permute-start.9 = (bf16[128,128]{1,0:T(8,128)(2,1)S(1)}, bf16[128,128]{1,0:T(8,128)(2,1)S(1)}, u32[]{:S(2)}, u32[]{:S(2)}) collective-permute-start(bf16[128,128]{1,0:T(8,128)(2,1)S(1)} %multiply_select_fusion), channel_id=1, source_target_pairs={{0,16},{1,17},{2,18},{3,19},{4,20},{5,21},{6,22},{7,23},{8,24},{9,... | collective-permute-start | bytes 98312 | tf_op jit(solution)/shard_map/ppermute | solution.py:32
  28.4 0.8 fusion.1
  29.2 0.0 collective-permute-done.7
  29.2 0.0 collective-permute-done.8
  29.2 10.6 %collective-permute-done.9 = bf16[128,128]{1,0:T(8,128)(2,1)S(1)} collective-permute-done((bf16[128,128]{1,0:T(8,128)(2,1)S(1)}, bf16[128,128]{1,0:T(8,128)(2,1)S(1)}, u32[]{:S(2)}, u32[]{:S(2)}) %collective-permute-start.9) | collective-permute-done | bytes 32800 | tf_op jit(solution)/shard_map/ppermute | solution.py:32
  39.8 3.4 %collective-permute-start.10 = (bf16[4,128,128]{2,1,0:T(8,128)(2,1)S(1)}, bf16[4,128,128]{2,1,0:T(8,128)(2,1)S(1)}, u32[]{:S(2)}, u32[]{:S(2)}) collective-permute-start(bf16[4,128,128]{2,1,0:T(8,128)(2,1)S(1)} %pad_maximum_fusion.refs_0_), channel_id=1, source_target_pairs={{0,2},{1,3},{2,4},{3,5},{4,6},{5,7},{6,0},{7,1},{8,10},{9,11},{10,... | collective-permute-start | bytes 393224 | tf_op jit(solution)/shard_map/ppermute | solution.py:32
  43.2 4.9 %collective-permute-start.11 = (bf16[4,128,128]{2,1,0:T(8,128)(2,1)S(1)}, bf16[4,128,128]{2,1,0:T(8,128)(2,1)S(1)}, u32[]{:S(2)}, u32[]{:S(2)}) collective-permute-start(bf16[4,128,128]{2,1,0:T(8,128)(2,1)S(1)} %pad_maximum_fusion.refs_0_), channel_id=1, source_target_pairs={{0,4},{1,5},{2,6},{3,7},{4,0},{5,1},{6,2},{7,3},{8,12},{9,13},{10,... | collective-permute-start | bytes 393224 | tf_op jit(solution)/shard_map/ppermute | solution.py:32
  48.1 2.6 %collective-permute-start.12 = (bf16[4,128,128]{2,1,0:T(8,128)(2,1)S(1)}, bf16[4,128,128]{2,1,0:T(8,128)(2,1)S(1)}, u32[]{:S(2)}, u32[]{:S(2)}) collective-permute-start(bf16[4,128,128]{2,1,0:T(8,128)(2,1)S(1)} %pad_maximum_fusion.refs_0_), channel_id=1, source_target_pairs={{0,6},{1,7},{2,0},{3,1},{4,2},{5,3},{6,4},{7,5},{8,14},{9,15},{10,... | collective-permute-start | bytes 393224 | tf_op jit(solution)/shard_map/ppermute | solution.py:32
  50.8 0.5 fusion.table
  51.3 3.9 %prep.1 = (s32[608]{0:T(1024)S(1)}, bf16[192,128,128]{2,1,0:T(8,128)(2,1)S(1)}) custom-call(s32[160]{0:T(256)} %own_k.1, s32[160]{0:T(256)} %own_out.1, s32[160]{0:T(256)} %own_live.1, s32[32]{0:T(128)} %help_k.1, s32[32]{0:T(128)} %help_out.1, s32[32]{0:T(128)} %help_live.1, s32[128]{0:T(128)} %fusion.table, bf16[160,128,128]{2,1,0:T(8,128)(2,1)} %own_tiles.1, ...), custom_call_target="tpu_custom_call" | custom-call | bytes 8388608 | tf_op jit(solution)/shard_map/prep/pallas_call | solution.py:232
  55.2 0.0 collective-permute-done.10.refs_1_
  55.2 0.0 collective-permute-done.11.refs_2_
  55.2 0.0 collective-permute-done.12.refs_3_
  55.3 0.8 pack.1
  56.1 5.8 %collective-permute-start.14 = (bf16[1296,128]{1,0:T(8,128)(2,1)S(1)}, bf16[1296,128]{1,0:T(8,128)(2,1)S(1)}, u32[]{:S(2)}, u32[]{:S(2)}) collective-permute-start(bf16[1296,128]{1,0:T(8,128)(2,1)S(1)} %get-tuple-element.49.rest_0_), channel_id=1, source_target_pairs={{0,64},{1,65},{2,66},{3,67},{4,68},{5,69},{6,70},{7,71},{8,72},{9,... | collective-permute-start | bytes 995336 | tf_op jit(solution)/shard_map/ppermute | solution.py:32
  61.9 6.5 %collective-permute-start.15 = (bf16[1296,128]{1,0:T(8,128)(2,1)S(1)}, bf16[1296,128]{1,0:T(8,128)(2,1)S(1)}, u32[]{:S(2)}, u32[]{:S(2)}) collective-permute-start(bf16[1296,128]{1,0:T(8,128)(2,1)S(1)} %get-tuple-element.49.rest_0_), channel_id=1, source_target_pairs={{0,1},{1,0},{2,3},{3,2},{4,5},{5,4},{6,7},{7,6},{8,9},{9,8},{10,11... | collective-permute-start | bytes 995336 | tf_op jit(solution)/shard_map/ppermute | solution.py:32
  68.4 1.9 %collective-permute-start.13 = (bf16[1296,128]{1,0:T(8,128)(2,1)S(1)}, bf16[1296,128]{1,0:T(8,128)(2,1)S(1)}, u32[]{:S(2)}, u32[]{:S(2)}) collective-permute-start(bf16[1296,128]{1,0:T(8,128)(2,1)S(1)} %get-tuple-element.49.rest_0_), channel_id=1, source_target_pairs={{0,32},{1,33},{2,34},{3,35},{4,36},{5,37},{6,38},{7,39},{8,40},{9,... | collective-permute-start | bytes 995336 | tf_op jit(solution)/shard_map/ppermute | solution.py:32
  70.4 5.4 %collective-permute-start.16 = (bf16[1296,128]{1,0:T(8,128)(2,1)S(1)}, bf16[1296,128]{1,0:T(8,128)(2,1)S(1)}, u32[]{:S(2)}, u32[]{:S(2)}) collective-permute-start(bf16[1296,128]{1,0:T(8,128)(2,1)S(1)} %get-tuple-element.49.rest_0_), channel_id=1, source_target_pairs={{0,96},{1,97},{2,98},{3,99},{4,100},{5,101},{6,102},{7,103},{8,104... | collective-permute-start | bytes 995336 | tf_op jit(solution)/shard_map/ppermute | solution.py:32
  75.8 0.0 collective-permute-done.14.rest_2_
  75.8 2.5 %collective-permute-start.17 = (bf16[1296,128]{1,0:T(8,128)(2,1)S(1)}, bf16[1296,128]{1,0:T(8,128)(2,1)S(1)}, u32[]{:S(2)}, u32[]{:S(2)}) collective-permute-start(bf16[1296,128]{1,0:T(8,128)(2,1)S(1)} %collective-permute-done.14.rest_2_), channel_id=1, source_target_pairs={{0,1},{1,0},{2,3},{3,2},{4,5},{5,4},{6,7},{7,6},{8,9},{9,8},{10,11... | collective-permute-start | bytes 995336 | tf_op jit(solution)/shard_map/ppermute | solution.py:32
  78.3 0.0 collective-permute-done.15.rest_1_
  78.3 1.1 %tasks0.3 = (f32[4,128,128]{2,1,0:T(8,128)S(1)}, s32[8,128]{1,0:T(8,128)S(1)}) custom-call(s32[608]{0:T(1024)S(1)} %get-tuple-element.46.lists_v, bf16[192,128,128]{2,1,0:T(8,128)(2,1)S(1)} %get-tuple-element.47.tiles, f32[4,128,128]{2,1,0:T(8,128)S(1)} %broadcast_in_dim.41.acc_in, s32[8,128]{1,0:T(8,128)S(1)} %broadcast_8_over_in.2.over_in, ...), custom_call_target="tpu_custom_call" | custom-call | flops 3019898880 | bytes 8388608 | tf_op jit(solution)/shard_map/tasks0/pallas_call | solution.py:200
  79.5 0.3 collective-permute-done.13.rest_0_
  79.7 2.7 %collective-permute-start.18 = (bf16[1296,128]{1,0:T(8,128)(2,1)S(1)}, bf16[1296,128]{1,0:T(8,128)(2,1)S(1)}, u32[]{:S(2)}, u32[]{:S(2)}) collective-permute-start(bf16[1296,128]{1,0:T(8,128)(2,1)S(1)} %collective-permute-done.13.rest_0_), channel_id=1, source_target_pairs={{0,1},{1,0},{2,3},{3,2},{4,5},{5,4},{6,7},{7,6},{8,9},{9,8},{10,11... | collective-permute-start | bytes 995336 | tf_op jit(solution)/shard_map/ppermute | solution.py:32
  82.4 1.3 %collective-permute-done.16.rest_1_ = bf16[1296,128]{1,0:T(8,128)(2,1)S(1)} collective-permute-done((bf16[1296,128]{1,0:T(8,128)(2,1)S(1)}, bf16[1296,128]{1,0:T(8,128)(2,1)S(1)}, u32[]{:S(2)}, u32[]{:S(2)}) %collective-permute-start.16) | collective-permute-done | bytes 331808 | tf_op jit(solution)/shard_map/ppermute | solution.py:32
  83.7 2.7 %collective-permute-start.19 = (bf16[1296,128]{1,0:T(8,128)(2,1)S(1)}, bf16[1296,128]{1,0:T(8,128)(2,1)S(1)}, u32[]{:S(2)}, u32[]{:S(2)}) collective-permute-start(bf16[1296,128]{1,0:T(8,128)(2,1)S(1)} %collective-permute-done.16.rest_1_), channel_id=1, source_target_pairs={{0,1},{1,0},{2,3},{3,2},{4,5},{5,4},{6,7},{7,6},{8,9},{9,8},{10,11... | collective-permute-start | bytes 995336 | tf_op jit(solution)/shard_map/ppermute | solution.py:32
  86.4 1.1 %tasks1.3 = (f32[4,128,128]{2,1,0:T(8,128)S(1)}, s32[8,128]{1,0:T(8,128)S(1)}) custom-call(s32[608]{0:T(1024)S(1)} %get-tuple-element.46.lists_v, bf16[192,128,128]{2,1,0:T(8,128)(2,1)S(1)} %get-tuple-element.47.tiles, f32[4,128,128]{2,1,0:T(8,128)S(1)} %get-tuple-element.53.acc_in, s32[8,128]{1,0:T(8,128)S(1)} %get-tuple-element.54.over_in, ...), custom_call_target="tpu_custom_call" | custom-call | flops 3019898880 | bytes 8388608 | tf_op jit(solution)/shard_map/tasks1/pallas_call | solution.py:200
  87.6 0.1 collective-permute-done.19.rest_1_
  87.7 1.8 %tasks2.3 = (f32[4,128,128]{2,1,0:T(8,128)S(1)}, s32[1]{0:T(128)}, bf16[128,512]{1,0:T(8,128)(2,1)}) custom-call(s32[608]{0:T(1024)S(1)} %get-tuple-element.46.lists_v, bf16[192,128,128]{2,1,0:T(8,128)(2,1)S(1)} %get-tuple-element.47.tiles, f32[4,128,128]{2,1,0:T(8,128)S(1)} %get-tuple-element.56.acc_in, s32[8,128]{1,0:T(8,128)S(1)} %get-tuple-element.57.over_in, ...), custom_call_target="tpu_custom_call" | custom-call | flops 2013265920 | bytes 8388608 | tf_op jit(solution)/shard_map/tasks2/pallas_call | solution.py:200
  (6 shorter events, 0.1 us)
Async XLA Ops:
  1.4 27.8 %collective-permute-start.7 = (bf16[128,128]{1,0:T(8,128)(2,1)S(1)}, bf16[128,128]{1,0:T(8,128)(2,1)S(1)}, u32[]{:S(2)}, u32[]{:S(2)}) collective-permute-start(bf16[128,128]{1,0:T(8,128)(2,1)S(1)} %multiply_select_fusion), channel_id=1, source_target_pairs={{0,8},{1,9},{2,10},{3,11},{4,12},{5,13},{6,14},{7,15},{8,16},{9,17... | collective-permute-start | bytes 98312 | tf_op jit(solution)/shard_map/ppermute | solution.py:32
  11.1 18.2 %collective-permute-start.8 = (bf16[128,128]{1,0:T(8,128)(2,1)S(1)}, bf16[128,128]{1,0:T(8,128)(2,1)S(1)}, u32[]{:S(2)}, u32[]{:S(2)}) collective-permute-start(bf16[128,128]{1,0:T(8,128)(2,1)S(1)} %multiply_select_fusion), channel_id=1, source_target_pairs={{0,24},{1,25},{2,26},{3,27},{4,28},{5,29},{6,30},{7,31},{8,0},{9,1... | collective-permute-start | bytes 98312 | tf_op jit(solution)/shard_map/ppermute | solution.py:32
  26.2 13.6 %collective-permute-start.9 = (bf16[128,128]{1,0:T(8,128)(2,1)S(1)}, bf16[128,128]{1,0:T(8,128)(2,1)S(1)}, u32[]{:S(2)}, u32[]{:S(2)}) collective-permute-start(bf16[128,128]{1,0:T(8,128)(2,1)S(1)} %multiply_select_fusion), channel_id=1, source_target_pairs={{0,16},{1,17},{2,18},{3,19},{4,20},{5,21},{6,22},{7,23},{8,24},{9,... | collective-permute-start | bytes 98312 | tf_op jit(solution)/shard_map/ppermute | solution.py:32
  39.8 15.4 %collective-permute-start.10 = (bf16[4,128,128]{2,1,0:T(8,128)(2,1)S(1)}, bf16[4,128,128]{2,1,0:T(8,128)(2,1)S(1)}, u32[]{:S(2)}, u32[]{:S(2)}) collective-permute-start(bf16[4,128,128]{2,1,0:T(8,128)(2,1)S(1)} %pad_maximum_fusion.refs_0_), channel_id=1, source_target_pairs={{0,2},{1,3},{2,4},{3,5},{4,6},{5,7},{6,0},{7,1},{8,10},{9,11},{10,... | collective-permute-start | bytes 393224 | tf_op jit(solution)/shard_map/ppermute | solution.py:32
  43.2 12.0 %collective-permute-start.11 = (bf16[4,128,128]{2,1,0:T(8,128)(2,1)S(1)}, bf16[4,128,128]{2,1,0:T(8,128)(2,1)S(1)}, u32[]{:S(2)}, u32[]{:S(2)}) collective-permute-start(bf16[4,128,128]{2,1,0:T(8,128)(2,1)S(1)} %pad_maximum_fusion.refs_0_), channel_id=1, source_target_pairs={{0,4},{1,5},{2,6},{3,7},{4,0},{5,1},{6,2},{7,3},{8,12},{9,13},{10,... | collective-permute-start | bytes 393224 | tf_op jit(solution)/shard_map/ppermute | solution.py:32
  48.1 7.1 %collective-permute-start.12 = (bf16[4,128,128]{2,1,0:T(8,128)(2,1)S(1)}, bf16[4,128,128]{2,1,0:T(8,128)(2,1)S(1)}, u32[]{:S(2)}, u32[]{:S(2)}) collective-permute-start(bf16[4,128,128]{2,1,0:T(8,128)(2,1)S(1)} %pad_maximum_fusion.refs_0_), channel_id=1, source_target_pairs={{0,6},{1,7},{2,0},{3,1},{4,2},{5,3},{6,4},{7,5},{8,14},{9,15},{10,... | collective-permute-start | bytes 393224 | tf_op jit(solution)/shard_map/ppermute | solution.py:32
  56.1 19.7 %collective-permute-start.14 = (bf16[1296,128]{1,0:T(8,128)(2,1)S(1)}, bf16[1296,128]{1,0:T(8,128)(2,1)S(1)}, u32[]{:S(2)}, u32[]{:S(2)}) collective-permute-start(bf16[1296,128]{1,0:T(8,128)(2,1)S(1)} %get-tuple-element.49.rest_0_), channel_id=1, source_target_pairs={{0,64},{1,65},{2,66},{3,67},{4,68},{5,69},{6,70},{7,71},{8,72},{9,... | collective-permute-start | bytes 995336 | tf_op jit(solution)/shard_map/ppermute | solution.py:32
  61.9 16.4 %collective-permute-start.15 = (bf16[1296,128]{1,0:T(8,128)(2,1)S(1)}, bf16[1296,128]{1,0:T(8,128)(2,1)S(1)}, u32[]{:S(2)}, u32[]{:S(2)}) collective-permute-start(bf16[1296,128]{1,0:T(8,128)(2,1)S(1)} %get-tuple-element.49.rest_0_), channel_id=1, source_target_pairs={{0,1},{1,0},{2,3},{3,2},{4,5},{5,4},{6,7},{7,6},{8,9},{9,8},{10,11... | collective-permute-start | bytes 995336 | tf_op jit(solution)/shard_map/ppermute | solution.py:32
  68.4 11.3 %collective-permute-start.13 = (bf16[1296,128]{1,0:T(8,128)(2,1)S(1)}, bf16[1296,128]{1,0:T(8,128)(2,1)S(1)}, u32[]{:S(2)}, u32[]{:S(2)}) collective-permute-start(bf16[1296,128]{1,0:T(8,128)(2,1)S(1)} %get-tuple-element.49.rest_0_), channel_id=1, source_target_pairs={{0,32},{1,33},{2,34},{3,35},{4,36},{5,37},{6,38},{7,39},{8,40},{9,... | collective-permute-start | bytes 995336 | tf_op jit(solution)/shard_map/ppermute | solution.py:32
  70.4 13.4 %collective-permute-start.16 = (bf16[1296,128]{1,0:T(8,128)(2,1)S(1)}, bf16[1296,128]{1,0:T(8,128)(2,1)S(1)}, u32[]{:S(2)}, u32[]{:S(2)}) collective-permute-start(bf16[1296,128]{1,0:T(8,128)(2,1)S(1)} %get-tuple-element.49.rest_0_), channel_id=1, source_target_pairs={{0,96},{1,97},{2,98},{3,99},{4,100},{5,101},{6,102},{7,103},{8,104... | collective-permute-start | bytes 995336 | tf_op jit(solution)/shard_map/ppermute | solution.py:32
  75.8 10.6 %collective-permute-start.17 = (bf16[1296,128]{1,0:T(8,128)(2,1)S(1)}, bf16[1296,128]{1,0:T(8,128)(2,1)S(1)}, u32[]{:S(2)}, u32[]{:S(2)}) collective-permute-start(bf16[1296,128]{1,0:T(8,128)(2,1)S(1)} %collective-permute-done.14.rest_2_), channel_id=1, source_target_pairs={{0,1},{1,0},{2,3},{3,2},{4,5},{5,4},{6,7},{7,6},{8,9},{9,8},{10,11... | collective-permute-start | bytes 995336 | tf_op jit(solution)/shard_map/ppermute | solution.py:32
  79.7 7.9 %collective-permute-start.18 = (bf16[1296,128]{1,0:T(8,128)(2,1)S(1)}, bf16[1296,128]{1,0:T(8,128)(2,1)S(1)}, u32[]{:S(2)}, u32[]{:S(2)}) collective-permute-start(bf16[1296,128]{1,0:T(8,128)(2,1)S(1)} %collective-permute-done.13.rest_0_), channel_id=1, source_target_pairs={{0,1},{1,0},{2,3},{3,2},{4,5},{5,4},{6,7},{7,6},{8,9},{9,8},{10,11... | collective-permute-start | bytes 995336 | tf_op jit(solution)/shard_map/ppermute | solution.py:32
  83.7 3.9 %collective-permute-start.19 = (bf16[1296,128]{1,0:T(8,128)(2,1)S(1)}, bf16[1296,128]{1,0:T(8,128)(2,1)S(1)}, u32[]{:S(2)}, u32[]{:S(2)}) collective-permute-start(bf16[1296,128]{1,0:T(8,128)(2,1)S(1)} %collective-permute-done.16.rest_1_), channel_id=1, source_target_pairs={{0,1},{1,0},{2,3},{3,2},{4,5},{5,4},{6,7},{7,6},{8,9},{9,8},{10,11... | collective-permute-start | bytes 995336 | tf_op jit(solution)/shard_map/ppermute | solution.py:32
